TPU v7x, 256 devices: a whole 4x4x8 slice. The times are simulated.
256 devices in a mesh: batch: 32 (over z, y_hi, core), feat: 8 (over y_lo, x).
Axes of the slice: x: 4, y: 4 (y_hi: 2, y_lo: 2; y = y_hi * 2 + y_lo), z: 8, core: 2. Of those that a mesh axis runs over, the one named last changes fastest.
Arguments:
- view_a: bfloat16 [4096, 8192], P('batch', 'feat'), may hold values from -256 to 256
- view_b: bfloat16 [4096, 8192], P('batch', 'feat'), may hold values from -256 to 256
Outputs:
- grad_a: bfloat16 [4096, 8192], P('batch', 'feat')
- grad_b: bfloat16 [4096, 8192], P('batch', 'feat')
- loss: float32 [], replicated
All inputs are finite; a program needn't handle non-finite values.
Results may differ from a plain program's by a relative error of at most 0.006.
Values may be sent and summed in bfloat16 or wider, within the bound.
No kernel may reach another device: no remote copies, remote signals or barrier semaphores. Data moves between devices by JAX's collectives and lax.ppermute only.
A program may use at most 128 MiB of HBM per device.

v0:
```python
import jax
import jax.numpy as jnp
from jax import lax
from jax.experimental import pallas as pl
from jax.experimental.pallas import tpu as pltpu
from jax.sharding import Mesh, PartitionSpec as P

WIDTH = 8192

redund_weight = 0.0051
eps_var = 1e-05

ROWS = ("z", "yh", "c")
FEAT = ("yl", "x")
RING = ("yh", "yl")
LIMIT = 24 * 1024 * 1024
VMEM = pl.BlockSpec(memory_space=pltpu.VMEM)
SMEM = pl.BlockSpec(memory_space=pltpu.SMEM)
f32 = jnp.float32
bf16 = jnp.bfloat16


def shape(*dims, dtype=f32):
    return jax.ShapeDtypeStruct(dims, dtype)


def call(kernel, name, ids, args, outs, scratch=(), aliases=(), flops=0):
    return pl.pallas_call(
        kernel,
        in_specs=[SMEM] + [VMEM] * len(args),
        out_specs=[VMEM] * len(outs),
        out_shape=outs,
        scratch_shapes=list(scratch),
        input_output_aliases=dict(aliases),
        cost_estimate=pl.CostEstimate(flops=flops, bytes_accessed=0, transcendentals=0),
        compiler_params=pltpu.CompilerParams(vmem_limit_bytes=LIMIT),
        name=name,
    )(ids, *args)


def swap(values, axes, step):
    count = lax.axis_size(axes)
    return lax.ppermute(values, axes, [(k, k ^ step) for k in range(count)])


def shift(values, steps):
    count = lax.axis_size("z")
    return lax.ppermute(values, "z", [(k, (k + steps) % count) for k in range(count)])


def exchange_sum(values, axes, steps):
    for step in steps:
        values = values + swap(values, axes, step)
    return values


def tie(values, *others):
    return lax.optimization_barrier((values, others))[0]


def standardize(values, mean, rstd):
    return ((values.astype(f32) - mean) * rstd).astype(bf16)


def column_sum(values):
    return jnp.sum(values, 0, keepdims=True)


def flat_rows(block):
    return block[...].reshape(-1, block.shape[-1])


def split_kernel(ids, keep, got, near, rest, whole):
    c, yl = ids[0], ids[1]
    half = keep.shape[0] // 2
    for k, place in enumerate((yl, 1 - yl)):
        here = pl.ds(pl.multiple_of(place * half, half), half)
        out = near if k == 0 else rest
        out[c] = keep[here]
        out[1 - c] = got[here]
        whole[2 * k : 2 * k + 2] = out[...]


def merge_kernel(ids, right_near, right_far, left_near, left_far, right, left):
    right[0:2], right[2:4] = right_near[...], right_far[...]
    left[0:2], left[2:4] = left_near[...], left_far[...]


def halves(block):
    return block.at[0:2], block.at[2:4]


def moments_kernel(given, near_count, ids, *refs):
    moments = refs[-1]
    before, blocks = refs[:given], refs[given:-1]
    if near_count == len(blocks):
        pairs = [halves(block) for block in blocks]
    else:
        pairs = list(zip(blocks[:near_count], blocks[near_count:]))
    for half in range(2):
        for j in range(2):
            row = 2 * half + j
            total = None
            for ref in before:
                term = ref[row : row + 1]
                total = term if total is None else total + term
            for pair in pairs:
                floats = flat_rows(pair[half]).astype(f32)
                term = column_sum(floats * floats if j else floats)
                total = term if total is None else total + term
            moments[row : row + 1] = total


def add_moments(ids, before, near, far):
    width = near[0].shape[-1]
    return call(
        lambda *refs: moments_kernel(len(before), len(near), *refs),
        "moments",
        ids,
        [*before, *near, *far],
        [shape(4, width)],
    )[0]


def fill_columns(cols, place, blocks, stats):
    for half, sources in enumerate(blocks):
        width = stats.shape[1]
        first = place
        for source in sources:
            size = source.shape[0] * source.shape[1]
            cols[first : first + size, half * width : (half + 1) * width] = standardize(
                flat_rows(source), stats[2 * half : 2 * half + 1], stats[2 * half + 1 : 2 * half + 2]
            )
            first += size
    return first


def inner(left, right):
    return lax.dot_general(
        left, right, (((1,), (1,)), ((), ())), preferred_element_type=f32
    ).astype(bf16)


def gram_kernel(total_rows, ids, *refs):
    mine, one, two, three = refs[:4]
    near, rest, near_whole, far, far_rest, far_whole = refs[4:10]
    pairs = [(near, far)] + [halves(block) for block in refs[10:-4]]
    streams = tuple(zip(*pairs))
    pieces, cols, rows, stats = refs[-4:]
    yl = ids[1]
    width = mine.shape[1]
    own = mine[...] + two[...]
    cross = one[...] + three[...]
    for half in range(2):
        sums = [
            own[2 * half + j : 2 * half + j + 1] + cross[2 - 2 * half + j : 3 - 2 * half + j]
            for j in range(2)
        ]
        mean = sums[0] * (1.0 / total_rows)
        stats[2 * half : 2 * half + 1] = mean
        stats[2 * half + 1 : 2 * half + 2] = lax.rsqrt(
            sums[1] * (1.0 / total_rows) - mean * mean + eps_var
        )
    count = rows.shape[0] // 4
    sources = (
        (near.at[0:2], rest.at[0:2], near_whole.at[0:2], near_whole.at[2:4]),
        (far.at[0:2], far_rest.at[0:2], far_whole.at[2:4], far_whole.at[0:2]),
    )
    for half in range(2):
        for k, source in enumerate(sources[half]):
            place = yl if k % 2 == 0 else 1 - yl
            first = pl.multiple_of((k // 2) * 2 * count + place * count, count)
            rows[pl.ds(first, count), half * width : (half + 1) * width] = standardize(
                flat_rows(source), stats[2 * half : 2 * half + 1], stats[2 * half + 1 : 2 * half + 2]
            )
    last = fill_columns(cols, 0, streams, stats)
    piece = pieces.shape[1]
    for first in range(0, last, piece):
        pieces[first // piece] = inner(cols[first : first + piece], rows[...])


def last_gram_kernel(ids, stats, rows, before, old, left, near, far, *refs):
    parts, (cols, pieces) = refs[:-2], refs[-2:]
    streams = tuple(zip(halves(left), (near, far)))
    del old
    count, piece, _ = before.shape
    x = ids[2]
    fill_columns(cols, count * piece, streams, stats)
    pieces[count ^ x] = inner(cols[count * piece :], rows[...])
    for k in range(count):
        pieces[k ^ x] = before[k]
    for k, part in enumerate(parts):
        part[...] = pieces[k]


def reduce_kernel(ids, *refs):
    total = refs[0][...].astype(f32)
    for ref in refs[1:-2]:
        total = total + ref[...].astype(f32)
    flipped = total.T
    refs[-2][...] = flipped.astype(bf16)
    refs[-1][...] = flipped


def native_kernel(ids, view_a, view_b, mine, theirs, norm, rstd, sums):
    c = ids[0]
    values = []
    for v, view in enumerate((view_a, view_b)):
        stats = jnp.where(c == v, mine[...], theirs[...])
        rstd[v : v + 1] = stats[1:2]
        rounded = standardize(view[...], stats[0:1], stats[1:2])
        norm[v] = rounded
        values.append(rounded.astype(f32))
        sums[v : v + 1] = column_sum(values[v])
    sums[2:3] = column_sum(values[0] * values[1])
    sums[3:4] = jnp.zeros_like(rstd[0:1])


def diagonal(totals, total_rows):
    corr = totals[2:3] * (1.0 / total_rows)
    return corr, -2.0 * (1.0 - corr) - 2.0 * redund_weight * corr


def loss_kernel(total_rows, share, ids, gram, other, totals, loss):
    corr, _ = diagonal(totals[...], total_rows)
    miss = 1.0 - corr
    diag = jnp.sum(miss * miss - redund_weight * (corr * corr), keepdims=True)
    frob = jnp.sum(gram[...] * other[...].astype(f32), keepdims=True)
    weight = 0.5 * redund_weight / (total_rows * total_rows)
    loss[...] = jnp.broadcast_to(share * diag + weight * frob, loss.shape)


def product_kernel(coupling, count_full, ids, *refs):
    full = refs[:count_full]
    cols, rows = refs[count_full : count_full + 2]
    targets, sums = refs[count_full + 2 : -2], refs[-2:]
    x = ids[2]
    piece = full[0].shape[1]
    count, width = targets[0].shape[0] // 2, targets[0].shape[1]
    chunk = width // 2
    lanes = width // 128
    for first_lane in range(0, 2 * width, chunk):
        here = slice(first_lane, first_lane + chunk)
        side, local = divmod(first_lane, width)
        product = None
        for step, part in enumerate(full):
            first = pl.multiple_of((x ^ step) * piece, piece)
            term = jnp.dot(part[...], cols[pl.ds(first, piece), here], preferred_element_type=f32)
            product = term if product is None else product + term
        product = coupling * product
        plain = column_sum(product)
        cross = column_sum(product * rows[:, here].astype(f32))
        for k in range(chunk // 128):
            row = local // 128 + k
            sums[side][row : row + 1] = plain[:, k * 128 : (k + 1) * 128]
            sums[side][lanes + row : lanes + row + 1] = cross[:, k * 128 : (k + 1) * 128]
        for k in range(2):
            target = targets[2 * k + side]
            target[:, local : local + chunk] = product[2 * count * k : 2 * count * (k + 1)].astype(
                target.dtype
            )


def add_kernel(ids, mine, *refs):
    come, (keep, give) = refs[:-2], refs[-2:]
    c = ids[0]
    half = keep.shape[0] // 2
    for h in range(2):
        for out, place in ((keep, c), (give, 1 - c)):
            here = pl.ds(pl.multiple_of((2 * h + place) * half, half), half)
            total = mine[here]
            for ref in come:
                total = total + ref[here].astype(f32)
            out[h * half : (h + 1) * half] = total.astype(out.dtype)


def final_kernel(scale, total_rows, ids, ours, theirs, totals, rstd, norm, mine, other, *outs):
    grad_a, grad_b, loss = outs
    c = ids[0]
    count, width = mine.shape
    lanes = width // 128
    back = [jnp.where(c == v, ours[...], theirs[...]) for v in range(2)]
    loss[...] = back[0][2 * lanes : 2 * lanes + 1] + back[1][2 * lanes : 2 * lanes + 1]
    _, diag_grad = diagonal(totals[...], total_rows)
    diag_grad = diag_grad * (1.0 / total_rows)
    for k in range(lanes):
        here = slice(k * 128, (k + 1) * 128)
        weight = diag_grad[:, here]
        same, cross = mine[:, here], other[:, here].astype(f32)
        for v, out in enumerate((grad_a, grad_b)):
            mean_grad = back[v][k : k + 1] + weight * totals[1 - v : 2 - v, here]
            mean_cross = back[v][lanes + k : lanes + k + 1] + weight * totals[2:3, here]
            grad = jnp.where(c == v, same, cross) + weight * norm[1 - v, :, here].astype(f32)
            out[:, here] = (
                (scale * rstd[v : v + 1, here])
                * (
                    grad
                    - mean_grad * (1.0 / total_rows)
                    - norm[v, :, here].astype(f32) * (mean_cross * (1.0 / total_rows))
                )
            ).astype(bf16)


def shards(view_a, view_b):
    count, width = view_a.shape
    total_rows = count * lax.axis_size(ROWS)
    places = [lax.axis_index(name) for name in ("c", "yl", "x")]
    ids = jnp.stack(places).astype(jnp.int32)
    half = count // 2
    block = shape(2, half, width, dtype=bf16)
    hops = lax.axis_size("z") // 2
    peers = lax.axis_size("x")

    first = places[0] == 0
    keep, give = jnp.where(first, view_a, view_b), jnp.where(first, view_b, view_a)
    near, rest, whole = call(
        split_kernel,
        "split",
        ids,
        [keep, swap(give, "c", 1)],
        [block, block, shape(4, half, width, dtype=bf16)],
    )

    far = swap(rest, RING, 1)
    whole_far, near_far, whole_near = swap(whole, RING, 3), swap(near, RING, 1), swap(whole, RING, 2)
    moments = add_moments(ids, [], [near], [far])
    opposite = shift(moments, hops)
    first = [shift(near, 1), shift(far, 1), shift(near, -1), shift(far, -1)]
    right, left = call(merge_kernel, "merge", ids, first, [shape(4, half, width, dtype=bf16)] * 2)
    right, left = tie((right, left), whole_far)
    moments = add_moments(ids, [moments], first[0::2], first[1::2])
    early, late = [right, left], []
    for hop in range(2, hops):
        if hop == 3:
            right, left = tie((right, left), whole_near, opposite, moments)
        right, left = shift(right, 1), shift(left, -1)
        last = hop == hops - 1
        early, late = early + [right] + [left] * (not last), late + [left] * last
        moments = add_moments(ids, [moments] + [opposite] * last, [right, left], [])
    right, left = tie((right, left), near_far)
    late += [shift(right[:2], 1), shift(left[2:], -1)]
    row_blocks = [near, rest, whole_near, far, near_far, whole_far]
    panel = 2 * half * lax.axis_size("z")
    piece = panel // peers
    pieces, cols, rows, stats = call(
        lambda *refs: gram_kernel(total_rows, *refs),
        "gram",
        ids,
        [moments] + [swap(moments, RING, k) for k in (1, 2, 3)] + row_blocks + early,
        [
            shape(peers - 1, piece, 4 * count, dtype=bf16),
            shape(panel, 2 * width, dtype=bf16),
            shape(4 * count, 2 * width, dtype=bf16),
            shape(4, width),
        ],
        flops=4 * count * panel * width * 3,
    )
    *parts, cols = call(
        last_gram_kernel,
        "last_gram",
        ids,
        [stats, rows, pieces, cols] + late,
        [shape(piece, 4 * count, dtype=bf16)] * peers + [shape(panel, 2 * width, dtype=bf16)],
        [pltpu.VMEM((peers, piece, 4 * count), bf16)],
        {4: peers},
    )

    come = [swap(parts[k], ("c", "x"), peers | k) for k in range(peers)]
    norm, rstd, sums = call(
        native_kernel,
        "native",
        ids,
        [view_a, view_b, stats[:2], swap(stats[:2], "c", 1)],
        [shape(2, count, width, dtype=bf16), shape(2, width), shape(4, width)],
    )
    sums = exchange_sum(sums, "c", (1,))
    sums = exchange_sum(sums, "yh", (1,))
    come[0] = tie(come[0], sums)
    low_gram, gram = call(
        reduce_kernel,
        "reduce",
        ids,
        come,
        [shape(4 * count, piece, dtype=bf16), shape(4 * count, piece)],
    )
    full = [low_gram] + [swap(low_gram, "x", k) for k in range(1, peers)]
    totals = exchange_sum(sums, "z", (1, 2, 4))
    gram_other = swap(low_gram, "c", 1)
    full[1] = tie(full[1], totals, gram_other)
    lanes = width // 128

    leave = shape(2 * count, width, dtype=bf16)
    mine, leave_far, leave_near, leave_both, near_sums, far_sums = call(
        lambda *refs: product_kernel(
            2.0 * redund_weight / (total_rows * total_rows), peers, *refs
        ),
        "products",
        ids,
        full + [cols, rows],
        [shape(2 * count, width), leave, leave, leave] + [shape(2 * lanes, 128)] * 2,
        flops=16 * count * panel * width,
    )
    come_far, come_both = swap(leave_far, RING, 1), swap(leave_both, RING, 3)
    come_near = swap(leave_near, RING, 2)
    loss = call(
        lambda *refs: loss_kernel(total_rows, 1.0 / lax.axis_size(ROWS), *refs),
        "loss",
        ids,
        [gram, gram_other, tie(totals, far_sums)],
        [shape(8, 128)],
        flops=10**11,
    )[0]
    loss = loss + swap(loss, "x", 1) + swap(loss, "x", 2) + swap(loss, "x", 3)
    sums = exchange_sum(jnp.concatenate([near_sums, loss, far_sums, loss]), "z", (1, 2, 4))
    sums = tie(sums, come_far, come_both, come_near)
    near_sums, far_sums = jnp.split(sums, 2)
    back = near_sums + swap(near_sums, RING, 2) + swap(far_sums, RING, 1) + swap(far_sums, RING, 3)
    keep, give = call(
        add_kernel,
        "add",
        ids,
        [mine, come_far, come_both, come_near],
        [shape(count, width), shape(count, width, dtype=bf16)],
    )
    grad_a, grad_b, loss = call(
        lambda *refs: final_kernel(
            total_rows * total_rows / (redund_weight * WIDTH), total_rows, *refs
        ),
        "finish",
        ids,
        [back, swap(back, "c", 1), totals, rstd, norm, keep, swap(give, "c", 1)],
        [shape(count, width, dtype=bf16)] * 2 + [shape(1, 128)],
    )
    return grad_a, grad_b, loss[0, 0]


def solution(mesh):
    fine = Mesh(mesh.devices.reshape(8, 2, 2, 2, 4), ROWS + FEAT)
    return jax.shard_map(
        shards,
        mesh=fine,
        in_specs=(P(ROWS, FEAT), P(ROWS, FEAT)),
        out_specs=(P(ROWS, FEAT), P(ROWS, FEAT), P()),
        check_vma=False,
    )
```

profile of v0, /device:TPU:1, one launch (start us, length us, event | category | flops | bytes accessed | tf_op | source)
XLA Modules:
  0.0 155.6 jit_solution(14045229668942242502)
XLA Ops:
  0.6 1.1 broadcast_select_fusion
  1.7 3.3 %collective-permute-start = (bf16[128,1024]{1,0:T(8,128)(2,1)S(1)}, bf16[128,1024]{1,0:T(8,128)(2,1)S(1)}, u32[]{:S(2)}, u32[]{:S(2)}) collective-permute-start(bf16[128,1024]{1,0:T(8,128)(2,1)S(1)} %get-tuple-element.83), channel_id=1, source_target_pairs={{0,8},{8,0},{1,9},{9,1},{2,10},{10,2},{3,11},{11,3},{4,12},{12,4},... | collective-permute-start | bytes 786440 | tf_op jit(solution)/shard_map/ppermute | solution.py:43
  5.1 1.1 collective-permute-done.got
  6.9 1.4 collective-permute-start.6
  8.4 5.6 %collective-permute-start.3 = (bf16[2,64,1024]{2,1,0:T(8,128)(2,1)S(1)}, bf16[2,64,1024]{2,1,0:T(8,128)(2,1)S(1)}, u32[]{:S(2)}, u32[]{:S(2)}) collective-permute-start(bf16[2,64,1024]{2,1,0:T(8,128)(2,1)S(1)} %get-tuple-element.43.refs_1_.refs_5_), channel_id=1, source_target_pairs={{0,224},{32,0},{64,32},{96,64},{128,96},{160,128},{192,160},{224,1... | collective-permute-start | bytes 786440 | tf_op jit(solution)/shard_map/ppermute | solution.py:48
  14.4 3.8 %collective-permute-start.5 = (bf16[2,64,1024]{2,1,0:T(8,128)(2,1)S(1)}, bf16[2,64,1024]{2,1,0:T(8,128)(2,1)S(1)}, u32[]{:S(2)}, u32[]{:S(2)}) collective-permute-start(bf16[2,64,1024]{2,1,0:T(8,128)(2,1)S(1)} %collective-permute-done.1.refs_2_.refs_8_), channel_id=1, source_target_pairs={{0,224},{32,0},{64,32},{96,64},{128,96},{160,128},{192,160},{224,1... | collective-permute-start | bytes 786440 | tf_op jit(solution)/shard_map/ppermute | solution.py:48
  18.6 3.1 %collective-permute-done.2.refs_2_.right_near = bf16[2,64,1024]{2,1,0:T(8,128)(2,1)S(1)} collective-permute-done((bf16[2,64,1024]{2,1,0:T(8,128)(2,1)S(1)}, bf16[2,64,1024]{2,1,0:T(8,128)(2,1)S(1)}, u32[]{:S(2)}, u32[]{:S(2)}) %collective-permute-start.2) | collective-permute-done | bytes 262176 | tf_op jit(solution)/shard_map/ppermute | solution.py:48
  21.7 2.7 %collective-permute-done.5.refs_5_.left_far = bf16[2,64,1024]{2,1,0:T(8,128)(2,1)S(1)} collective-permute-done((bf16[2,64,1024]{2,1,0:T(8,128)(2,1)S(1)}, bf16[2,64,1024]{2,1,0:T(8,128)(2,1)S(1)}, u32[]{:S(2)}, u32[]{:S(2)}) %collective-permute-start.5) | collective-permute-done | bytes 262176 | tf_op jit(solution)/shard_map/ppermute | solution.py:48
  24.5 3.4 %collective-permute-done.4.refs_4_.right_far = bf16[2,64,1024]{2,1,0:T(8,128)(2,1)S(1)} collective-permute-done((bf16[2,64,1024]{2,1,0:T(8,128)(2,1)S(1)}, bf16[2,64,1024]{2,1,0:T(8,128)(2,1)S(1)}, u32[]{:S(2)}, u32[]{:S(2)}) %collective-permute-start.4) | collective-permute-done | bytes 262176 | tf_op jit(solution)/shard_map/ppermute | solution.py:48
  28.6 2.7 %collective-permute-start.8 = (bf16[4,64,1024]{2,1,0:T(8,128)(2,1)S(1)}, bf16[4,64,1024]{2,1,0:T(8,128)(2,1)S(1)}, u32[]{:S(2)}, u32[]{:S(2)}) collective-permute-start(bf16[4,64,1024]{2,1,0:T(8,128)(2,1)S(1)} %get-tuple-element.49.refs_12_), channel_id=1, source_target_pairs={{0,224},{32,0},{64,32},{96,64},{128,96},{160,128},{192,160},{224,1... | collective-permute-start | bytes 1572872 | tf_op jit(solution)/shard_map/ppermute | solution.py:48
  31.2 0.8 collective-permute-start.10
  32.1 0.7 moments.4.refs_1_
  32.8 1.6 %collective-permute-start.9 = (f32[4,1024]{1,0:T(4,128)S(1)}, f32[4,1024]{1,0:T(4,128)S(1)}, u32[]{:S(2)}, u32[]{:S(2)}) collective-permute-start(f32[4,1024]{1,0:T(4,128)S(1)} %moments.4.refs_1_), channel_id=1, source_target_pairs={{0,128},{32,160},{64,192},{96,224},{128,0},{160,32},{192,64},{224,... | collective-permute-start | bytes 49160 | tf_op jit(solution)/shard_map/ppermute | solution.py:48
  34.4 0.8 moments.5.refs_1_
  35.2 6.7 %collective-permute-done.7.refs_2_.refs_13_ = bf16[4,64,1024]{2,1,0:T(8,128)(2,1)S(1)} collective-permute-done((bf16[4,64,1024]{2,1,0:T(8,128)(2,1)S(1)}, bf16[4,64,1024]{2,1,0:T(8,128)(2,1)S(1)}, u32[]{:S(2)}, u32[]{:S(2)}) %collective-permute-start.7) | collective-permute-done | bytes 524320 | tf_op jit(solution)/shard_map/ppermute | solution.py:48
  41.9 0.8 moments.6.refs_1_
  42.7 1.2 collective-permute-done.10.refs_7_
  44.0 2.7 %collective-permute-start.12 = (bf16[4,64,1024]{2,1,0:T(8,128)(2,1)S(1)}, bf16[4,64,1024]{2,1,0:T(8,128)(2,1)S(1)}, u32[]{:S(2)}, u32[]{:S(2)}) collective-permute-start(bf16[4,64,1024]{2,1,0:T(8,128)(2,1)S(1)} %collective-permute-done.8.refs_3_.refs_14_), channel_id=1, source_target_pairs={{0,224},{32,0},{64,32},{96,64},{128,96},{160,128},{192,160},{224,1... | collective-permute-start | bytes 1572872 | tf_op jit(solution)/shard_map/ppermute | solution.py:48
  46.7 5.5 %collective-permute-done.16.refs_9_ = bf16[2,64,1024]{2,1,0:T(8,128)(2,1)S(1)} collective-permute-done((bf16[2,64,1024]{2,1,0:T(8,128)(2,1)S(1)}, bf16[2,64,1024]{2,1,0:T(8,128)(2,1)S(1)}, u32[]{:S(2)}, u32[]{:S(2)}) %collective-permute-start.16) | collective-permute-done | bytes 262176 | tf_op jit(solution)/shard_map/ppermute | solution.py:43
  52.2 3.3 %collective-permute-done.11.refs_3_.refs_15_ = bf16[4,64,1024]{2,1,0:T(8,128)(2,1)S(1)} collective-permute-done((bf16[4,64,1024]{2,1,0:T(8,128)(2,1)S(1)}, bf16[4,64,1024]{2,1,0:T(8,128)(2,1)S(1)}, u32[]{:S(2)}, u32[]{:S(2)}) %collective-permute-start.11) | collective-permute-done | bytes 524320 | tf_op jit(solution)/shard_map/ppermute | solution.py:48
  55.6 2.5 %collective-permute-start.18 = (bf16[2,64,1024]{2,1,0:T(8,128)(2,1)S(1)}, bf16[2,64,1024]{2,1,0:T(8,128)(2,1)S(1)}, u32[]{:S(2)}, u32[]{:S(2)}) collective-permute-start(bf16[2,64,1024]{2,1,0:T(8,128)(2,1)S(1)} %slice.14), channel_id=1, source_target_pairs={{0,224},{32,0},{64,32},{96,64},{128,96},{160,128},{192,160},{224,1... | collective-permute-start | bytes 786440 | tf_op jit(solution)/shard_map/ppermute | solution.py:48
  58.0 0.8 moments.7.refs_1_
  58.9 1.0 collective-permute-start.14
  60.0 2.2 %collective-permute-start.13 = (f32[4,1024]{1,0:T(4,128)S(1)}, f32[4,1024]{1,0:T(4,128)S(1)}, u32[]{:S(2)}, u32[]{:S(2)}) collective-permute-start(f32[4,1024]{1,0:T(4,128)S(1)} %moments.7.refs_1_), channel_id=1, source_target_pairs={{0,4},{4,0},{16,20},{20,16},{1,5},{5,1},{17,21},{21,17},{2,6},{6,2... | collective-permute-start | bytes 49160 | tf_op jit(solution)/shard_map/ppermute | solution.py:43
  63.1 0.7 collective-permute-done.13.refs_2_
  63.8 3.2 %gram.1 = (bf16[3,256,512]{2,1,0:T(8,128)(2,1)S(1)}, bf16[1024,2048]{1,0:T(8,128)(2,1)S(1)}, bf16[512,2048]{1,0:T(8,128)(2,1)S(1)}, f32[4,1024]{1,0:T(4,128)S(1)}) custom-call(s32[3]{0:T(128)S(1)} %pad_add_fusion.ids.refs_0_, f32[4,1024]{1,0:T(4,128)S(1)} %moments.7.refs_1_, f32[4,1024]{1,0:T(4,128)S(1)} %collective-permute-done.13.refs_2_, ...), custom_call_target="tpu_custom_call" | custom-call | flops 1610612736 | tf_op jit(solution)/shard_map/gram/pallas_call | solution.py:28
  67.0 1.4 last_gram.1
  68.5 5.8 %collective-permute-start.19 = (bf16[256,512]{1,0:T(8,128)(2,1)S(1)}, bf16[256,512]{1,0:T(8,128)(2,1)S(1)}, u32[]{:S(2)}, u32[]{:S(2)}) collective-permute-start(bf16[256,512]{1,0:T(8,128)(2,1)S(1)} %get-tuple-element.58), channel_id=1, source_target_pairs={{0,8},{1,9},{2,10},{3,11},{8,0},{9,1},{10,2},{11,3},{4,12},{5,13},... | collective-permute-start | bytes 786440 | tf_op jit(solution)/shard_map/ppermute | solution.py:43
  74.3 1.2 collective-permute-start.23
  75.5 2.8 %collective-permute-start.24 = (bf16[256,512]{1,0:T(8,128)(2,1)S(1)}, bf16[256,512]{1,0:T(8,128)(2,1)S(1)}, u32[]{:S(2)}, u32[]{:S(2)}) collective-permute-start(bf16[256,512]{1,0:T(8,128)(2,1)S(1)} %get-tuple-element.62), channel_id=1, source_target_pairs={{0,10},{1,11},{2,8},{3,9},{8,2},{9,3},{10,0},{11,1},{4,14},{5,15},... | collective-permute-start | bytes 786440 | tf_op jit(solution)/shard_map/ppermute | solution.py:43
  78.9 0.8 collective-permute-done.20.theirs
  79.7 0.8 native.1
  81.0 0.8 collective-permute-done.21
  81.8 1.7 %collective-permute-start.22 = (f32[4,1024]{1,0:T(4,128)S(1)}, f32[4,1024]{1,0:T(4,128)S(1)}, u32[]{:S(2)}, u32[]{:S(2)}) collective-permute-start(f32[4,1024]{1,0:T(4,128)S(1)} %add.43), channel_id=1, source_target_pairs={{0,16},{16,0},{1,17},{17,1},{2,18},{18,2},{3,19},{19,3},{4,20},{20... | collective-permute-start | bytes 49160 | tf_op jit(solution)/shard_map/ppermute | solution.py:43
  83.6 2.6 %collective-permute-done.22 = f32[4,1024]{1,0:T(4,128)S(1)} collective-permute-done((f32[4,1024]{1,0:T(4,128)S(1)}, f32[4,1024]{1,0:T(4,128)S(1)}, u32[]{:S(2)}, u32[]{:S(2)}) %collective-permute-start.22) | collective-permute-done | bytes 16416 | tf_op jit(solution)/shard_map/ppermute | solution.py:43
  86.2 4.0 %collective-permute-done.24.refs_2_ = bf16[256,512]{1,0:T(8,128)(2,1)S(1)} collective-permute-done((bf16[256,512]{1,0:T(8,128)(2,1)S(1)}, bf16[256,512]{1,0:T(8,128)(2,1)S(1)}, u32[]{:S(2)}, u32[]{:S(2)}) %collective-permute-start.24) | collective-permute-done | bytes 262176 | tf_op jit(solution)/shard_map/ppermute | solution.py:43
  90.3 2.9 %collective-permute-done.25.refs_3_ = bf16[256,512]{1,0:T(8,128)(2,1)S(1)} collective-permute-done((bf16[256,512]{1,0:T(8,128)(2,1)S(1)}, bf16[256,512]{1,0:T(8,128)(2,1)S(1)}, u32[]{:S(2)}, u32[]{:S(2)}) %collective-permute-start.25) | collective-permute-done | bytes 262176 | tf_op jit(solution)/shard_map/ppermute | solution.py:43
  93.1 0.7 reduce.1
  94.3 3.0 %collective-permute-start.31 = (bf16[512,256]{1,0:T(8,128)(2,1)S(1)}, bf16[512,256]{1,0:T(8,128)(2,1)S(1)}, u32[]{:S(2)}, u32[]{:S(2)}) collective-permute-start(bf16[512,256]{1,0:T(8,128)(2,1)S(1)} %get-tuple-element.64.refs_1_), channel_id=1, source_target_pairs={{0,2},{1,3},{2,0},{3,1},{4,6},{5,7},{6,4},{7,5},{8,10},{9,11},{10,... | collective-permute-start | bytes 786440 | tf_op jit(solution)/shard_map/ppermute | solution.py:43
  97.3 2.9 %collective-permute-done.27 = f32[4,1024]{1,0:T(4,128)S(1)} collective-permute-done((f32[4,1024]{1,0:T(4,128)S(1)}, f32[4,1024]{1,0:T(4,128)S(1)}, u32[]{:S(2)}, u32[]{:S(2)}) %collective-permute-start.27) | collective-permute-done | bytes 16416 | tf_op jit(solution)/shard_map/ppermute | solution.py:43
  100.2 0.9 collective-permute-start.28
  101.1 2.9 %collective-permute-done.28 = f32[4,1024]{1,0:T(4,128)S(1)} collective-permute-done((f32[4,1024]{1,0:T(4,128)S(1)}, f32[4,1024]{1,0:T(4,128)S(1)}, u32[]{:S(2)}, u32[]{:S(2)}) %collective-permute-start.28) | collective-permute-done | bytes 16416 | tf_op jit(solution)/shard_map/ppermute | solution.py:43
  104.0 2.4 %collective-permute-start.29 = (f32[4,1024]{1,0:T(4,128)S(1)}, f32[4,1024]{1,0:T(4,128)S(1)}, u32[]{:S(2)}, u32[]{:S(2)}) collective-permute-start(f32[4,1024]{1,0:T(4,128)S(1)} %add.46), channel_id=1, source_target_pairs={{0,128},{32,160},{64,192},{96,224},{128,0},{160,32},{192,64},{224,... | collective-permute-start | bytes 49160 | tf_op jit(solution)/shard_map/ppermute | solution.py:43
  106.4 4.1 %collective-permute-done.29 = f32[4,1024]{1,0:T(4,128)S(1)} collective-permute-done((f32[4,1024]{1,0:T(4,128)S(1)}, f32[4,1024]{1,0:T(4,128)S(1)}, u32[]{:S(2)}, u32[]{:S(2)}) %collective-permute-start.29) | collective-permute-done | bytes 16416 | tf_op jit(solution)/shard_map/ppermute | solution.py:43
  110.5 3.1 %products.1 = (f32[256,1024]{1,0:T(8,128)S(1)}, bf16[256,1024]{1,0:T(8,128)(2,1)S(1)}, bf16[256,1024]{1,0:T(8,128)(2,1)S(1)}, bf16[256,1024]{1,0:T(8,128)(2,1)S(...) custom-call(s32[3]{0:T(128)S(1)} %pad_add_fusion.ids.refs_0_, bf16[512,256]{1,0:T(8,128)(2,1)S(1)} %get-tuple-element.64.refs_1_, ...), custom_call_target="tpu_custom_call" | custom-call | flops 2147483648 | tf_op jit(solution)/shard_map/products/pallas_call | solution.py:28
  113.7 0.8 loss.1
  114.9 1.6 collective-permute-start.34
  116.4 1.4 collective-permute-start.33
  117.8 1.6 collective-permute-start.39
  119.4 0.7 collective-permute-start.40
  120.0 1.2 collective-permute-start.41
  121.4 2.7 %collective-permute-done.36 = f32[48,128]{1,0:T(8,128)S(1)} collective-permute-done((f32[48,128]{1,0:T(8,128)S(1)}, f32[48,128]{1,0:T(8,128)S(1)}, u32[]{:S(2)}, u32[]{:S(2)}) %collective-permute-start.36) | collective-permute-done | bytes 24608 | tf_op jit(solution)/shard_map/ppermute | solution.py:43
  124.0 0.8 collective-permute-start.37
  124.8 2.8 %collective-permute-done.37 = f32[48,128]{1,0:T(8,128)S(1)} collective-permute-done((f32[48,128]{1,0:T(8,128)S(1)}, f32[48,128]{1,0:T(8,128)S(1)}, u32[]{:S(2)}, u32[]{:S(2)}) %collective-permute-start.37) | collective-permute-done | bytes 24608 | tf_op jit(solution)/shard_map/ppermute | solution.py:43
  127.6 2.4 %collective-permute-start.38 = (f32[48,128]{1,0:T(8,128)S(1)}, f32[48,128]{1,0:T(8,128)S(1)}, u32[]{:S(2)}, u32[]{:S(2)}) collective-permute-start(f32[48,128]{1,0:T(8,128)S(1)} %add.52), channel_id=1, source_target_pairs={{0,128},{32,160},{64,192},{96,224},{128,0},{160,32},{192,64},{224,... | collective-permute-start | bytes 73736 | tf_op jit(solution)/shard_map/ppermute | solution.py:43
  130.0 4.2 %collective-permute-done.38 = f32[48,128]{1,0:T(8,128)S(1)} collective-permute-done((f32[48,128]{1,0:T(8,128)S(1)}, f32[48,128]{1,0:T(8,128)S(1)}, u32[]{:S(2)}, u32[]{:S(2)}) %collective-permute-start.38) | collective-permute-done | bytes 24608 | tf_op jit(solution)/shard_map/ppermute | solution.py:43
  134.2 5.3 %collective-permute-done.41.refs_2_ = bf16[256,1024]{1,0:T(8,128)(2,1)S(1)} collective-permute-done((bf16[256,1024]{1,0:T(8,128)(2,1)S(1)}, bf16[256,1024]{1,0:T(8,128)(2,1)S(1)}, u32[]{:S(2)}, u32[]{:S(2)}) %collective-permute-start.41) | collective-permute-done | bytes 524320 | tf_op jit(solution)/shard_map/ppermute | solution.py:43
  139.5 0.8 add.68
  140.2 6.8 %collective-permute-start.46 = (bf16[128,1024]{1,0:T(8,128)(2,1)S(1)}, bf16[128,1024]{1,0:T(8,128)(2,1)S(1)}, u32[]{:S(2)}, u32[]{:S(2)}) collective-permute-start(bf16[128,1024]{1,0:T(8,128)(2,1)S(1)} %get-tuple-element.79), channel_id=1, source_target_pairs={{0,8},{8,0},{1,9},{9,1},{2,10},{10,2},{3,11},{11,3},{4,12},{12,4},... | collective-permute-start | bytes 786440 | tf_op jit(solution)/shard_map/ppermute | solution.py:43
  148.3 1.4 collective-permute-start.43
  149.7 1.4 collective-permute-done.42
  151.7 1.3 collective-permute-start.45
  153.0 0.8 collective-permute-done.45.refs_2_
  153.9 1.7 %finish.1 = (bf16[128,1024]{1,0:T(8,128)(2,1)}, bf16[128,1024]{1,0:T(8,128)(2,1)}, f32[1,128]{1,0:T(1,128)}) custom-call(s32[3]{0:T(128)S(1)} %pad_add_fusion.ids.refs_0_, f32[24,128]{1,0:T(8,128)S(1)} %add_add_fusion.refs_1_, f32[24,128]{1,0:T(8,128)S(1)} %collective-permute-done.45.refs_2_, f32[4,1024]{1,0:T(4,128)S(1)} %add.47.refs_3_, ...), custom_call_target="tpu_custom_call" | custom-call | tf_op jit(solution)/shard_map/finish/pallas_call | solution.py:28
  (65 shorter events, 7.4 us)
Async XLA Ops:
  1.7 4.5 %collective-permute-start = (bf16[128,1024]{1,0:T(8,128)(2,1)S(1)}, bf16[128,1024]{1,0:T(8,128)(2,1)S(1)}, u32[]{:S(2)}, u32[]{:S(2)}) collective-permute-start(bf16[128,1024]{1,0:T(8,128)(2,1)S(1)} %get-tuple-element.83), channel_id=1, source_target_pairs={{0,8},{8,0},{1,9},{9,1},{2,10},{10,2},{3,11},{11,3},{4,12},{12,4},... | collective-permute-start | bytes 786440 | tf_op jit(solution)/shard_map/ppermute | solution.py:43
  6.8 7.6 %collective-permute-start.1 = (bf16[2,64,1024]{2,1,0:T(8,128)(2,1)S(1)}, bf16[2,64,1024]{2,1,0:T(8,128)(2,1)S(1)}, u32[]{:S(2)}, u32[]{:S(2)}) collective-permute-start(bf16[2,64,1024]{2,1,0:T(8,128)(2,1)S(1)} %get-tuple-element.44.refs_6_), channel_id=1, source_target_pairs={{0,4},{4,0},{16,20},{20,16},{1,5},{5,1},{17,21},{21,17},{2,6},{6,2... | collective-permute-start | bytes 786440 | tf_op jit(solution)/shard_map/ppermute | solution.py:43
  6.9 21.6 %collective-permute-start.6 = (bf16[4,64,1024]{2,1,0:T(8,128)(2,1)S(1)}, bf16[4,64,1024]{2,1,0:T(8,128)(2,1)S(1)}, u32[]{:S(2)}, u32[]{:S(2)}) collective-permute-start(bf16[4,64,1024]{2,1,0:T(8,128)(2,1)S(1)} %get-tuple-element.47), channel_id=1, source_target_pairs={{0,20},{4,16},{16,4},{20,0},{1,21},{5,17},{17,5},{21,1},{2,22},{6,... | collective-permute-start | bytes 1572872 | tf_op jit(solution)/shard_map/ppermute | solution.py:43
  8.4 10.2 %collective-permute-start.3 = (bf16[2,64,1024]{2,1,0:T(8,128)(2,1)S(1)}, bf16[2,64,1024]{2,1,0:T(8,128)(2,1)S(1)}, u32[]{:S(2)}, u32[]{:S(2)}) collective-permute-start(bf16[2,64,1024]{2,1,0:T(8,128)(2,1)S(1)} %get-tuple-element.43.refs_1_.refs_5_), channel_id=1, source_target_pairs={{0,224},{32,0},{64,32},{96,64},{128,96},{160,128},{192,160},{224,1... | collective-permute-start | bytes 786440 | tf_op jit(solution)/shard_map/ppermute | solution.py:48
  13.9 7.8 %collective-permute-start.2 = (bf16[2,64,1024]{2,1,0:T(8,128)(2,1)S(1)}, bf16[2,64,1024]{2,1,0:T(8,128)(2,1)S(1)}, u32[]{:S(2)}, u32[]{:S(2)}) collective-permute-start(bf16[2,64,1024]{2,1,0:T(8,128)(2,1)S(1)} %get-tuple-element.43.refs_1_.refs_5_), channel_id=1, source_target_pairs={{0,32},{32,64},{64,96},{96,128},{128,160},{160,192},{192,224},{224... | collective-permute-start | bytes 786440 | tf_op jit(solution)/shard_map/ppermute | solution.py:48
  14.4 10.0 %collective-permute-start.5 = (bf16[2,64,1024]{2,1,0:T(8,128)(2,1)S(1)}, bf16[2,64,1024]{2,1,0:T(8,128)(2,1)S(1)}, u32[]{:S(2)}, u32[]{:S(2)}) collective-permute-start(bf16[2,64,1024]{2,1,0:T(8,128)(2,1)S(1)} %collective-permute-done.1.refs_2_.refs_8_), channel_id=1, source_target_pairs={{0,224},{32,0},{64,32},{96,64},{128,96},{160,128},{192,160},{224,1... | collective-permute-start | bytes 786440 | tf_op jit(solution)/shard_map/ppermute | solution.py:48
  18.3 9.6 %collective-permute-start.4 = (bf16[2,64,1024]{2,1,0:T(8,128)(2,1)S(1)}, bf16[2,64,1024]{2,1,0:T(8,128)(2,1)S(1)}, u32[]{:S(2)}, u32[]{:S(2)}) collective-permute-start(bf16[2,64,1024]{2,1,0:T(8,128)(2,1)S(1)} %collective-permute-done.1.refs_2_.refs_8_), channel_id=1, source_target_pairs={{0,32},{32,64},{64,96},{96,128},{128,160},{160,192},{192,224},{224... | collective-permute-start | bytes 786440 | tf_op jit(solution)/shard_map/ppermute | solution.py:48
  28.5 13.4 %collective-permute-start.7 = (bf16[4,64,1024]{2,1,0:T(8,128)(2,1)S(1)}, bf16[4,64,1024]{2,1,0:T(8,128)(2,1)S(1)}, u32[]{:S(2)}, u32[]{:S(2)}) collective-permute-start(bf16[4,64,1024]{2,1,0:T(8,128)(2,1)S(1)} %get-tuple-element.48.refs_11_), channel_id=1, source_target_pairs={{0,32},{32,64},{64,96},{96,128},{128,160},{160,192},{192,224},{224... | collective-permute-start | bytes 1572872 | tf_op jit(solution)/shard_map/ppermute | solution.py:48
  28.6 13.3 %collective-permute-start.8 = (bf16[4,64,1024]{2,1,0:T(8,128)(2,1)S(1)}, bf16[4,64,1024]{2,1,0:T(8,128)(2,1)S(1)}, u32[]{:S(2)}, u32[]{:S(2)}) collective-permute-start(bf16[4,64,1024]{2,1,0:T(8,128)(2,1)S(1)} %get-tuple-element.49.refs_12_), channel_id=1, source_target_pairs={{0,224},{32,0},{64,32},{96,64},{128,96},{160,128},{192,160},{224,1... | collective-permute-start | bytes 1572872 | tf_op jit(solution)/shard_map/ppermute | solution.py:48
  31.2 12.7 %collective-permute-start.10 = (bf16[4,64,1024]{2,1,0:T(8,128)(2,1)S(1)}, bf16[4,64,1024]{2,1,0:T(8,128)(2,1)S(1)}, u32[]{:S(2)}, u32[]{:S(2)}) collective-permute-start(bf16[4,64,1024]{2,1,0:T(8,128)(2,1)S(1)} %get-tuple-element.47), channel_id=1, source_target_pairs={{0,16},{4,20},{16,0},{20,4},{1,17},{5,21},{17,1},{21,5},{2,18},{6,... | collective-permute-start | bytes 1572872 | tf_op jit(solution)/shard_map/ppermute | solution.py:43
  32.8 10.0 %collective-permute-start.9 = (f32[4,1024]{1,0:T(4,128)S(1)}, f32[4,1024]{1,0:T(4,128)S(1)}, u32[]{:S(2)}, u32[]{:S(2)}) collective-permute-start(f32[4,1024]{1,0:T(4,128)S(1)} %moments.4.refs_1_), channel_id=1, source_target_pairs={{0,128},{32,160},{64,192},{96,224},{128,0},{160,32},{192,64},{224,... | collective-permute-start | bytes 49160 | tf_op jit(solution)/shard_map/ppermute | solution.py:48
  44.0 11.5 %collective-permute-start.11 = (bf16[4,64,1024]{2,1,0:T(8,128)(2,1)S(1)}, bf16[4,64,1024]{2,1,0:T(8,128)(2,1)S(1)}, u32[]{:S(2)}, u32[]{:S(2)}) collective-permute-start(bf16[4,64,1024]{2,1,0:T(8,128)(2,1)S(1)} %collective-permute-done.7.refs_2_.refs_13_), channel_id=1, source_target_pairs={{0,32},{32,64},{64,96},{96,128},{128,160},{160,192},{192,224},{224... | collective-permute-start | bytes 1572872 | tf_op jit(solution)/shard_map/ppermute | solution.py:48
  44.0 11.5 %collective-permute-start.12 = (bf16[4,64,1024]{2,1,0:T(8,128)(2,1)S(1)}, bf16[4,64,1024]{2,1,0:T(8,128)(2,1)S(1)}, u32[]{:S(2)}, u32[]{:S(2)}) collective-permute-start(bf16[4,64,1024]{2,1,0:T(8,128)(2,1)S(1)} %collective-permute-done.8.refs_3_.refs_14_), channel_id=1, source_target_pairs={{0,224},{32,0},{64,32},{96,64},{128,96},{160,128},{192,160},{224,1... | collective-permute-start | bytes 1572872 | tf_op jit(solution)/shard_map/ppermute | solution.py:48
  46.7 5.5 %collective-permute-start.16 = (bf16[2,64,1024]{2,1,0:T(8,128)(2,1)S(1)}, bf16[2,64,1024]{2,1,0:T(8,128)(2,1)S(1)}, u32[]{:S(2)}, u32[]{:S(2)}) collective-permute-start(bf16[2,64,1024]{2,1,0:T(8,128)(2,1)S(1)} %get-tuple-element.43.refs_1_.refs_5_), channel_id=1, source_target_pairs={{0,4},{4,0},{16,20},{20,16},{1,5},{5,1},{17,21},{21,17},{2,6},{6,2... | collective-permute-start | bytes 786440 | tf_op jit(solution)/shard_map/ppermute | solution.py:43
  55.6 11.5 %collective-permute-start.18 = (bf16[2,64,1024]{2,1,0:T(8,128)(2,1)S(1)}, bf16[2,64,1024]{2,1,0:T(8,128)(2,1)S(1)}, u32[]{:S(2)}, u32[]{:S(2)}) collective-permute-start(bf16[2,64,1024]{2,1,0:T(8,128)(2,1)S(1)} %slice.14), channel_id=1, source_target_pairs={{0,224},{32,0},{64,32},{96,64},{128,96},{160,128},{192,160},{224,1... | collective-permute-start | bytes 786440 | tf_op jit(solution)/shard_map/ppermute | solution.py:48
  58.0 9.0 %collective-permute-start.17 = (bf16[2,64,1024]{2,1,0:T(8,128)(2,1)S(1)}, bf16[2,64,1024]{2,1,0:T(8,128)(2,1)S(1)}, u32[]{:S(2)}, u32[]{:S(2)}) collective-permute-start(bf16[2,64,1024]{2,1,0:T(8,128)(2,1)S(1)} %slice.13), channel_id=1, source_target_pairs={{0,32},{32,64},{64,96},{96,128},{128,160},{160,192},{192,224},{224... | collective-permute-start | bytes 786440 | tf_op jit(solution)/shard_map/ppermute | solution.py:48
  58.8 3.9 %collective-permute-start.15 = (f32[4,1024]{1,0:T(4,128)S(1)}, f32[4,1024]{1,0:T(4,128)S(1)}, u32[]{:S(2)}, u32[]{:S(2)}) collective-permute-start(f32[4,1024]{1,0:T(4,128)S(1)} %moments.7.refs_1_), channel_id=1, source_target_pairs={{0,20},{4,16},{16,4},{20,0},{1,21},{5,17},{17,5},{21,1},{2,22},{6,... | collective-permute-start | bytes 49160 | tf_op jit(solution)/shard_map/ppermute | solution.py:43
  58.9 4.2 %collective-permute-start.14 = (f32[4,1024]{1,0:T(4,128)S(1)}, f32[4,1024]{1,0:T(4,128)S(1)}, u32[]{:S(2)}, u32[]{:S(2)}) collective-permute-start(f32[4,1024]{1,0:T(4,128)S(1)} %moments.7.refs_1_), channel_id=1, source_target_pairs={{0,16},{4,20},{16,0},{20,4},{1,17},{5,21},{17,1},{21,5},{2,18},{6,... | collective-permute-start | bytes 49160 | tf_op jit(solution)/shard_map/ppermute | solution.py:43
  60.0 3.8 %collective-permute-start.13 = (f32[4,1024]{1,0:T(4,128)S(1)}, f32[4,1024]{1,0:T(4,128)S(1)}, u32[]{:S(2)}, u32[]{:S(2)}) collective-permute-start(f32[4,1024]{1,0:T(4,128)S(1)} %moments.7.refs_1_), channel_id=1, source_target_pairs={{0,4},{4,0},{16,20},{20,16},{1,5},{5,1},{17,21},{21,17},{2,6},{6,2... | collective-permute-start | bytes 49160 | tf_op jit(solution)/shard_map/ppermute | solution.py:43
  67.0 12.7 %copy-start = (bf16[128,1024]{1,0:T(8,128)(2,1)S(1)}, bf16[128,1024]{1,0:T(8,128)(2,1)}, u32[]{:S(2)}) copy-start(bf16[128,1024]{1,0:T(8,128)(2,1)} %view_b.1) | copy-start | bytes 786436
  67.0 12.7 %copy-start.1 = (bf16[128,1024]{1,0:T(8,128)(2,1)S(1)}, bf16[128,1024]{1,0:T(8,128)(2,1)}, u32[]{:S(2)}) copy-start(bf16[128,1024]{1,0:T(8,128)(2,1)} %view_a.1) | copy-start | bytes 786436
  68.5 17.7 %collective-permute-start.19 = (bf16[256,512]{1,0:T(8,128)(2,1)S(1)}, bf16[256,512]{1,0:T(8,128)(2,1)S(1)}, u32[]{:S(2)}, u32[]{:S(2)}) collective-permute-start(bf16[256,512]{1,0:T(8,128)(2,1)S(1)} %get-tuple-element.58), channel_id=1, source_target_pairs={{0,8},{1,9},{2,10},{3,11},{8,0},{9,1},{10,2},{11,3},{4,12},{5,13},... | collective-permute-start | bytes 786440 | tf_op jit(solution)/shard_map/ppermute | solution.py:43
  74.3 11.9 %collective-permute-start.23 = (bf16[256,512]{1,0:T(8,128)(2,1)S(1)}, bf16[256,512]{1,0:T(8,128)(2,1)S(1)}, u32[]{:S(2)}, u32[]{:S(2)}) collective-permute-start(bf16[256,512]{1,0:T(8,128)(2,1)S(1)} %get-tuple-element.61), channel_id=1, source_target_pairs={{0,9},{1,8},{2,11},{3,10},{8,1},{9,0},{10,3},{11,2},{4,13},{5,12},... | collective-permute-start | bytes 786440 | tf_op jit(solution)/shard_map/ppermute | solution.py:43
  75.5 14.7 %collective-permute-start.24 = (bf16[256,512]{1,0:T(8,128)(2,1)S(1)}, bf16[256,512]{1,0:T(8,128)(2,1)S(1)}, u32[]{:S(2)}, u32[]{:S(2)}) collective-permute-start(bf16[256,512]{1,0:T(8,128)(2,1)S(1)} %get-tuple-element.62), channel_id=1, source_target_pairs={{0,10},{1,11},{2,8},{3,9},{8,2},{9,3},{10,0},{11,1},{4,14},{5,15},... | collective-permute-start | bytes 786440 | tf_op jit(solution)/shard_map/ppermute | solution.py:43
  78.3 14.8 %collective-permute-start.25 = (bf16[256,512]{1,0:T(8,128)(2,1)S(1)}, bf16[256,512]{1,0:T(8,128)(2,1)S(1)}, u32[]{:S(2)}, u32[]{:S(2)}) collective-permute-start(bf16[256,512]{1,0:T(8,128)(2,1)S(1)} %get-tuple-element.63), channel_id=1, source_target_pairs={{0,11},{1,10},{2,9},{3,8},{8,3},{9,2},{10,1},{11,0},{4,15},{5,14},... | collective-permute-start | bytes 786440 | tf_op jit(solution)/shard_map/ppermute | solution.py:43
  78.4 1.3 collective-permute-start.20
  80.6 1.3 collective-permute-start.21
  81.8 4.4 %collective-permute-start.22 = (f32[4,1024]{1,0:T(4,128)S(1)}, f32[4,1024]{1,0:T(4,128)S(1)}, u32[]{:S(2)}, u32[]{:S(2)}) collective-permute-start(f32[4,1024]{1,0:T(4,128)S(1)} %add.43), channel_id=1, source_target_pairs={{0,16},{16,0},{1,17},{17,1},{2,18},{18,2},{3,19},{19,3},{4,20},{20... | collective-permute-start | bytes 49160 | tf_op jit(solution)/shard_map/ppermute | solution.py:43
  93.9 16.6 %collective-permute-start.30 = (bf16[512,256]{1,0:T(8,128)(2,1)S(1)}, bf16[512,256]{1,0:T(8,128)(2,1)S(1)}, u32[]{:S(2)}, u32[]{:S(2)}) collective-permute-start(bf16[512,256]{1,0:T(8,128)(2,1)S(1)} %get-tuple-element.64.refs_1_), channel_id=1, source_target_pairs={{0,8},{8,0},{1,9},{9,1},{2,10},{10,2},{3,11},{11,3},{4,12},{12,4},... | collective-permute-start | bytes 786440 | tf_op jit(solution)/shard_map/ppermute | solution.py:43
  94.1 16.4 %collective-permute-start.26 = (bf16[512,256]{1,0:T(8,128)(2,1)S(1)}, bf16[512,256]{1,0:T(8,128)(2,1)S(1)}, u32[]{:S(2)}, u32[]{:S(2)}) collective-permute-start(bf16[512,256]{1,0:T(8,128)(2,1)S(1)} %get-tuple-element.64.refs_1_), channel_id=1, source_target_pairs={{0,1},{1,0},{2,3},{3,2},{4,5},{5,4},{6,7},{7,6},{8,9},{9,8},{10,11... | collective-permute-start | bytes 786440 | tf_op jit(solution)/shard_map/ppermute | solution.py:43
  94.1 16.5 %collective-permute-start.32 = (bf16[512,256]{1,0:T(8,128)(2,1)S(1)}, bf16[512,256]{1,0:T(8,128)(2,1)S(1)}, u32[]{:S(2)}, u32[]{:S(2)}) collective-permute-start(bf16[512,256]{1,0:T(8,128)(2,1)S(1)} %get-tuple-element.64.refs_1_), channel_id=1, source_target_pairs={{0,3},{1,2},{2,1},{3,0},{4,7},{5,6},{6,5},{7,4},{8,11},{9,10},{10,... | collective-permute-start | bytes 786440 | tf_op jit(solution)/shard_map/ppermute | solution.py:43
  94.3 16.2 %collective-permute-start.31 = (bf16[512,256]{1,0:T(8,128)(2,1)S(1)}, bf16[512,256]{1,0:T(8,128)(2,1)S(1)}, u32[]{:S(2)}, u32[]{:S(2)}) collective-permute-start(bf16[512,256]{1,0:T(8,128)(2,1)S(1)} %get-tuple-element.64.refs_1_), channel_id=1, source_target_pairs={{0,2},{1,3},{2,0},{3,1},{4,6},{5,7},{6,4},{7,5},{8,10},{9,11},{10,... | collective-permute-start | bytes 786440 | tf_op jit(solution)/shard_map/ppermute | solution.py:43
  97.3 2.9 %collective-permute-start.27 = (f32[4,1024]{1,0:T(4,128)S(1)}, f32[4,1024]{1,0:T(4,128)S(1)}, u32[]{:S(2)}, u32[]{:S(2)}) collective-permute-start(f32[4,1024]{1,0:T(4,128)S(1)} %add.44), channel_id=1, source_target_pairs={{0,32},{32,0},{64,96},{96,64},{128,160},{160,128},{192,224},{224,1... | collective-permute-start | bytes 49160 | tf_op jit(solution)/shard_map/ppermute | solution.py:43
  100.2 3.8 %collective-permute-start.28 = (f32[4,1024]{1,0:T(4,128)S(1)}, f32[4,1024]{1,0:T(4,128)S(1)}, u32[]{:S(2)}, u32[]{:S(2)}) collective-permute-start(f32[4,1024]{1,0:T(4,128)S(1)} %add.45), channel_id=1, source_target_pairs={{0,64},{32,96},{64,0},{96,32},{128,192},{160,224},{192,128},{224,1... | collective-permute-start | bytes 49160 | tf_op jit(solution)/shard_map/ppermute | solution.py:43
  104.0 6.5 %collective-permute-start.29 = (f32[4,1024]{1,0:T(4,128)S(1)}, f32[4,1024]{1,0:T(4,128)S(1)}, u32[]{:S(2)}, u32[]{:S(2)}) collective-permute-start(f32[4,1024]{1,0:T(4,128)S(1)} %add.46), channel_id=1, source_target_pairs={{0,128},{32,160},{64,192},{96,224},{128,0},{160,32},{192,64},{224,... | collective-permute-start | bytes 49160 | tf_op jit(solution)/shard_map/ppermute | solution.py:43
  114.5 5.5 %collective-permute-start.35 = (f32[8,128]{1,0:T(8,128)S(1)}, f32[8,128]{1,0:T(8,128)S(1)}, u32[]{:S(2)}, u32[]{:S(2)}) collective-permute-start(f32[8,128]{1,0:T(8,128)S(1)} %loss.1), channel_id=1, source_target_pairs={{0,3},{1,2},{2,1},{3,0},{4,7},{5,6},{6,5},{7,4},{8,11},{9,10},{10,... | collective-permute-start | bytes 12296 | tf_op jit(solution)/shard_map/ppermute | solution.py:43
  114.9 6.3 %collective-permute-start.34 = (f32[8,128]{1,0:T(8,128)S(1)}, f32[8,128]{1,0:T(8,128)S(1)}, u32[]{:S(2)}, u32[]{:S(2)}) collective-permute-start(f32[8,128]{1,0:T(8,128)S(1)} %loss.1), channel_id=1, source_target_pairs={{0,2},{1,3},{2,0},{3,1},{4,6},{5,7},{6,4},{7,5},{8,10},{9,11},{10,... | collective-permute-start | bytes 12296 | tf_op jit(solution)/shard_map/ppermute | solution.py:43
  116.4 4.8 %collective-permute-start.33 = (f32[8,128]{1,0:T(8,128)S(1)}, f32[8,128]{1,0:T(8,128)S(1)}, u32[]{:S(2)}, u32[]{:S(2)}) collective-permute-start(f32[8,128]{1,0:T(8,128)S(1)} %loss.1), channel_id=1, source_target_pairs={{0,1},{1,0},{2,3},{3,2},{4,5},{5,4},{6,7},{7,6},{8,9},{9,8},{10,11... | collective-permute-start | bytes 12296 | tf_op jit(solution)/shard_map/ppermute | solution.py:43
  117.8 16.4 %collective-permute-start.39 = (bf16[256,1024]{1,0:T(8,128)(2,1)S(1)}, bf16[256,1024]{1,0:T(8,128)(2,1)S(1)}, u32[]{:S(2)}, u32[]{:S(2)}) collective-permute-start(bf16[256,1024]{1,0:T(8,128)(2,1)S(1)} %get-tuple-element.71), channel_id=1, source_target_pairs={{0,4},{4,0},{16,20},{20,16},{1,5},{5,1},{17,21},{21,17},{2,6},{6,2... | collective-permute-start | bytes 1572872 | tf_op jit(solution)/shard_map/ppermute | solution.py:43
  119.4 14.8 %collective-permute-start.40 = (bf16[256,1024]{1,0:T(8,128)(2,1)S(1)}, bf16[256,1024]{1,0:T(8,128)(2,1)S(1)}, u32[]{:S(2)}, u32[]{:S(2)}) collective-permute-start(bf16[256,1024]{1,0:T(8,128)(2,1)S(1)} %get-tuple-element.72), channel_id=1, source_target_pairs={{0,20},{4,16},{16,4},{20,0},{1,21},{5,17},{17,5},{21,1},{2,22},{6,... | collective-permute-start | bytes 1572872 | tf_op jit(solution)/shard_map/ppermute | solution.py:43
  120.0 19.4 %collective-permute-start.41 = (bf16[256,1024]{1,0:T(8,128)(2,1)S(1)}, bf16[256,1024]{1,0:T(8,128)(2,1)S(1)}, u32[]{:S(2)}, u32[]{:S(2)}) collective-permute-start(bf16[256,1024]{1,0:T(8,128)(2,1)S(1)} %get-tuple-element.73), channel_id=1, source_target_pairs={{0,16},{4,20},{16,0},{20,4},{1,17},{5,21},{17,1},{21,5},{2,18},{6,... | collective-permute-start | bytes 1572872 | tf_op jit(solution)/shard_map/ppermute | solution.py:43
  121.2 2.8 %collective-permute-start.36 = (f32[48,128]{1,0:T(8,128)S(1)}, f32[48,128]{1,0:T(8,128)S(1)}, u32[]{:S(2)}, u32[]{:S(2)}) collective-permute-start(f32[48,128]{1,0:T(8,128)S(1)} %pad_maximum_fusion), channel_id=1, source_target_pairs={{0,32},{32,0},{64,96},{96,64},{128,160},{160,128},{192,224},{224,1... | collective-permute-start | bytes 73736 | tf_op jit(solution)/shard_map/ppermute | solution.py:43
  124.0 3.6 %collective-permute-start.37 = (f32[48,128]{1,0:T(8,128)S(1)}, f32[48,128]{1,0:T(8,128)S(1)}, u32[]{:S(2)}, u32[]{:S(2)}) collective-permute-start(f32[48,128]{1,0:T(8,128)S(1)} %fusion), channel_id=1, source_target_pairs={{0,64},{32,96},{64,0},{96,32},{128,192},{160,224},{192,128},{224,1... | collective-permute-start | bytes 73736 | tf_op jit(solution)/shard_map/ppermute | solution.py:43
  127.6 6.6 %collective-permute-start.38 = (f32[48,128]{1,0:T(8,128)S(1)}, f32[48,128]{1,0:T(8,128)S(1)}, u32[]{:S(2)}, u32[]{:S(2)}) collective-permute-start(f32[48,128]{1,0:T(8,128)S(1)} %add.52), channel_id=1, source_target_pairs={{0,128},{32,160},{64,192},{96,224},{128,0},{160,32},{192,64},{224,... | collective-permute-start | bytes 73736 | tf_op jit(solution)/shard_map/ppermute | solution.py:43
  140.2 13.6 %collective-permute-start.46 = (bf16[128,1024]{1,0:T(8,128)(2,1)S(1)}, bf16[128,1024]{1,0:T(8,128)(2,1)S(1)}, u32[]{:S(2)}, u32[]{:S(2)}) collective-permute-start(bf16[128,1024]{1,0:T(8,128)(2,1)S(1)} %get-tuple-element.79), channel_id=1, source_target_pairs={{0,8},{8,0},{1,9},{9,1},{2,10},{10,2},{3,11},{11,3},{4,12},{12,4},... | collective-permute-start | bytes 786440 | tf_op jit(solution)/shard_map/ppermute | solution.py:43
  147.0 4.1 %collective-permute-start.42 = (f32[24,128]{1,0:T(8,128)S(1)}, f32[24,128]{1,0:T(8,128)S(1)}, u32[]{:S(2)}, u32[]{:S(2)}) collective-permute-start(f32[24,128]{1,0:T(8,128)S(1)} %get-tuple-element.85), channel_id=1, source_target_pairs={{0,16},{4,20},{16,0},{20,4},{1,17},{5,21},{17,1},{21,5},{2,18},{6,... | collective-permute-start | bytes 36872 | tf_op jit(solution)/shard_map/ppermute | solution.py:43
  147.7 4.1 %collective-permute-start.44 = (f32[24,128]{1,0:T(8,128)S(1)}, f32[24,128]{1,0:T(8,128)S(1)}, u32[]{:S(2)}, u32[]{:S(2)}) collective-permute-start(f32[24,128]{1,0:T(8,128)S(1)} %get-tuple-element.86), channel_id=1, source_target_pairs={{0,20},{4,16},{16,4},{20,0},{1,21},{5,17},{17,5},{21,1},{2,22},{6,... | collective-permute-start | bytes 36872 | tf_op jit(solution)/shard_map/ppermute | solution.py:43
  148.3 3.4 %collective-permute-start.43 = (f32[24,128]{1,0:T(8,128)S(1)}, f32[24,128]{1,0:T(8,128)S(1)}, u32[]{:S(2)}, u32[]{:S(2)}) collective-permute-start(f32[24,128]{1,0:T(8,128)S(1)} %get-tuple-element.86), channel_id=1, source_target_pairs={{0,4},{4,0},{16,20},{20,16},{1,5},{5,1},{17,21},{21,17},{2,6},{6,2... | collective-permute-start | bytes 36872 | tf_op jit(solution)/shard_map/ppermute | solution.py:43
  151.7 2.1 %collective-permute-start.45 = (f32[24,128]{1,0:T(8,128)S(1)}, f32[24,128]{1,0:T(8,128)S(1)}, u32[]{:S(2)}, u32[]{:S(2)}) collective-permute-start(f32[24,128]{1,0:T(8,128)S(1)} %add_add_fusion.refs_1_), channel_id=1, source_target_pairs={{0,8},{8,0},{1,9},{9,1},{2,10},{10,2},{3,11},{11,3},{4,12},{12,4},... | collective-permute-start | bytes 36872 | tf_op jit(solution)/shard_map/ppermute | solution.py:43
where the time goes:
time: 156 us
  waiting for transfers between devices  68.5 us (44%)
  starting transfers between devices  68 us (44%)
  Pallas kernels  16.9 us (11%)
    ppermute x36, starting transfers between devices, swap(): return lax.ppermute(values, axes, [(k, k ^ step) for k in range(count)])  49.1 us
    ppermute x36, waiting for transfers between devices, swap(): return lax.ppermute(values, axes, [(k, k ^ step) for k in range(count)])  48.8 us
    ppermute x11, waiting for transfers between devices, shift(): lax.ppermute(values, 'z', [(k, (k + steps) % count) for k in range(count)])  19.7 us
    ppermute x11, starting transfers between devices, shift(): lax.ppermute(values, 'z', [(k, (k + steps) % count) for k in range(count)])  18.9 us
    pallas_call x14, Pallas kernels, call(): pl.pallas_call(kernel, in_specs=[SMEM] + [VMEM] * len(args), out_specs=[V...  16.9 us
  transfers between devices with their start and end apart: 47, of which 28 were waited for; matrix products, arithmetic and copies ran while one was open for 0% of the time, Pallas kernels for 5%

commit v1 on v0

--- a/solution.py
+++ b/solution.py
@@ -375,6 +375,7 @@
     )
     sums = exchange_sum(sums, "c", (1,))
     sums = exchange_sum(sums, "yh", (1,))
+    sums = exchange_sum(sums, "z", (1,))
     come[0] = tie(come[0], sums)
     low_gram, gram = call(
         reduce_kernel,
@@ -384,7 +385,7 @@
         [shape(4 * count, piece, dtype=bf16), shape(4 * count, piece)],
     )
     full = [low_gram] + [swap(low_gram, "x", k) for k in range(1, peers)]
-    totals = exchange_sum(sums, "z", (1, 2, 4))
+    totals = exchange_sum(sums, "z", (2, 4))
     gram_other = swap(low_gram, "c", 1)
     full[1] = tie(full[1], totals, gram_other)
     lanes = width // 128

time: 156 us -> 154 us (0.987)
  starting transfers between devices: 68 us -> 64.4 us
  waiting for transfers between devices: 68.5 us -> 70.1 us
    ppermute x36, starting transfers between devices: 49.1 us -> 45.5 us  [swap(): return lax.ppermute(values, axes, [(k, k ^ step) for k in range(count)])]
    ppermute x36, waiting for transfers between devices: 48.8 us -> 50.4 us  [swap(): return lax.ppermute(values, axes, [(k, k ^ step) for k in range(count)])]
  transfers between devices with their start and end apart: 47 -> 47, of which waited for: 28 -> 29; matrix products, arithmetic and copies ran while one was open for 0% -> 0% of each run, Pallas kernels for 5% -> 5%
where the time goes in v1:
time: 154 us
  waiting for transfers between devices  70.1 us (46%)
  starting transfers between devices  64.4 us (42%)
  Pallas kernels  16.9 us (11%)
    ppermute x36, waiting for transfers between devices, swap(): return lax.ppermute(values, axes, [(k, k ^ step) for k in range(count)])  50.4 us
    ppermute x36, starting transfers between devices, swap(): return lax.ppermute(values, axes, [(k, k ^ step) for k in range(count)])  45.5 us
    ppermute x11, waiting for transfers between devices, shift(): lax.ppermute(values, 'z', [(k, (k + steps) % count) for k in range(count)])  19.7 us
    ppermute x11, starting transfers between devices, shift(): lax.ppermute(values, 'z', [(k, (k + steps) % count) for k in range(count)])  18.9 us
    pallas_call x14, Pallas kernels, call(): pl.pallas_call(kernel, in_specs=[SMEM] + [VMEM] * len(args), out_specs=[V...  16.9 us
  transfers between devices with their start and end apart: 47, of which 29 were waited for; matrix products, arithmetic and copies ran while one was open for 0% of the time, Pallas kernels for 5%

profile of v1, /device:TPU:1, one launch (start us, length us, event | category | flops | bytes accessed | tf_op | source)
XLA Modules:
  0.0 153.6 jit_solution(8606239673922093254)
XLA Ops:
  0.6 1.1 broadcast_select_fusion
  1.7 3.3 %collective-permute-start = (bf16[128,1024]{1,0:T(8,128)(2,1)S(1)}, bf16[128,1024]{1,0:T(8,128)(2,1)S(1)}, u32[]{:S(2)}, u32[]{:S(2)}) collective-permute-start(bf16[128,1024]{1,0:T(8,128)(2,1)S(1)} %get-tuple-element.83), channel_id=1, source_target_pairs={{0,8},{8,0},{1,9},{9,1},{2,10},{10,2},{3,11},{11,3},{4,12},{12,4},... | collective-permute-start | bytes 786440 | tf_op jit(solution)/shard_map/ppermute | solution.py:43
  5.1 1.1 collective-permute-done.got
  6.9 1.4 collective-permute-start.6
  8.4 5.6 %collective-permute-start.3 = (bf16[2,64,1024]{2,1,0:T(8,128)(2,1)S(1)}, bf16[2,64,1024]{2,1,0:T(8,128)(2,1)S(1)}, u32[]{:S(2)}, u32[]{:S(2)}) collective-permute-start(bf16[2,64,1024]{2,1,0:T(8,128)(2,1)S(1)} %get-tuple-element.43.refs_1_.refs_5_), channel_id=1, source_target_pairs={{0,224},{32,0},{64,32},{96,64},{128,96},{160,128},{192,160},{224,1... | collective-permute-start | bytes 786440 | tf_op jit(solution)/shard_map/ppermute | solution.py:48
  14.4 3.8 %collective-permute-start.5 = (bf16[2,64,1024]{2,1,0:T(8,128)(2,1)S(1)}, bf16[2,64,1024]{2,1,0:T(8,128)(2,1)S(1)}, u32[]{:S(2)}, u32[]{:S(2)}) collective-permute-start(bf16[2,64,1024]{2,1,0:T(8,128)(2,1)S(1)} %collective-permute-done.1.refs_2_.refs_8_), channel_id=1, source_target_pairs={{0,224},{32,0},{64,32},{96,64},{128,96},{160,128},{192,160},{224,1... | collective-permute-start | bytes 786440 | tf_op jit(solution)/shard_map/ppermute | solution.py:48
  18.6 3.1 %collective-permute-done.2.refs_2_.right_near = bf16[2,64,1024]{2,1,0:T(8,128)(2,1)S(1)} collective-permute-done((bf16[2,64,1024]{2,1,0:T(8,128)(2,1)S(1)}, bf16[2,64,1024]{2,1,0:T(8,128)(2,1)S(1)}, u32[]{:S(2)}, u32[]{:S(2)}) %collective-permute-start.2) | collective-permute-done | bytes 262176 | tf_op jit(solution)/shard_map/ppermute | solution.py:48
  21.7 2.7 %collective-permute-done.5.refs_5_.left_far = bf16[2,64,1024]{2,1,0:T(8,128)(2,1)S(1)} collective-permute-done((bf16[2,64,1024]{2,1,0:T(8,128)(2,1)S(1)}, bf16[2,64,1024]{2,1,0:T(8,128)(2,1)S(1)}, u32[]{:S(2)}, u32[]{:S(2)}) %collective-permute-start.5) | collective-permute-done | bytes 262176 | tf_op jit(solution)/shard_map/ppermute | solution.py:48
  24.5 3.4 %collective-permute-done.4.refs_4_.right_far = bf16[2,64,1024]{2,1,0:T(8,128)(2,1)S(1)} collective-permute-done((bf16[2,64,1024]{2,1,0:T(8,128)(2,1)S(1)}, bf16[2,64,1024]{2,1,0:T(8,128)(2,1)S(1)}, u32[]{:S(2)}, u32[]{:S(2)}) %collective-permute-start.4) | collective-permute-done | bytes 262176 | tf_op jit(solution)/shard_map/ppermute | solution.py:48
  28.6 2.7 %collective-permute-start.8 = (bf16[4,64,1024]{2,1,0:T(8,128)(2,1)S(1)}, bf16[4,64,1024]{2,1,0:T(8,128)(2,1)S(1)}, u32[]{:S(2)}, u32[]{:S(2)}) collective-permute-start(bf16[4,64,1024]{2,1,0:T(8,128)(2,1)S(1)} %get-tuple-element.49.refs_12_), channel_id=1, source_target_pairs={{0,224},{32,0},{64,32},{96,64},{128,96},{160,128},{192,160},{224,1... | collective-permute-start | bytes 1572872 | tf_op jit(solution)/shard_map/ppermute | solution.py:48
  31.2 0.8 collective-permute-start.10
  32.1 0.7 moments.4.refs_1_
  32.8 1.6 %collective-permute-start.9 = (f32[4,1024]{1,0:T(4,128)S(1)}, f32[4,1024]{1,0:T(4,128)S(1)}, u32[]{:S(2)}, u32[]{:S(2)}) collective-permute-start(f32[4,1024]{1,0:T(4,128)S(1)} %moments.4.refs_1_), channel_id=1, source_target_pairs={{0,128},{32,160},{64,192},{96,224},{128,0},{160,32},{192,64},{224,... | collective-permute-start | bytes 49160 | tf_op jit(solution)/shard_map/ppermute | solution.py:48
  34.4 0.8 moments.5.refs_1_
  35.2 6.7 %collective-permute-done.7.refs_2_.refs_13_ = bf16[4,64,1024]{2,1,0:T(8,128)(2,1)S(1)} collective-permute-done((bf16[4,64,1024]{2,1,0:T(8,128)(2,1)S(1)}, bf16[4,64,1024]{2,1,0:T(8,128)(2,1)S(1)}, u32[]{:S(2)}, u32[]{:S(2)}) %collective-permute-start.7) | collective-permute-done | bytes 524320 | tf_op jit(solution)/shard_map/ppermute | solution.py:48
  41.9 0.8 moments.6.refs_1_
  42.7 1.2 collective-permute-done.10.refs_7_
  44.0 2.7 %collective-permute-start.12 = (bf16[4,64,1024]{2,1,0:T(8,128)(2,1)S(1)}, bf16[4,64,1024]{2,1,0:T(8,128)(2,1)S(1)}, u32[]{:S(2)}, u32[]{:S(2)}) collective-permute-start(bf16[4,64,1024]{2,1,0:T(8,128)(2,1)S(1)} %collective-permute-done.8.refs_3_.refs_14_), channel_id=1, source_target_pairs={{0,224},{32,0},{64,32},{96,64},{128,96},{160,128},{192,160},{224,1... | collective-permute-start | bytes 1572872 | tf_op jit(solution)/shard_map/ppermute | solution.py:48
  46.7 5.5 %collective-permute-done.16.refs_9_ = bf16[2,64,1024]{2,1,0:T(8,128)(2,1)S(1)} collective-permute-done((bf16[2,64,1024]{2,1,0:T(8,128)(2,1)S(1)}, bf16[2,64,1024]{2,1,0:T(8,128)(2,1)S(1)}, u32[]{:S(2)}, u32[]{:S(2)}) %collective-permute-start.16) | collective-permute-done | bytes 262176 | tf_op jit(solution)/shard_map/ppermute | solution.py:43
  52.2 3.3 %collective-permute-done.11.refs_3_.refs_15_ = bf16[4,64,1024]{2,1,0:T(8,128)(2,1)S(1)} collective-permute-done((bf16[4,64,1024]{2,1,0:T(8,128)(2,1)S(1)}, bf16[4,64,1024]{2,1,0:T(8,128)(2,1)S(1)}, u32[]{:S(2)}, u32[]{:S(2)}) %collective-permute-start.11) | collective-permute-done | bytes 524320 | tf_op jit(solution)/shard_map/ppermute | solution.py:48
  55.6 2.5 %collective-permute-start.18 = (bf16[2,64,1024]{2,1,0:T(8,128)(2,1)S(1)}, bf16[2,64,1024]{2,1,0:T(8,128)(2,1)S(1)}, u32[]{:S(2)}, u32[]{:S(2)}) collective-permute-start(bf16[2,64,1024]{2,1,0:T(8,128)(2,1)S(1)} %slice.14), channel_id=1, source_target_pairs={{0,224},{32,0},{64,32},{96,64},{128,96},{160,128},{192,160},{224,1... | collective-permute-start | bytes 786440 | tf_op jit(solution)/shard_map/ppermute | solution.py:48
  58.0 0.8 moments.7.refs_1_
  58.9 1.0 collective-permute-start.14
  60.0 2.2 %collective-permute-start.13 = (f32[4,1024]{1,0:T(4,128)S(1)}, f32[4,1024]{1,0:T(4,128)S(1)}, u32[]{:S(2)}, u32[]{:S(2)}) collective-permute-start(f32[4,1024]{1,0:T(4,128)S(1)} %moments.7.refs_1_), channel_id=1, source_target_pairs={{0,4},{4,0},{16,20},{20,16},{1,5},{5,1},{17,21},{21,17},{2,6},{6,2... | collective-permute-start | bytes 49160 | tf_op jit(solution)/shard_map/ppermute | solution.py:43
  63.1 0.7 collective-permute-done.13.refs_2_
  63.8 3.2 %gram.1 = (bf16[3,256,512]{2,1,0:T(8,128)(2,1)S(1)}, bf16[1024,2048]{1,0:T(8,128)(2,1)S(1)}, bf16[512,2048]{1,0:T(8,128)(2,1)S(1)}, f32[4,1024]{1,0:T(4,128)S(1)}) custom-call(s32[3]{0:T(128)S(1)} %pad_add_fusion.ids.refs_0_, f32[4,1024]{1,0:T(4,128)S(1)} %moments.7.refs_1_, f32[4,1024]{1,0:T(4,128)S(1)} %collective-permute-done.13.refs_2_, ...), custom_call_target="tpu_custom_call" | custom-call | flops 1610612736 | tf_op jit(solution)/shard_map/gram/pallas_call | solution.py:28
  67.0 1.4 last_gram.1
  68.5 5.8 %collective-permute-start.19 = (bf16[256,512]{1,0:T(8,128)(2,1)S(1)}, bf16[256,512]{1,0:T(8,128)(2,1)S(1)}, u32[]{:S(2)}, u32[]{:S(2)}) collective-permute-start(bf16[256,512]{1,0:T(8,128)(2,1)S(1)} %get-tuple-element.58), channel_id=1, source_target_pairs={{0,8},{1,9},{2,10},{3,11},{8,0},{9,1},{10,2},{11,3},{4,12},{5,13},... | collective-permute-start | bytes 786440 | tf_op jit(solution)/shard_map/ppermute | solution.py:43
  74.3 1.2 collective-permute-start.24
  75.5 2.8 %collective-permute-start.25 = (bf16[256,512]{1,0:T(8,128)(2,1)S(1)}, bf16[256,512]{1,0:T(8,128)(2,1)S(1)}, u32[]{:S(2)}, u32[]{:S(2)}) collective-permute-start(bf16[256,512]{1,0:T(8,128)(2,1)S(1)} %get-tuple-element.62), channel_id=1, source_target_pairs={{0,10},{1,11},{2,8},{3,9},{8,2},{9,3},{10,0},{11,1},{4,14},{5,15},... | collective-permute-start | bytes 786440 | tf_op jit(solution)/shard_map/ppermute | solution.py:43
  78.9 0.8 collective-permute-done.20.theirs
  79.7 0.8 native.1
  81.0 0.8 collective-permute-done.21
  81.8 1.7 %collective-permute-start.22 = (f32[4,1024]{1,0:T(4,128)S(1)}, f32[4,1024]{1,0:T(4,128)S(1)}, u32[]{:S(2)}, u32[]{:S(2)}) collective-permute-start(f32[4,1024]{1,0:T(4,128)S(1)} %add.43), channel_id=1, source_target_pairs={{0,16},{16,0},{1,17},{17,1},{2,18},{18,2},{3,19},{19,3},{4,20},{20... | collective-permute-start | bytes 49160 | tf_op jit(solution)/shard_map/ppermute | solution.py:43
  83.6 2.6 %collective-permute-done.22 = f32[4,1024]{1,0:T(4,128)S(1)} collective-permute-done((f32[4,1024]{1,0:T(4,128)S(1)}, f32[4,1024]{1,0:T(4,128)S(1)}, u32[]{:S(2)}, u32[]{:S(2)}) %collective-permute-start.22) | collective-permute-done | bytes 16416 | tf_op jit(solution)/shard_map/ppermute | solution.py:43
  86.2 2.9 %collective-permute-done.23 = f32[4,1024]{1,0:T(4,128)S(1)} collective-permute-done((f32[4,1024]{1,0:T(4,128)S(1)}, f32[4,1024]{1,0:T(4,128)S(1)}, u32[]{:S(2)}, u32[]{:S(2)}) %collective-permute-start.23) | collective-permute-done | bytes 16416 | tf_op jit(solution)/shard_map/ppermute | solution.py:43
  89.1 1.1 collective-permute-done.25.refs_2_
  90.3 2.9 %collective-permute-done.26.refs_3_ = bf16[256,512]{1,0:T(8,128)(2,1)S(1)} collective-permute-done((bf16[256,512]{1,0:T(8,128)(2,1)S(1)}, bf16[256,512]{1,0:T(8,128)(2,1)S(1)}, u32[]{:S(2)}, u32[]{:S(2)}) %collective-permute-start.26) | collective-permute-done | bytes 262176 | tf_op jit(solution)/shard_map/ppermute | solution.py:43
  93.1 0.7 reduce.1
  94.5 2.8 %collective-permute-start.31 = (bf16[512,256]{1,0:T(8,128)(2,1)S(1)}, bf16[512,256]{1,0:T(8,128)(2,1)S(1)}, u32[]{:S(2)}, u32[]{:S(2)}) collective-permute-start(bf16[512,256]{1,0:T(8,128)(2,1)S(1)} %get-tuple-element.64.refs_1_), channel_id=1, source_target_pairs={{0,2},{1,3},{2,0},{3,1},{4,6},{5,7},{6,4},{7,5},{8,10},{9,11},{10,... | collective-permute-start | bytes 786440 | tf_op jit(solution)/shard_map/ppermute | solution.py:43
  97.3 3.8 %collective-permute-done.28 = f32[4,1024]{1,0:T(4,128)S(1)} collective-permute-done((f32[4,1024]{1,0:T(4,128)S(1)}, f32[4,1024]{1,0:T(4,128)S(1)}, u32[]{:S(2)}, u32[]{:S(2)}) %collective-permute-start.28) | collective-permute-done | bytes 16416 | tf_op jit(solution)/shard_map/ppermute | solution.py:43
  101.1 1.5 collective-permute-start.29
  102.6 5.0 %collective-permute-done.29 = f32[4,1024]{1,0:T(4,128)S(1)} collective-permute-done((f32[4,1024]{1,0:T(4,128)S(1)}, f32[4,1024]{1,0:T(4,128)S(1)}, u32[]{:S(2)}, u32[]{:S(2)}) %collective-permute-start.29) | collective-permute-done | bytes 16416 | tf_op jit(solution)/shard_map/ppermute | solution.py:43
  107.6 0.9 collective-permute-done.32.refs_4_
  108.6 3.1 %products.1 = (f32[256,1024]{1,0:T(8,128)S(1)}, bf16[256,1024]{1,0:T(8,128)(2,1)S(1)}, bf16[256,1024]{1,0:T(8,128)(2,1)S(1)}, bf16[256,1024]{1,0:T(8,128)(2,1)S(...) custom-call(s32[3]{0:T(128)S(1)} %pad_add_fusion.ids.refs_0_, bf16[512,256]{1,0:T(8,128)(2,1)S(1)} %get-tuple-element.64.refs_1_, ...), custom_call_target="tpu_custom_call" | custom-call | flops 2147483648 | tf_op jit(solution)/shard_map/products/pallas_call | solution.py:28
  111.7 0.8 loss.1
  112.5 1.1 collective-permute-start.35
  114.1 1.7 %collective-permute-start.33 = (f32[8,128]{1,0:T(8,128)S(1)}, f32[8,128]{1,0:T(8,128)S(1)}, u32[]{:S(2)}, u32[]{:S(2)}) collective-permute-start(f32[8,128]{1,0:T(8,128)S(1)} %loss.1), channel_id=1, source_target_pairs={{0,1},{1,0},{2,3},{3,2},{4,5},{5,4},{6,7},{7,6},{8,9},{9,8},{10,11... | collective-permute-start | bytes 12296 | tf_op jit(solution)/shard_map/ppermute | solution.py:43
  115.9 1.6 %collective-permute-start.39 = (bf16[256,1024]{1,0:T(8,128)(2,1)S(1)}, bf16[256,1024]{1,0:T(8,128)(2,1)S(1)}, u32[]{:S(2)}, u32[]{:S(2)}) collective-permute-start(bf16[256,1024]{1,0:T(8,128)(2,1)S(1)} %get-tuple-element.71), channel_id=1, source_target_pairs={{0,4},{4,0},{16,20},{20,16},{1,5},{5,1},{17,21},{21,17},{2,6},{6,2... | collective-permute-start | bytes 1572872 | tf_op jit(solution)/shard_map/ppermute | solution.py:43
  117.4 0.7 collective-permute-start.40
  118.1 1.2 collective-permute-start.41
  119.4 3.0 %collective-permute-done.36 = f32[48,128]{1,0:T(8,128)S(1)} collective-permute-done((f32[48,128]{1,0:T(8,128)S(1)}, f32[48,128]{1,0:T(8,128)S(1)}, u32[]{:S(2)}, u32[]{:S(2)}) %collective-permute-start.36) | collective-permute-done | bytes 24608 | tf_op jit(solution)/shard_map/ppermute | solution.py:43
  122.3 0.7 collective-permute-start.37
  123.1 3.1 %collective-permute-done.37 = f32[48,128]{1,0:T(8,128)S(1)} collective-permute-done((f32[48,128]{1,0:T(8,128)S(1)}, f32[48,128]{1,0:T(8,128)S(1)}, u32[]{:S(2)}, u32[]{:S(2)}) %collective-permute-start.37) | collective-permute-done | bytes 24608 | tf_op jit(solution)/shard_map/ppermute | solution.py:43
  126.2 2.4 %collective-permute-start.38 = (f32[48,128]{1,0:T(8,128)S(1)}, f32[48,128]{1,0:T(8,128)S(1)}, u32[]{:S(2)}, u32[]{:S(2)}) collective-permute-start(f32[48,128]{1,0:T(8,128)S(1)} %add.52), channel_id=1, source_target_pairs={{0,128},{32,160},{64,192},{96,224},{128,0},{160,32},{192,64},{224,... | collective-permute-start | bytes 73736 | tf_op jit(solution)/shard_map/ppermute | solution.py:43
  128.6 4.2 %collective-permute-done.38 = f32[48,128]{1,0:T(8,128)S(1)} collective-permute-done((f32[48,128]{1,0:T(8,128)S(1)}, f32[48,128]{1,0:T(8,128)S(1)}, u32[]{:S(2)}, u32[]{:S(2)}) %collective-permute-start.38) | collective-permute-done | bytes 24608 | tf_op jit(solution)/shard_map/ppermute | solution.py:43
  132.8 6.5 %collective-permute-done.41.refs_2_ = bf16[256,1024]{1,0:T(8,128)(2,1)S(1)} collective-permute-done((bf16[256,1024]{1,0:T(8,128)(2,1)S(1)}, bf16[256,1024]{1,0:T(8,128)(2,1)S(1)}, u32[]{:S(2)}, u32[]{:S(2)}) %collective-permute-start.41) | collective-permute-done | bytes 524320 | tf_op jit(solution)/shard_map/ppermute | solution.py:43
  139.3 0.8 add.68
  140.1 5.0 %collective-permute-start.46 = (bf16[128,1024]{1,0:T(8,128)(2,1)S(1)}, bf16[128,1024]{1,0:T(8,128)(2,1)S(1)}, u32[]{:S(2)}, u32[]{:S(2)}) collective-permute-start(bf16[128,1024]{1,0:T(8,128)(2,1)S(1)} %get-tuple-element.79), channel_id=1, source_target_pairs={{0,8},{8,0},{1,9},{9,1},{2,10},{10,2},{3,11},{11,3},{4,12},{12,4},... | collective-permute-start | bytes 786440 | tf_op jit(solution)/shard_map/ppermute | solution.py:43
  146.3 1.4 collective-permute-start.43
  147.7 1.4 collective-permute-done.42
  149.8 1.3 collective-permute-start.45
  151.1 0.8 collective-permute-done.45.refs_2_
  151.9 1.7 %finish.1 = (bf16[128,1024]{1,0:T(8,128)(2,1)}, bf16[128,1024]{1,0:T(8,128)(2,1)}, f32[1,128]{1,0:T(1,128)}) custom-call(s32[3]{0:T(128)S(1)} %pad_add_fusion.ids.refs_0_, f32[24,128]{1,0:T(8,128)S(1)} %add_add_fusion.refs_1_, f32[24,128]{1,0:T(8,128)S(1)} %collective-permute-done.45.refs_2_, f32[4,1024]{1,0:T(4,128)S(1)} %add.47.refs_3_, ...), custom_call_target="tpu_custom_call" | custom-call | tf_op jit(solution)/shard_map/finish/pallas_call | solution.py:28
  (65 shorter events, 7.7 us)
Async XLA Ops:
  1.7 4.5 %collective-permute-start = (bf16[128,1024]{1,0:T(8,128)(2,1)S(1)}, bf16[128,1024]{1,0:T(8,128)(2,1)S(1)}, u32[]{:S(2)}, u32[]{:S(2)}) collective-permute-start(bf16[128,1024]{1,0:T(8,128)(2,1)S(1)} %get-tuple-element.83), channel_id=1, source_target_pairs={{0,8},{8,0},{1,9},{9,1},{2,10},{10,2},{3,11},{11,3},{4,12},{12,4},... | collective-permute-start | bytes 786440 | tf_op jit(solution)/shard_map/ppermute | solution.py:43
  6.8 7.6 %collective-permute-start.1 = (bf16[2,64,1024]{2,1,0:T(8,128)(2,1)S(1)}, bf16[2,64,1024]{2,1,0:T(8,128)(2,1)S(1)}, u32[]{:S(2)}, u32[]{:S(2)}) collective-permute-start(bf16[2,64,1024]{2,1,0:T(8,128)(2,1)S(1)} %get-tuple-element.44.refs_6_), channel_id=1, source_target_pairs={{0,4},{4,0},{16,20},{20,16},{1,5},{5,1},{17,21},{21,17},{2,6},{6,2... | collective-permute-start | bytes 786440 | tf_op jit(solution)/shard_map/ppermute | solution.py:43
  6.9 21.6 %collective-permute-start.6 = (bf16[4,64,1024]{2,1,0:T(8,128)(2,1)S(1)}, bf16[4,64,1024]{2,1,0:T(8,128)(2,1)S(1)}, u32[]{:S(2)}, u32[]{:S(2)}) collective-permute-start(bf16[4,64,1024]{2,1,0:T(8,128)(2,1)S(1)} %get-tuple-element.47), channel_id=1, source_target_pairs={{0,20},{4,16},{16,4},{20,0},{1,21},{5,17},{17,5},{21,1},{2,22},{6,... | collective-permute-start | bytes 1572872 | tf_op jit(solution)/shard_map/ppermute | solution.py:43
  8.4 10.2 %collective-permute-start.3 = (bf16[2,64,1024]{2,1,0:T(8,128)(2,1)S(1)}, bf16[2,64,1024]{2,1,0:T(8,128)(2,1)S(1)}, u32[]{:S(2)}, u32[]{:S(2)}) collective-permute-start(bf16[2,64,1024]{2,1,0:T(8,128)(2,1)S(1)} %get-tuple-element.43.refs_1_.refs_5_), channel_id=1, source_target_pairs={{0,224},{32,0},{64,32},{96,64},{128,96},{160,128},{192,160},{224,1... | collective-permute-start | bytes 786440 | tf_op jit(solution)/shard_map/ppermute | solution.py:48
  13.9 7.8 %collective-permute-start.2 = (bf16[2,64,1024]{2,1,0:T(8,128)(2,1)S(1)}, bf16[2,64,1024]{2,1,0:T(8,128)(2,1)S(1)}, u32[]{:S(2)}, u32[]{:S(2)}) collective-permute-start(bf16[2,64,1024]{2,1,0:T(8,128)(2,1)S(1)} %get-tuple-element.43.refs_1_.refs_5_), channel_id=1, source_target_pairs={{0,32},{32,64},{64,96},{96,128},{128,160},{160,192},{192,224},{224... | collective-permute-start | bytes 786440 | tf_op jit(solution)/shard_map/ppermute | solution.py:48
  14.4 10.0 %collective-permute-start.5 = (bf16[2,64,1024]{2,1,0:T(8,128)(2,1)S(1)}, bf16[2,64,1024]{2,1,0:T(8,128)(2,1)S(1)}, u32[]{:S(2)}, u32[]{:S(2)}) collective-permute-start(bf16[2,64,1024]{2,1,0:T(8,128)(2,1)S(1)} %collective-permute-done.1.refs_2_.refs_8_), channel_id=1, source_target_pairs={{0,224},{32,0},{64,32},{96,64},{128,96},{160,128},{192,160},{224,1... | collective-permute-start | bytes 786440 | tf_op jit(solution)/shard_map/ppermute | solution.py:48
  18.3 9.6 %collective-permute-start.4 = (bf16[2,64,1024]{2,1,0:T(8,128)(2,1)S(1)}, bf16[2,64,1024]{2,1,0:T(8,128)(2,1)S(1)}, u32[]{:S(2)}, u32[]{:S(2)}) collective-permute-start(bf16[2,64,1024]{2,1,0:T(8,128)(2,1)S(1)} %collective-permute-done.1.refs_2_.refs_8_), channel_id=1, source_target_pairs={{0,32},{32,64},{64,96},{96,128},{128,160},{160,192},{192,224},{224... | collective-permute-start | bytes 786440 | tf_op jit(solution)/shard_map/ppermute | solution.py:48
  28.5 13.4 %collective-permute-start.7 = (bf16[4,64,1024]{2,1,0:T(8,128)(2,1)S(1)}, bf16[4,64,1024]{2,1,0:T(8,128)(2,1)S(1)}, u32[]{:S(2)}, u32[]{:S(2)}) collective-permute-start(bf16[4,64,1024]{2,1,0:T(8,128)(2,1)S(1)} %get-tuple-element.48.refs_11_), channel_id=1, source_target_pairs={{0,32},{32,64},{64,96},{96,128},{128,160},{160,192},{192,224},{224... | collective-permute-start | bytes 1572872 | tf_op jit(solution)/shard_map/ppermute | solution.py:48
  28.6 13.3 %collective-permute-start.8 = (bf16[4,64,1024]{2,1,0:T(8,128)(2,1)S(1)}, bf16[4,64,1024]{2,1,0:T(8,128)(2,1)S(1)}, u32[]{:S(2)}, u32[]{:S(2)}) collective-permute-start(bf16[4,64,1024]{2,1,0:T(8,128)(2,1)S(1)} %get-tuple-element.49.refs_12_), channel_id=1, source_target_pairs={{0,224},{32,0},{64,32},{96,64},{128,96},{160,128},{192,160},{224,1... | collective-permute-start | bytes 1572872 | tf_op jit(solution)/shard_map/ppermute | solution.py:48
  31.2 12.7 %collective-permute-start.10 = (bf16[4,64,1024]{2,1,0:T(8,128)(2,1)S(1)}, bf16[4,64,1024]{2,1,0:T(8,128)(2,1)S(1)}, u32[]{:S(2)}, u32[]{:S(2)}) collective-permute-start(bf16[4,64,1024]{2,1,0:T(8,128)(2,1)S(1)} %get-tuple-element.47), channel_id=1, source_target_pairs={{0,16},{4,20},{16,0},{20,4},{1,17},{5,21},{17,1},{21,5},{2,18},{6,... | collective-permute-start | bytes 1572872 | tf_op jit(solution)/shard_map/ppermute | solution.py:43
  32.8 10.0 %collective-permute-start.9 = (f32[4,1024]{1,0:T(4,128)S(1)}, f32[4,1024]{1,0:T(4,128)S(1)}, u32[]{:S(2)}, u32[]{:S(2)}) collective-permute-start(f32[4,1024]{1,0:T(4,128)S(1)} %moments.4.refs_1_), channel_id=1, source_target_pairs={{0,128},{32,160},{64,192},{96,224},{128,0},{160,32},{192,64},{224,... | collective-permute-start | bytes 49160 | tf_op jit(solution)/shard_map/ppermute | solution.py:48
  44.0 11.5 %collective-permute-start.11 = (bf16[4,64,1024]{2,1,0:T(8,128)(2,1)S(1)}, bf16[4,64,1024]{2,1,0:T(8,128)(2,1)S(1)}, u32[]{:S(2)}, u32[]{:S(2)}) collective-permute-start(bf16[4,64,1024]{2,1,0:T(8,128)(2,1)S(1)} %collective-permute-done.7.refs_2_.refs_13_), channel_id=1, source_target_pairs={{0,32},{32,64},{64,96},{96,128},{128,160},{160,192},{192,224},{224... | collective-permute-start | bytes 1572872 | tf_op jit(solution)/shard_map/ppermute | solution.py:48
  44.0 11.5 %collective-permute-start.12 = (bf16[4,64,1024]{2,1,0:T(8,128)(2,1)S(1)}, bf16[4,64,1024]{2,1,0:T(8,128)(2,1)S(1)}, u32[]{:S(2)}, u32[]{:S(2)}) collective-permute-start(bf16[4,64,1024]{2,1,0:T(8,128)(2,1)S(1)} %collective-permute-done.8.refs_3_.refs_14_), channel_id=1, source_target_pairs={{0,224},{32,0},{64,32},{96,64},{128,96},{160,128},{192,160},{224,1... | collective-permute-start | bytes 1572872 | tf_op jit(solution)/shard_map/ppermute | solution.py:48
  46.7 5.5 %collective-permute-start.16 = (bf16[2,64,1024]{2,1,0:T(8,128)(2,1)S(1)}, bf16[2,64,1024]{2,1,0:T(8,128)(2,1)S(1)}, u32[]{:S(2)}, u32[]{:S(2)}) collective-permute-start(bf16[2,64,1024]{2,1,0:T(8,128)(2,1)S(1)} %get-tuple-element.43.refs_1_.refs_5_), channel_id=1, source_target_pairs={{0,4},{4,0},{16,20},{20,16},{1,5},{5,1},{17,21},{21,17},{2,6},{6,2... | collective-permute-start | bytes 786440 | tf_op jit(solution)/shard_map/ppermute | solution.py:43
  55.6 11.5 %collective-permute-start.18 = (bf16[2,64,1024]{2,1,0:T(8,128)(2,1)S(1)}, bf16[2,64,1024]{2,1,0:T(8,128)(2,1)S(1)}, u32[]{:S(2)}, u32[]{:S(2)}) collective-permute-start(bf16[2,64,1024]{2,1,0:T(8,128)(2,1)S(1)} %slice.14), channel_id=1, source_target_pairs={{0,224},{32,0},{64,32},{96,64},{128,96},{160,128},{192,160},{224,1... | collective-permute-start | bytes 786440 | tf_op jit(solution)/shard_map/ppermute | solution.py:48
  58.0 9.0 %collective-permute-start.17 = (bf16[2,64,1024]{2,1,0:T(8,128)(2,1)S(1)}, bf16[2,64,1024]{2,1,0:T(8,128)(2,1)S(1)}, u32[]{:S(2)}, u32[]{:S(2)}) collective-permute-start(bf16[2,64,1024]{2,1,0:T(8,128)(2,1)S(1)} %slice.13), channel_id=1, source_target_pairs={{0,32},{32,64},{64,96},{96,128},{128,160},{160,192},{192,224},{224... | collective-permute-start | bytes 786440 | tf_op jit(solution)/shard_map/ppermute | solution.py:48
  58.8 3.9 %collective-permute-start.15 = (f32[4,1024]{1,0:T(4,128)S(1)}, f32[4,1024]{1,0:T(4,128)S(1)}, u32[]{:S(2)}, u32[]{:S(2)}) collective-permute-start(f32[4,1024]{1,0:T(4,128)S(1)} %moments.7.refs_1_), channel_id=1, source_target_pairs={{0,20},{4,16},{16,4},{20,0},{1,21},{5,17},{17,5},{21,1},{2,22},{6,... | collective-permute-start | bytes 49160 | tf_op jit(solution)/shard_map/ppermute | solution.py:43
  58.9 4.2 %collective-permute-start.14 = (f32[4,1024]{1,0:T(4,128)S(1)}, f32[4,1024]{1,0:T(4,128)S(1)}, u32[]{:S(2)}, u32[]{:S(2)}) collective-permute-start(f32[4,1024]{1,0:T(4,128)S(1)} %moments.7.refs_1_), channel_id=1, source_target_pairs={{0,16},{4,20},{16,0},{20,4},{1,17},{5,21},{17,1},{21,5},{2,18},{6,... | collective-permute-start | bytes 49160 | tf_op jit(solution)/shard_map/ppermute | solution.py:43
  60.0 3.8 %collective-permute-start.13 = (f32[4,1024]{1,0:T(4,128)S(1)}, f32[4,1024]{1,0:T(4,128)S(1)}, u32[]{:S(2)}, u32[]{:S(2)}) collective-permute-start(f32[4,1024]{1,0:T(4,128)S(1)} %moments.7.refs_1_), channel_id=1, source_target_pairs={{0,4},{4,0},{16,20},{20,16},{1,5},{5,1},{17,21},{21,17},{2,6},{6,2... | collective-permute-start | bytes 49160 | tf_op jit(solution)/shard_map/ppermute | solution.py:43
  67.0 12.7 %copy-start = (bf16[128,1024]{1,0:T(8,128)(2,1)S(1)}, bf16[128,1024]{1,0:T(8,128)(2,1)}, u32[]{:S(2)}) copy-start(bf16[128,1024]{1,0:T(8,128)(2,1)} %view_b.1) | copy-start | bytes 786436
  67.0 12.7 %copy-start.1 = (bf16[128,1024]{1,0:T(8,128)(2,1)S(1)}, bf16[128,1024]{1,0:T(8,128)(2,1)}, u32[]{:S(2)}) copy-start(bf16[128,1024]{1,0:T(8,128)(2,1)} %view_a.1) | copy-start | bytes 786436
  68.5 20.6 %collective-permute-start.19 = (bf16[256,512]{1,0:T(8,128)(2,1)S(1)}, bf16[256,512]{1,0:T(8,128)(2,1)S(1)}, u32[]{:S(2)}, u32[]{:S(2)}) collective-permute-start(bf16[256,512]{1,0:T(8,128)(2,1)S(1)} %get-tuple-element.58), channel_id=1, source_target_pairs={{0,8},{1,9},{2,10},{3,11},{8,0},{9,1},{10,2},{11,3},{4,12},{5,13},... | collective-permute-start | bytes 786440 | tf_op jit(solution)/shard_map/ppermute | solution.py:43
  74.3 14.8 %collective-permute-start.24 = (bf16[256,512]{1,0:T(8,128)(2,1)S(1)}, bf16[256,512]{1,0:T(8,128)(2,1)S(1)}, u32[]{:S(2)}, u32[]{:S(2)}) collective-permute-start(bf16[256,512]{1,0:T(8,128)(2,1)S(1)} %get-tuple-element.61), channel_id=1, source_target_pairs={{0,9},{1,8},{2,11},{3,10},{8,1},{9,0},{10,3},{11,2},{4,13},{5,12},... | collective-permute-start | bytes 786440 | tf_op jit(solution)/shard_map/ppermute | solution.py:43
  75.5 14.7 %collective-permute-start.25 = (bf16[256,512]{1,0:T(8,128)(2,1)S(1)}, bf16[256,512]{1,0:T(8,128)(2,1)S(1)}, u32[]{:S(2)}, u32[]{:S(2)}) collective-permute-start(bf16[256,512]{1,0:T(8,128)(2,1)S(1)} %get-tuple-element.62), channel_id=1, source_target_pairs={{0,10},{1,11},{2,8},{3,9},{8,2},{9,3},{10,0},{11,1},{4,14},{5,15},... | collective-permute-start | bytes 786440 | tf_op jit(solution)/shard_map/ppermute | solution.py:43
  78.3 14.8 %collective-permute-start.26 = (bf16[256,512]{1,0:T(8,128)(2,1)S(1)}, bf16[256,512]{1,0:T(8,128)(2,1)S(1)}, u32[]{:S(2)}, u32[]{:S(2)}) collective-permute-start(bf16[256,512]{1,0:T(8,128)(2,1)S(1)} %get-tuple-element.63), channel_id=1, source_target_pairs={{0,11},{1,10},{2,9},{3,8},{8,3},{9,2},{10,1},{11,0},{4,15},{5,14},... | collective-permute-start | bytes 786440 | tf_op jit(solution)/shard_map/ppermute | solution.py:43
  78.4 1.3 collective-permute-start.20
  80.6 1.3 collective-permute-start.21
  81.8 4.4 %collective-permute-start.22 = (f32[4,1024]{1,0:T(4,128)S(1)}, f32[4,1024]{1,0:T(4,128)S(1)}, u32[]{:S(2)}, u32[]{:S(2)}) collective-permute-start(f32[4,1024]{1,0:T(4,128)S(1)} %add.43), channel_id=1, source_target_pairs={{0,16},{16,0},{1,17},{17,1},{2,18},{18,2},{3,19},{19,3},{4,20},{20... | collective-permute-start | bytes 49160 | tf_op jit(solution)/shard_map/ppermute | solution.py:43
  86.2 2.9 %collective-permute-start.23 = (f32[4,1024]{1,0:T(4,128)S(1)}, f32[4,1024]{1,0:T(4,128)S(1)}, u32[]{:S(2)}, u32[]{:S(2)}) collective-permute-start(f32[4,1024]{1,0:T(4,128)S(1)} %add.44), channel_id=1, source_target_pairs={{0,32},{32,0},{64,96},{96,64},{128,160},{160,128},{192,224},{224,1... | collective-permute-start | bytes 49160 | tf_op jit(solution)/shard_map/ppermute | solution.py:43
  93.9 13.8 %collective-permute-start.30 = (bf16[512,256]{1,0:T(8,128)(2,1)S(1)}, bf16[512,256]{1,0:T(8,128)(2,1)S(1)}, u32[]{:S(2)}, u32[]{:S(2)}) collective-permute-start(bf16[512,256]{1,0:T(8,128)(2,1)S(1)} %get-tuple-element.64.refs_1_), channel_id=1, source_target_pairs={{0,8},{8,0},{1,9},{9,1},{2,10},{10,2},{3,11},{11,3},{4,12},{12,4},... | collective-permute-start | bytes 786440 | tf_op jit(solution)/shard_map/ppermute | solution.py:43
  94.1 13.6 %collective-permute-start.27 = (bf16[512,256]{1,0:T(8,128)(2,1)S(1)}, bf16[512,256]{1,0:T(8,128)(2,1)S(1)}, u32[]{:S(2)}, u32[]{:S(2)}) collective-permute-start(bf16[512,256]{1,0:T(8,128)(2,1)S(1)} %get-tuple-element.64.refs_1_), channel_id=1, source_target_pairs={{0,1},{1,0},{2,3},{3,2},{4,5},{5,4},{6,7},{7,6},{8,9},{9,8},{10,11... | collective-permute-start | bytes 786440 | tf_op jit(solution)/shard_map/ppermute | solution.py:43
  94.1 14.5 %collective-permute-start.32 = (bf16[512,256]{1,0:T(8,128)(2,1)S(1)}, bf16[512,256]{1,0:T(8,128)(2,1)S(1)}, u32[]{:S(2)}, u32[]{:S(2)}) collective-permute-start(bf16[512,256]{1,0:T(8,128)(2,1)S(1)} %get-tuple-element.64.refs_1_), channel_id=1, source_target_pairs={{0,3},{1,2},{2,1},{3,0},{4,7},{5,6},{6,5},{7,4},{8,11},{9,10},{10,... | collective-permute-start | bytes 786440 | tf_op jit(solution)/shard_map/ppermute | solution.py:43
  94.5 14.0 %collective-permute-start.31 = (bf16[512,256]{1,0:T(8,128)(2,1)S(1)}, bf16[512,256]{1,0:T(8,128)(2,1)S(1)}, u32[]{:S(2)}, u32[]{:S(2)}) collective-permute-start(bf16[512,256]{1,0:T(8,128)(2,1)S(1)} %get-tuple-element.64.refs_1_), channel_id=1, source_target_pairs={{0,2},{1,3},{2,0},{3,1},{4,6},{5,7},{6,4},{7,5},{8,10},{9,11},{10,... | collective-permute-start | bytes 786440 | tf_op jit(solution)/shard_map/ppermute | solution.py:43
  97.3 3.8 %collective-permute-start.28 = (f32[4,1024]{1,0:T(4,128)S(1)}, f32[4,1024]{1,0:T(4,128)S(1)}, u32[]{:S(2)}, u32[]{:S(2)}) collective-permute-start(f32[4,1024]{1,0:T(4,128)S(1)} %add.45), channel_id=1, source_target_pairs={{0,64},{32,96},{64,0},{96,32},{128,192},{160,224},{192,128},{224,1... | collective-permute-start | bytes 49160 | tf_op jit(solution)/shard_map/ppermute | solution.py:43
  101.1 6.5 %collective-permute-start.29 = (f32[4,1024]{1,0:T(4,128)S(1)}, f32[4,1024]{1,0:T(4,128)S(1)}, u32[]{:S(2)}, u32[]{:S(2)}) collective-permute-start(f32[4,1024]{1,0:T(4,128)S(1)} %add.46), channel_id=1, source_target_pairs={{0,128},{32,160},{64,192},{96,224},{128,0},{160,32},{192,64},{224,... | collective-permute-start | bytes 49160 | tf_op jit(solution)/shard_map/ppermute | solution.py:43
  112.5 5.5 %collective-permute-start.35 = (f32[8,128]{1,0:T(8,128)S(1)}, f32[8,128]{1,0:T(8,128)S(1)}, u32[]{:S(2)}, u32[]{:S(2)}) collective-permute-start(f32[8,128]{1,0:T(8,128)S(1)} %loss.1), channel_id=1, source_target_pairs={{0,3},{1,2},{2,1},{3,0},{4,7},{5,6},{6,5},{7,4},{8,11},{9,10},{10,... | collective-permute-start | bytes 12296 | tf_op jit(solution)/shard_map/ppermute | solution.py:43
  113.6 5.6 %collective-permute-start.34 = (f32[8,128]{1,0:T(8,128)S(1)}, f32[8,128]{1,0:T(8,128)S(1)}, u32[]{:S(2)}, u32[]{:S(2)}) collective-permute-start(f32[8,128]{1,0:T(8,128)S(1)} %loss.1), channel_id=1, source_target_pairs={{0,2},{1,3},{2,0},{3,1},{4,6},{5,7},{6,4},{7,5},{8,10},{9,11},{10,... | collective-permute-start | bytes 12296 | tf_op jit(solution)/shard_map/ppermute | solution.py:43
  114.1 5.1 %collective-permute-start.33 = (f32[8,128]{1,0:T(8,128)S(1)}, f32[8,128]{1,0:T(8,128)S(1)}, u32[]{:S(2)}, u32[]{:S(2)}) collective-permute-start(f32[8,128]{1,0:T(8,128)S(1)} %loss.1), channel_id=1, source_target_pairs={{0,1},{1,0},{2,3},{3,2},{4,5},{5,4},{6,7},{7,6},{8,9},{9,8},{10,11... | collective-permute-start | bytes 12296 | tf_op jit(solution)/shard_map/ppermute | solution.py:43
  115.9 17.0 %collective-permute-start.39 = (bf16[256,1024]{1,0:T(8,128)(2,1)S(1)}, bf16[256,1024]{1,0:T(8,128)(2,1)S(1)}, u32[]{:S(2)}, u32[]{:S(2)}) collective-permute-start(bf16[256,1024]{1,0:T(8,128)(2,1)S(1)} %get-tuple-element.71), channel_id=1, source_target_pairs={{0,4},{4,0},{16,20},{20,16},{1,5},{5,1},{17,21},{21,17},{2,6},{6,2... | collective-permute-start | bytes 1572872 | tf_op jit(solution)/shard_map/ppermute | solution.py:43
  117.4 15.4 %collective-permute-start.40 = (bf16[256,1024]{1,0:T(8,128)(2,1)S(1)}, bf16[256,1024]{1,0:T(8,128)(2,1)S(1)}, u32[]{:S(2)}, u32[]{:S(2)}) collective-permute-start(bf16[256,1024]{1,0:T(8,128)(2,1)S(1)} %get-tuple-element.72), channel_id=1, source_target_pairs={{0,20},{4,16},{16,4},{20,0},{1,21},{5,17},{17,5},{21,1},{2,22},{6,... | collective-permute-start | bytes 1572872 | tf_op jit(solution)/shard_map/ppermute | solution.py:43
  118.1 21.2 %collective-permute-start.41 = (bf16[256,1024]{1,0:T(8,128)(2,1)S(1)}, bf16[256,1024]{1,0:T(8,128)(2,1)S(1)}, u32[]{:S(2)}, u32[]{:S(2)}) collective-permute-start(bf16[256,1024]{1,0:T(8,128)(2,1)S(1)} %get-tuple-element.73), channel_id=1, source_target_pairs={{0,16},{4,20},{16,0},{20,4},{1,17},{5,21},{17,1},{21,5},{2,18},{6,... | collective-permute-start | bytes 1572872 | tf_op jit(solution)/shard_map/ppermute | solution.py:43
  119.3 3.1 %collective-permute-start.36 = (f32[48,128]{1,0:T(8,128)S(1)}, f32[48,128]{1,0:T(8,128)S(1)}, u32[]{:S(2)}, u32[]{:S(2)}) collective-permute-start(f32[48,128]{1,0:T(8,128)S(1)} %pad_maximum_fusion), channel_id=1, source_target_pairs={{0,32},{32,0},{64,96},{96,64},{128,160},{160,128},{192,224},{224,1... | collective-permute-start | bytes 73736 | tf_op jit(solution)/shard_map/ppermute | solution.py:43
  122.3 3.9 %collective-permute-start.37 = (f32[48,128]{1,0:T(8,128)S(1)}, f32[48,128]{1,0:T(8,128)S(1)}, u32[]{:S(2)}, u32[]{:S(2)}) collective-permute-start(f32[48,128]{1,0:T(8,128)S(1)} %fusion), channel_id=1, source_target_pairs={{0,64},{32,96},{64,0},{96,32},{128,192},{160,224},{192,128},{224,1... | collective-permute-start | bytes 73736 | tf_op jit(solution)/shard_map/ppermute | solution.py:43
  126.2 6.6 %collective-permute-start.38 = (f32[48,128]{1,0:T(8,128)S(1)}, f32[48,128]{1,0:T(8,128)S(1)}, u32[]{:S(2)}, u32[]{:S(2)}) collective-permute-start(f32[48,128]{1,0:T(8,128)S(1)} %add.52), channel_id=1, source_target_pairs={{0,128},{32,160},{64,192},{96,224},{128,0},{160,32},{192,64},{224,... | collective-permute-start | bytes 73736 | tf_op jit(solution)/shard_map/ppermute | solution.py:43
  140.1 11.8 %collective-permute-start.46 = (bf16[128,1024]{1,0:T(8,128)(2,1)S(1)}, bf16[128,1024]{1,0:T(8,128)(2,1)S(1)}, u32[]{:S(2)}, u32[]{:S(2)}) collective-permute-start(bf16[128,1024]{1,0:T(8,128)(2,1)S(1)} %get-tuple-element.79), channel_id=1, source_target_pairs={{0,8},{8,0},{1,9},{9,1},{2,10},{10,2},{3,11},{11,3},{4,12},{12,4},... | collective-permute-start | bytes 786440 | tf_op jit(solution)/shard_map/ppermute | solution.py:43
  145.1 4.1 %collective-permute-start.42 = (f32[24,128]{1,0:T(8,128)S(1)}, f32[24,128]{1,0:T(8,128)S(1)}, u32[]{:S(2)}, u32[]{:S(2)}) collective-permute-start(f32[24,128]{1,0:T(8,128)S(1)} %get-tuple-element.85), channel_id=1, source_target_pairs={{0,16},{4,20},{16,0},{20,4},{1,17},{5,21},{17,1},{21,5},{2,18},{6,... | collective-permute-start | bytes 36872 | tf_op jit(solution)/shard_map/ppermute | solution.py:43
  145.7 4.1 %collective-permute-start.44 = (f32[24,128]{1,0:T(8,128)S(1)}, f32[24,128]{1,0:T(8,128)S(1)}, u32[]{:S(2)}, u32[]{:S(2)}) collective-permute-start(f32[24,128]{1,0:T(8,128)S(1)} %get-tuple-element.86), channel_id=1, source_target_pairs={{0,20},{4,16},{16,4},{20,0},{1,21},{5,17},{17,5},{21,1},{2,22},{6,... | collective-permute-start | bytes 36872 | tf_op jit(solution)/shard_map/ppermute | solution.py:43
  146.3 3.4 %collective-permute-start.43 = (f32[24,128]{1,0:T(8,128)S(1)}, f32[24,128]{1,0:T(8,128)S(1)}, u32[]{:S(2)}, u32[]{:S(2)}) collective-permute-start(f32[24,128]{1,0:T(8,128)S(1)} %get-tuple-element.86), channel_id=1, source_target_pairs={{0,4},{4,0},{16,20},{20,16},{1,5},{5,1},{17,21},{21,17},{2,6},{6,2... | collective-permute-start | bytes 36872 | tf_op jit(solution)/shard_map/ppermute | solution.py:43
  149.8 2.1 %collective-permute-start.45 = (f32[24,128]{1,0:T(8,128)S(1)}, f32[24,128]{1,0:T(8,128)S(1)}, u32[]{:S(2)}, u32[]{:S(2)}) collective-permute-start(f32[24,128]{1,0:T(8,128)S(1)} %add_add_fusion.refs_1_), channel_id=1, source_target_pairs={{0,8},{8,0},{1,9},{9,1},{2,10},{10,2},{3,11},{11,3},{4,12},{12,4},... | collective-permute-start | bytes 36872 | tf_op jit(solution)/shard_map/ppermute | solution.py:43

commit v2 on v1

--- a/solution.py
+++ b/solution.py
@@ -230,18 +230,17 @@
     loss[...] = jnp.broadcast_to(share * diag + weight * frob, loss.shape)
 
 
-def product_kernel(coupling, count_full, ids, *refs):
+def product_kernel(coupling, side, count_full, ids, *refs):
     full = refs[:count_full]
     cols, rows = refs[count_full : count_full + 2]
-    targets, sums = refs[count_full + 2 : -2], refs[-2:]
+    targets, sums = refs[count_full + 2 : -1], refs[-1]
     x = ids[2]
     piece = full[0].shape[1]
     count, width = targets[0].shape[0] // 2, targets[0].shape[1]
     chunk = width // 2
     lanes = width // 128
-    for first_lane in range(0, 2 * width, chunk):
-        here = slice(first_lane, first_lane + chunk)
-        side, local = divmod(first_lane, width)
+    for local in range(0, width, chunk):
+        here = slice(side * width + local, side * width + local + chunk)
         product = None
         for step, part in enumerate(full):
             first = pl.multiple_of((x ^ step) * piece, piece)
@@ -252,10 +251,9 @@
         cross = column_sum(product * rows[:, here].astype(f32))
         for k in range(chunk // 128):
             row = local // 128 + k
-            sums[side][row : row + 1] = plain[:, k * 128 : (k + 1) * 128]
-            sums[side][lanes + row : lanes + row + 1] = cross[:, k * 128 : (k + 1) * 128]
-        for k in range(2):
-            target = targets[2 * k + side]
+            sums[row : row + 1] = plain[:, k * 128 : (k + 1) * 128]
+            sums[lanes + row : lanes + row + 1] = cross[:, k * 128 : (k + 1) * 128]
+        for k, target in enumerate(targets):
             target[:, local : local + chunk] = product[2 * count * k : 2 * count * (k + 1)].astype(
                 target.dtype
             )
@@ -390,17 +388,22 @@
     full[1] = tie(full[1], totals, gram_other)
     lanes = width // 128
 
-    leave = shape(2 * count, width, dtype=bf16)
-    mine, leave_far, leave_near, leave_both, near_sums, far_sums = call(
-        lambda *refs: product_kernel(
-            2.0 * redund_weight / (total_rows * total_rows), peers, *refs
-        ),
-        "products",
-        ids,
-        full + [cols, rows],
-        [shape(2 * count, width), leave, leave, leave] + [shape(2 * lanes, 128)] * 2,
-        flops=16 * count * panel * width,
-    )
+
+    def product(side, dtype, flops):
+        return call(
+            lambda *refs: product_kernel(
+                2.0 * redund_weight / (total_rows * total_rows), side, peers, *refs
+            ),
+            "products",
+            ids,
+            full + [cols, rows],
+            [shape(2 * count, width, dtype=dtype), shape(2 * count, width, dtype=bf16)]
+            + [shape(2 * lanes, 128)],
+            flops=flops,
+        )
+
+    leave_far, leave_both, far_sums = product(1, bf16, 8 * count * panel * width)
+    mine, leave_near, near_sums = product(0, f32, 10**11)
     come_far, come_both = swap(leave_far, RING, 1), swap(leave_both, RING, 3)
     come_near = swap(leave_near, RING, 2)
     loss = call(

time: 154 us -> 152 us (0.987)
  waiting for transfers between devices: 70.1 us -> 68.1 us
    ppermute x36, waiting for transfers between devices: 50.4 us -> 48.4 us  [swap(): return lax.ppermute(values, axes, [(k, k ^ step) for k in range(count)])]
    pallas_call x14 -> x15, Pallas kernels: 16.9 us -> 17.6 us  [call(): pl.pallas_call(kernel, in_specs=[SMEM] + [VMEM] * len(args), out_specs=[V...]
  transfers between devices with their start and end apart: 47 -> 47, of which waited for: 29 -> 29; matrix products, arithmetic and copies ran while one was open for 0% -> 0% of each run, Pallas kernels for 5% -> 6%
where the time goes in v2:
time: 152 us
  waiting for transfers between devices  68.1 us (45%)
  starting transfers between devices  64.5 us (42%)
  Pallas kernels  17.6 us (12%)
    ppermute x36, waiting for transfers between devices, swap(): return lax.ppermute(values, axes, [(k, k ^ step) for k in range(count)])  48.4 us
    ppermute x36, starting transfers between devices, swap(): return lax.ppermute(values, axes, [(k, k ^ step) for k in range(count)])  45.6 us
    ppermute x11, waiting for transfers between devices, shift(): lax.ppermute(values, 'z', [(k, (k + steps) % count) for k in range(count)])  19.7 us
    ppermute x11, starting transfers between devices, shift(): lax.ppermute(values, 'z', [(k, (k + steps) % count) for k in range(count)])  18.9 us
    pallas_call x15, Pallas kernels, call(): pl.pallas_call(kernel, in_specs=[SMEM] + [VMEM] * len(args), out_specs=[V...  17.6 us
  transfers between devices with their start and end apart: 47, of which 29 were waited for; matrix products, arithmetic and copies ran while one was open for 0% of the time, Pallas kernels for 6%

profile of v2, /device:TPU:1, one launch (start us, length us, event | category | flops | bytes accessed | tf_op | source)
XLA Modules:
  0.0 152.4 jit_solution(1660155377332378696)
XLA Ops:
  0.6 1.1 broadcast_select_fusion
  1.7 3.3 %collective-permute-start = (bf16[128,1024]{1,0:T(8,128)(2,1)S(1)}, bf16[128,1024]{1,0:T(8,128)(2,1)S(1)}, u32[]{:S(2)}, u32[]{:S(2)}) collective-permute-start(bf16[128,1024]{1,0:T(8,128)(2,1)S(1)} %get-tuple-element.83), channel_id=1, source_target_pairs={{0,8},{8,0},{1,9},{9,1},{2,10},{10,2},{3,11},{11,3},{4,12},{12,4},... | collective-permute-start | bytes 786440 | tf_op jit(solution)/shard_map/ppermute | solution.py:43
  5.1 1.1 collective-permute-done.got
  6.9 1.4 collective-permute-start.6
  8.4 5.6 %collective-permute-start.3 = (bf16[2,64,1024]{2,1,0:T(8,128)(2,1)S(1)}, bf16[2,64,1024]{2,1,0:T(8,128)(2,1)S(1)}, u32[]{:S(2)}, u32[]{:S(2)}) collective-permute-start(bf16[2,64,1024]{2,1,0:T(8,128)(2,1)S(1)} %get-tuple-element.43.refs_1_.refs_5_), channel_id=1, source_target_pairs={{0,224},{32,0},{64,32},{96,64},{128,96},{160,128},{192,160},{224,1... | collective-permute-start | bytes 786440 | tf_op jit(solution)/shard_map/ppermute | solution.py:48
  14.4 3.8 %collective-permute-start.5 = (bf16[2,64,1024]{2,1,0:T(8,128)(2,1)S(1)}, bf16[2,64,1024]{2,1,0:T(8,128)(2,1)S(1)}, u32[]{:S(2)}, u32[]{:S(2)}) collective-permute-start(bf16[2,64,1024]{2,1,0:T(8,128)(2,1)S(1)} %collective-permute-done.1.refs_2_.refs_8_), channel_id=1, source_target_pairs={{0,224},{32,0},{64,32},{96,64},{128,96},{160,128},{192,160},{224,1... | collective-permute-start | bytes 786440 | tf_op jit(solution)/shard_map/ppermute | solution.py:48
  18.6 3.1 %collective-permute-done.2.refs_2_.right_near = bf16[2,64,1024]{2,1,0:T(8,128)(2,1)S(1)} collective-permute-done((bf16[2,64,1024]{2,1,0:T(8,128)(2,1)S(1)}, bf16[2,64,1024]{2,1,0:T(8,128)(2,1)S(1)}, u32[]{:S(2)}, u32[]{:S(2)}) %collective-permute-start.2) | collective-permute-done | bytes 262176 | tf_op jit(solution)/shard_map/ppermute | solution.py:48
  21.7 2.7 %collective-permute-done.5.refs_5_.left_far = bf16[2,64,1024]{2,1,0:T(8,128)(2,1)S(1)} collective-permute-done((bf16[2,64,1024]{2,1,0:T(8,128)(2,1)S(1)}, bf16[2,64,1024]{2,1,0:T(8,128)(2,1)S(1)}, u32[]{:S(2)}, u32[]{:S(2)}) %collective-permute-start.5) | collective-permute-done | bytes 262176 | tf_op jit(solution)/shard_map/ppermute | solution.py:48
  24.5 3.4 %collective-permute-done.4.refs_4_.right_far = bf16[2,64,1024]{2,1,0:T(8,128)(2,1)S(1)} collective-permute-done((bf16[2,64,1024]{2,1,0:T(8,128)(2,1)S(1)}, bf16[2,64,1024]{2,1,0:T(8,128)(2,1)S(1)}, u32[]{:S(2)}, u32[]{:S(2)}) %collective-permute-start.4) | collective-permute-done | bytes 262176 | tf_op jit(solution)/shard_map/ppermute | solution.py:48
  28.6 2.7 %collective-permute-start.8 = (bf16[4,64,1024]{2,1,0:T(8,128)(2,1)S(1)}, bf16[4,64,1024]{2,1,0:T(8,128)(2,1)S(1)}, u32[]{:S(2)}, u32[]{:S(2)}) collective-permute-start(bf16[4,64,1024]{2,1,0:T(8,128)(2,1)S(1)} %get-tuple-element.49.refs_12_), channel_id=1, source_target_pairs={{0,224},{32,0},{64,32},{96,64},{128,96},{160,128},{192,160},{224,1... | collective-permute-start | bytes 1572872 | tf_op jit(solution)/shard_map/ppermute | solution.py:48
  31.2 0.8 collective-permute-start.10
  32.1 0.7 moments.4.refs_1_
  32.8 1.6 %collective-permute-start.9 = (f32[4,1024]{1,0:T(4,128)S(1)}, f32[4,1024]{1,0:T(4,128)S(1)}, u32[]{:S(2)}, u32[]{:S(2)}) collective-permute-start(f32[4,1024]{1,0:T(4,128)S(1)} %moments.4.refs_1_), channel_id=1, source_target_pairs={{0,128},{32,160},{64,192},{96,224},{128,0},{160,32},{192,64},{224,... | collective-permute-start | bytes 49160 | tf_op jit(solution)/shard_map/ppermute | solution.py:48
  34.4 0.8 moments.5.refs_1_
  35.2 6.7 %collective-permute-done.7.refs_2_.refs_13_ = bf16[4,64,1024]{2,1,0:T(8,128)(2,1)S(1)} collective-permute-done((bf16[4,64,1024]{2,1,0:T(8,128)(2,1)S(1)}, bf16[4,64,1024]{2,1,0:T(8,128)(2,1)S(1)}, u32[]{:S(2)}, u32[]{:S(2)}) %collective-permute-start.7) | collective-permute-done | bytes 524320 | tf_op jit(solution)/shard_map/ppermute | solution.py:48
  41.9 0.8 moments.6.refs_1_
  42.7 1.2 collective-permute-done.10.refs_7_
  44.0 2.7 %collective-permute-start.12 = (bf16[4,64,1024]{2,1,0:T(8,128)(2,1)S(1)}, bf16[4,64,1024]{2,1,0:T(8,128)(2,1)S(1)}, u32[]{:S(2)}, u32[]{:S(2)}) collective-permute-start(bf16[4,64,1024]{2,1,0:T(8,128)(2,1)S(1)} %collective-permute-done.8.refs_3_.refs_14_), channel_id=1, source_target_pairs={{0,224},{32,0},{64,32},{96,64},{128,96},{160,128},{192,160},{224,1... | collective-permute-start | bytes 1572872 | tf_op jit(solution)/shard_map/ppermute | solution.py:48
  46.7 5.5 %collective-permute-done.16.refs_9_ = bf16[2,64,1024]{2,1,0:T(8,128)(2,1)S(1)} collective-permute-done((bf16[2,64,1024]{2,1,0:T(8,128)(2,1)S(1)}, bf16[2,64,1024]{2,1,0:T(8,128)(2,1)S(1)}, u32[]{:S(2)}, u32[]{:S(2)}) %collective-permute-start.16) | collective-permute-done | bytes 262176 | tf_op jit(solution)/shard_map/ppermute | solution.py:43
  52.2 3.3 %collective-permute-done.11.refs_3_.refs_15_ = bf16[4,64,1024]{2,1,0:T(8,128)(2,1)S(1)} collective-permute-done((bf16[4,64,1024]{2,1,0:T(8,128)(2,1)S(1)}, bf16[4,64,1024]{2,1,0:T(8,128)(2,1)S(1)}, u32[]{:S(2)}, u32[]{:S(2)}) %collective-permute-start.11) | collective-permute-done | bytes 524320 | tf_op jit(solution)/shard_map/ppermute | solution.py:48
  55.6 2.5 %collective-permute-start.18 = (bf16[2,64,1024]{2,1,0:T(8,128)(2,1)S(1)}, bf16[2,64,1024]{2,1,0:T(8,128)(2,1)S(1)}, u32[]{:S(2)}, u32[]{:S(2)}) collective-permute-start(bf16[2,64,1024]{2,1,0:T(8,128)(2,1)S(1)} %slice.14), channel_id=1, source_target_pairs={{0,224},{32,0},{64,32},{96,64},{128,96},{160,128},{192,160},{224,1... | collective-permute-start | bytes 786440 | tf_op jit(solution)/shard_map/ppermute | solution.py:48
  58.0 0.8 moments.7.refs_1_
  58.9 1.0 collective-permute-start.14
  60.0 2.2 %collective-permute-start.13 = (f32[4,1024]{1,0:T(4,128)S(1)}, f32[4,1024]{1,0:T(4,128)S(1)}, u32[]{:S(2)}, u32[]{:S(2)}) collective-permute-start(f32[4,1024]{1,0:T(4,128)S(1)} %moments.7.refs_1_), channel_id=1, source_target_pairs={{0,4},{4,0},{16,20},{20,16},{1,5},{5,1},{17,21},{21,17},{2,6},{6,2... | collective-permute-start | bytes 49160 | tf_op jit(solution)/shard_map/ppermute | solution.py:43
  63.8 3.2 %gram.1 = (bf16[3,256,512]{2,1,0:T(8,128)(2,1)S(1)}, bf16[1024,2048]{1,0:T(8,128)(2,1)S(1)}, bf16[512,2048]{1,0:T(8,128)(2,1)S(1)}, f32[4,1024]{1,0:T(4,128)S(1)}) custom-call(s32[3]{0:T(128)S(1)} %pad_add_fusion.ids.refs_0_, f32[4,1024]{1,0:T(4,128)S(1)} %moments.7.refs_1_, f32[4,1024]{1,0:T(4,128)S(1)} %collective-permute-done.13.refs_2_, ...), custom_call_target="tpu_custom_call" | custom-call | flops 1610612736 | tf_op jit(solution)/shard_map/gram/pallas_call | solution.py:28
  67.0 1.4 last_gram.1
  68.5 5.8 %collective-permute-start.19 = (bf16[256,512]{1,0:T(8,128)(2,1)S(1)}, bf16[256,512]{1,0:T(8,128)(2,1)S(1)}, u32[]{:S(2)}, u32[]{:S(2)}) collective-permute-start(bf16[256,512]{1,0:T(8,128)(2,1)S(1)} %get-tuple-element.58), channel_id=1, source_target_pairs={{0,8},{1,9},{2,10},{3,11},{8,0},{9,1},{10,2},{11,3},{4,12},{5,13},... | collective-permute-start | bytes 786440 | tf_op jit(solution)/shard_map/ppermute | solution.py:43
  74.3 1.2 collective-permute-start.24
  75.5 2.8 %collective-permute-start.25 = (bf16[256,512]{1,0:T(8,128)(2,1)S(1)}, bf16[256,512]{1,0:T(8,128)(2,1)S(1)}, u32[]{:S(2)}, u32[]{:S(2)}) collective-permute-start(bf16[256,512]{1,0:T(8,128)(2,1)S(1)} %get-tuple-element.62), channel_id=1, source_target_pairs={{0,10},{1,11},{2,8},{3,9},{8,2},{9,3},{10,0},{11,1},{4,14},{5,15},... | collective-permute-start | bytes 786440 | tf_op jit(solution)/shard_map/ppermute | solution.py:43
  78.9 0.8 collective-permute-done.20.theirs
  79.7 0.8 native.1
  81.0 0.8 collective-permute-done.21
  81.8 1.7 %collective-permute-start.22 = (f32[4,1024]{1,0:T(4,128)S(1)}, f32[4,1024]{1,0:T(4,128)S(1)}, u32[]{:S(2)}, u32[]{:S(2)}) collective-permute-start(f32[4,1024]{1,0:T(4,128)S(1)} %add.43), channel_id=1, source_target_pairs={{0,16},{16,0},{1,17},{17,1},{2,18},{18,2},{3,19},{19,3},{4,20},{20... | collective-permute-start | bytes 49160 | tf_op jit(solution)/shard_map/ppermute | solution.py:43
  83.6 2.6 %collective-permute-done.22 = f32[4,1024]{1,0:T(4,128)S(1)} collective-permute-done((f32[4,1024]{1,0:T(4,128)S(1)}, f32[4,1024]{1,0:T(4,128)S(1)}, u32[]{:S(2)}, u32[]{:S(2)}) %collective-permute-start.22) | collective-permute-done | bytes 16416 | tf_op jit(solution)/shard_map/ppermute | solution.py:43
  86.2 2.9 %collective-permute-done.23 = f32[4,1024]{1,0:T(4,128)S(1)} collective-permute-done((f32[4,1024]{1,0:T(4,128)S(1)}, f32[4,1024]{1,0:T(4,128)S(1)}, u32[]{:S(2)}, u32[]{:S(2)}) %collective-permute-start.23) | collective-permute-done | bytes 16416 | tf_op jit(solution)/shard_map/ppermute | solution.py:43
  89.1 1.1 collective-permute-done.25.refs_2_
  90.2 2.9 %collective-permute-done.26.refs_3_ = bf16[256,512]{1,0:T(8,128)(2,1)S(1)} collective-permute-done((bf16[256,512]{1,0:T(8,128)(2,1)S(1)}, bf16[256,512]{1,0:T(8,128)(2,1)S(1)}, u32[]{:S(2)}, u32[]{:S(2)}) %collective-permute-start.26) | collective-permute-done | bytes 262176 | tf_op jit(solution)/shard_map/ppermute | solution.py:43
  93.1 0.7 reduce.1
  94.5 2.8 %collective-permute-start.31 = (bf16[512,256]{1,0:T(8,128)(2,1)S(1)}, bf16[512,256]{1,0:T(8,128)(2,1)S(1)}, u32[]{:S(2)}, u32[]{:S(2)}) collective-permute-start(bf16[512,256]{1,0:T(8,128)(2,1)S(1)} %get-tuple-element.64.refs_1_), channel_id=1, source_target_pairs={{0,2},{1,3},{2,0},{3,1},{4,6},{5,7},{6,4},{7,5},{8,10},{9,11},{10,... | collective-permute-start | bytes 786440 | tf_op jit(solution)/shard_map/ppermute | solution.py:43
  97.3 3.8 %collective-permute-done.28 = f32[4,1024]{1,0:T(4,128)S(1)} collective-permute-done((f32[4,1024]{1,0:T(4,128)S(1)}, f32[4,1024]{1,0:T(4,128)S(1)}, u32[]{:S(2)}, u32[]{:S(2)}) %collective-permute-start.28) | collective-permute-done | bytes 16416 | tf_op jit(solution)/shard_map/ppermute | solution.py:43
  101.1 1.5 collective-permute-start.29
  102.6 5.0 %collective-permute-done.29 = f32[4,1024]{1,0:T(4,128)S(1)} collective-permute-done((f32[4,1024]{1,0:T(4,128)S(1)}, f32[4,1024]{1,0:T(4,128)S(1)}, u32[]{:S(2)}, u32[]{:S(2)}) %collective-permute-start.29) | collective-permute-done | bytes 16416 | tf_op jit(solution)/shard_map/ppermute | solution.py:43
  107.6 0.9 collective-permute-done.32.refs_4_
  108.6 1.9 %products.3 = (bf16[256,1024]{1,0:T(8,128)(2,1)S(1)}, bf16[256,1024]{1,0:T(8,128)(2,1)S(1)}, f32[16,128]{1,0:T(8,128)S(1)}) custom-call(s32[3]{0:T(128)S(1)} %pad_add_fusion.ids.refs_0_, bf16[512,256]{1,0:T(8,128)(2,1)S(1)} %get-tuple-element.64.refs_1_, bf16[512,256]{1,0:T(8,128)(2,1)S(1)} %collective-permute-done.27.refs_2_, ...), custom_call_target="tpu_custom_call" | custom-call | flops 1073741824 | tf_op jit(solution)/shard_map/products/pallas_call | solution.py:28
  110.5 0.8 loss.1
  111.3 1.1 collective-permute-start.35
  112.9 1.7 %collective-permute-start.33 = (f32[8,128]{1,0:T(8,128)S(1)}, f32[8,128]{1,0:T(8,128)S(1)}, u32[]{:S(2)}, u32[]{:S(2)}) collective-permute-start(f32[8,128]{1,0:T(8,128)S(1)} %loss.1), channel_id=1, source_target_pairs={{0,1},{1,0},{2,3},{3,2},{4,5},{5,4},{6,7},{7,6},{8,9},{9,8},{10,11... | collective-permute-start | bytes 12296 | tf_op jit(solution)/shard_map/ppermute | solution.py:43
  114.6 1.6 %collective-permute-start.39 = (bf16[256,1024]{1,0:T(8,128)(2,1)S(1)}, bf16[256,1024]{1,0:T(8,128)(2,1)S(1)}, u32[]{:S(2)}, u32[]{:S(2)}) collective-permute-start(bf16[256,1024]{1,0:T(8,128)(2,1)S(1)} %get-tuple-element.71), channel_id=1, source_target_pairs={{0,4},{4,0},{16,20},{20,16},{1,5},{5,1},{17,21},{21,17},{2,6},{6,2... | collective-permute-start | bytes 1572872 | tf_op jit(solution)/shard_map/ppermute | solution.py:43
  116.9 1.9 %products.2 = (f32[256,1024]{1,0:T(8,128)S(1)}, bf16[256,1024]{1,0:T(8,128)(2,1)S(1)}, f32[16,128]{1,0:T(8,128)S(1)}) custom-call(s32[3]{0:T(128)S(1)} %pad_add_fusion.ids.refs_0_, bf16[512,256]{1,0:T(8,128)(2,1)S(1)} %get-tuple-element.64.refs_1_, bf16[512,256]{1,0:T(8,128)(2,1)S(1)} %collective-permute-done.27.refs_2_, ...), custom_call_target="tpu_custom_call" | custom-call | flops 99999997952 | tf_op jit(solution)/shard_map/products/pallas_call | solution.py:28
  118.8 1.3 collective-permute-start.41
  120.2 3.0 %collective-permute-done.36 = f32[48,128]{1,0:T(8,128)S(1)} collective-permute-done((f32[48,128]{1,0:T(8,128)S(1)}, f32[48,128]{1,0:T(8,128)S(1)}, u32[]{:S(2)}, u32[]{:S(2)}) %collective-permute-start.36) | collective-permute-done | bytes 24608 | tf_op jit(solution)/shard_map/ppermute | solution.py:43
  123.1 0.7 collective-permute-start.37
  123.9 3.1 %collective-permute-done.37 = f32[48,128]{1,0:T(8,128)S(1)} collective-permute-done((f32[48,128]{1,0:T(8,128)S(1)}, f32[48,128]{1,0:T(8,128)S(1)}, u32[]{:S(2)}, u32[]{:S(2)}) %collective-permute-start.37) | collective-permute-done | bytes 24608 | tf_op jit(solution)/shard_map/ppermute | solution.py:43
  127.0 2.4 %collective-permute-start.38 = (f32[48,128]{1,0:T(8,128)S(1)}, f32[48,128]{1,0:T(8,128)S(1)}, u32[]{:S(2)}, u32[]{:S(2)}) collective-permute-start(f32[48,128]{1,0:T(8,128)S(1)} %add.52), channel_id=1, source_target_pairs={{0,128},{32,160},{64,192},{96,224},{128,0},{160,32},{192,64},{224,... | collective-permute-start | bytes 73736 | tf_op jit(solution)/shard_map/ppermute | solution.py:43
  129.4 4.2 %collective-permute-done.38 = f32[48,128]{1,0:T(8,128)S(1)} collective-permute-done((f32[48,128]{1,0:T(8,128)S(1)}, f32[48,128]{1,0:T(8,128)S(1)}, u32[]{:S(2)}, u32[]{:S(2)}) %collective-permute-start.38) | collective-permute-done | bytes 24608 | tf_op jit(solution)/shard_map/ppermute | solution.py:43
  133.6 4.5 %collective-permute-done.41.refs_2_ = bf16[256,1024]{1,0:T(8,128)(2,1)S(1)} collective-permute-done((bf16[256,1024]{1,0:T(8,128)(2,1)S(1)}, bf16[256,1024]{1,0:T(8,128)(2,1)S(1)}, u32[]{:S(2)}, u32[]{:S(2)}) %collective-permute-start.41) | collective-permute-done | bytes 524320 | tf_op jit(solution)/shard_map/ppermute | solution.py:43
  138.1 0.8 add.68
  138.9 5.0 %collective-permute-start.46 = (bf16[128,1024]{1,0:T(8,128)(2,1)S(1)}, bf16[128,1024]{1,0:T(8,128)(2,1)S(1)}, u32[]{:S(2)}, u32[]{:S(2)}) collective-permute-start(bf16[128,1024]{1,0:T(8,128)(2,1)S(1)} %get-tuple-element.79), channel_id=1, source_target_pairs={{0,8},{8,0},{1,9},{9,1},{2,10},{10,2},{3,11},{11,3},{4,12},{12,4},... | collective-permute-start | bytes 786440 | tf_op jit(solution)/shard_map/ppermute | solution.py:43
  144.5 0.7 collective-permute-start.44
  145.2 1.3 collective-permute-start.43
  146.5 1.4 collective-permute-done.42
  148.6 1.3 collective-permute-start.45
  149.9 0.8 collective-permute-done.45.refs_2_
  150.7 1.7 %finish.1 = (bf16[128,1024]{1,0:T(8,128)(2,1)}, bf16[128,1024]{1,0:T(8,128)(2,1)}, f32[1,128]{1,0:T(1,128)}) custom-call(s32[3]{0:T(128)S(1)} %pad_add_fusion.ids.refs_0_, f32[24,128]{1,0:T(8,128)S(1)} %add_add_fusion.refs_1_, f32[24,128]{1,0:T(8,128)S(1)} %collective-permute-done.45.refs_2_, f32[4,1024]{1,0:T(4,128)S(1)} %add.47.refs_3_, ...), custom_call_target="tpu_custom_call" | custom-call | tf_op jit(solution)/shard_map/finish/pallas_call | solution.py:28
  (66 shorter events, 8.4 us)
Async XLA Ops:
  1.7 4.5 %collective-permute-start = (bf16[128,1024]{1,0:T(8,128)(2,1)S(1)}, bf16[128,1024]{1,0:T(8,128)(2,1)S(1)}, u32[]{:S(2)}, u32[]{:S(2)}) collective-permute-start(bf16[128,1024]{1,0:T(8,128)(2,1)S(1)} %get-tuple-element.83), channel_id=1, source_target_pairs={{0,8},{8,0},{1,9},{9,1},{2,10},{10,2},{3,11},{11,3},{4,12},{12,4},... | collective-permute-start | bytes 786440 | tf_op jit(solution)/shard_map/ppermute | solution.py:43
  6.8 7.6 %collective-permute-start.1 = (bf16[2,64,1024]{2,1,0:T(8,128)(2,1)S(1)}, bf16[2,64,1024]{2,1,0:T(8,128)(2,1)S(1)}, u32[]{:S(2)}, u32[]{:S(2)}) collective-permute-start(bf16[2,64,1024]{2,1,0:T(8,128)(2,1)S(1)} %get-tuple-element.44.refs_6_), channel_id=1, source_target_pairs={{0,4},{4,0},{16,20},{20,16},{1,5},{5,1},{17,21},{21,17},{2,6},{6,2... | collective-permute-start | bytes 786440 | tf_op jit(solution)/shard_map/ppermute | solution.py:43
  6.9 21.6 %collective-permute-start.6 = (bf16[4,64,1024]{2,1,0:T(8,128)(2,1)S(1)}, bf16[4,64,1024]{2,1,0:T(8,128)(2,1)S(1)}, u32[]{:S(2)}, u32[]{:S(2)}) collective-permute-start(bf16[4,64,1024]{2,1,0:T(8,128)(2,1)S(1)} %get-tuple-element.47), channel_id=1, source_target_pairs={{0,20},{4,16},{16,4},{20,0},{1,21},{5,17},{17,5},{21,1},{2,22},{6,... | collective-permute-start | bytes 1572872 | tf_op jit(solution)/shard_map/ppermute | solution.py:43
  8.4 10.2 %collective-permute-start.3 = (bf16[2,64,1024]{2,1,0:T(8,128)(2,1)S(1)}, bf16[2,64,1024]{2,1,0:T(8,128)(2,1)S(1)}, u32[]{:S(2)}, u32[]{:S(2)}) collective-permute-start(bf16[2,64,1024]{2,1,0:T(8,128)(2,1)S(1)} %get-tuple-element.43.refs_1_.refs_5_), channel_id=1, source_target_pairs={{0,224},{32,0},{64,32},{96,64},{128,96},{160,128},{192,160},{224,1... | collective-permute-start | bytes 786440 | tf_op jit(solution)/shard_map/ppermute | solution.py:48
  13.9 7.8 %collective-permute-start.2 = (bf16[2,64,1024]{2,1,0:T(8,128)(2,1)S(1)}, bf16[2,64,1024]{2,1,0:T(8,128)(2,1)S(1)}, u32[]{:S(2)}, u32[]{:S(2)}) collective-permute-start(bf16[2,64,1024]{2,1,0:T(8,128)(2,1)S(1)} %get-tuple-element.43.refs_1_.refs_5_), channel_id=1, source_target_pairs={{0,32},{32,64},{64,96},{96,128},{128,160},{160,192},{192,224},{224... | collective-permute-start | bytes 786440 | tf_op jit(solution)/shard_map/ppermute | solution.py:48
  14.4 10.0 %collective-permute-start.5 = (bf16[2,64,1024]{2,1,0:T(8,128)(2,1)S(1)}, bf16[2,64,1024]{2,1,0:T(8,128)(2,1)S(1)}, u32[]{:S(2)}, u32[]{:S(2)}) collective-permute-start(bf16[2,64,1024]{2,1,0:T(8,128)(2,1)S(1)} %collective-permute-done.1.refs_2_.refs_8_), channel_id=1, source_target_pairs={{0,224},{32,0},{64,32},{96,64},{128,96},{160,128},{192,160},{224,1... | collective-permute-start | bytes 786440 | tf_op jit(solution)/shard_map/ppermute | solution.py:48
  18.3 9.6 %collective-permute-start.4 = (bf16[2,64,1024]{2,1,0:T(8,128)(2,1)S(1)}, bf16[2,64,1024]{2,1,0:T(8,128)(2,1)S(1)}, u32[]{:S(2)}, u32[]{:S(2)}) collective-permute-start(bf16[2,64,1024]{2,1,0:T(8,128)(2,1)S(1)} %collective-permute-done.1.refs_2_.refs_8_), channel_id=1, source_target_pairs={{0,32},{32,64},{64,96},{96,128},{128,160},{160,192},{192,224},{224... | collective-permute-start | bytes 786440 | tf_op jit(solution)/shard_map/ppermute | solution.py:48
  28.5 13.4 %collective-permute-start.7 = (bf16[4,64,1024]{2,1,0:T(8,128)(2,1)S(1)}, bf16[4,64,1024]{2,1,0:T(8,128)(2,1)S(1)}, u32[]{:S(2)}, u32[]{:S(2)}) collective-permute-start(bf16[4,64,1024]{2,1,0:T(8,128)(2,1)S(1)} %get-tuple-element.48.refs_11_), channel_id=1, source_target_pairs={{0,32},{32,64},{64,96},{96,128},{128,160},{160,192},{192,224},{224... | collective-permute-start | bytes 1572872 | tf_op jit(solution)/shard_map/ppermute | solution.py:48
  28.6 13.3 %collective-permute-start.8 = (bf16[4,64,1024]{2,1,0:T(8,128)(2,1)S(1)}, bf16[4,64,1024]{2,1,0:T(8,128)(2,1)S(1)}, u32[]{:S(2)}, u32[]{:S(2)}) collective-permute-start(bf16[4,64,1024]{2,1,0:T(8,128)(2,1)S(1)} %get-tuple-element.49.refs_12_), channel_id=1, source_target_pairs={{0,224},{32,0},{64,32},{96,64},{128,96},{160,128},{192,160},{224,1... | collective-permute-start | bytes 1572872 | tf_op jit(solution)/shard_map/ppermute | solution.py:48
  31.2 12.7 %collective-permute-start.10 = (bf16[4,64,1024]{2,1,0:T(8,128)(2,1)S(1)}, bf16[4,64,1024]{2,1,0:T(8,128)(2,1)S(1)}, u32[]{:S(2)}, u32[]{:S(2)}) collective-permute-start(bf16[4,64,1024]{2,1,0:T(8,128)(2,1)S(1)} %get-tuple-element.47), channel_id=1, source_target_pairs={{0,16},{4,20},{16,0},{20,4},{1,17},{5,21},{17,1},{21,5},{2,18},{6,... | collective-permute-start | bytes 1572872 | tf_op jit(solution)/shard_map/ppermute | solution.py:43
  32.8 10.0 %collective-permute-start.9 = (f32[4,1024]{1,0:T(4,128)S(1)}, f32[4,1024]{1,0:T(4,128)S(1)}, u32[]{:S(2)}, u32[]{:S(2)}) collective-permute-start(f32[4,1024]{1,0:T(4,128)S(1)} %moments.4.refs_1_), channel_id=1, source_target_pairs={{0,128},{32,160},{64,192},{96,224},{128,0},{160,32},{192,64},{224,... | collective-permute-start | bytes 49160 | tf_op jit(solution)/shard_map/ppermute | solution.py:48
  44.0 11.5 %collective-permute-start.11 = (bf16[4,64,1024]{2,1,0:T(8,128)(2,1)S(1)}, bf16[4,64,1024]{2,1,0:T(8,128)(2,1)S(1)}, u32[]{:S(2)}, u32[]{:S(2)}) collective-permute-start(bf16[4,64,1024]{2,1,0:T(8,128)(2,1)S(1)} %collective-permute-done.7.refs_2_.refs_13_), channel_id=1, source_target_pairs={{0,32},{32,64},{64,96},{96,128},{128,160},{160,192},{192,224},{224... | collective-permute-start | bytes 1572872 | tf_op jit(solution)/shard_map/ppermute | solution.py:48
  44.0 11.5 %collective-permute-start.12 = (bf16[4,64,1024]{2,1,0:T(8,128)(2,1)S(1)}, bf16[4,64,1024]{2,1,0:T(8,128)(2,1)S(1)}, u32[]{:S(2)}, u32[]{:S(2)}) collective-permute-start(bf16[4,64,1024]{2,1,0:T(8,128)(2,1)S(1)} %collective-permute-done.8.refs_3_.refs_14_), channel_id=1, source_target_pairs={{0,224},{32,0},{64,32},{96,64},{128,96},{160,128},{192,160},{224,1... | collective-permute-start | bytes 1572872 | tf_op jit(solution)/shard_map/ppermute | solution.py:48
  46.7 5.5 %collective-permute-start.16 = (bf16[2,64,1024]{2,1,0:T(8,128)(2,1)S(1)}, bf16[2,64,1024]{2,1,0:T(8,128)(2,1)S(1)}, u32[]{:S(2)}, u32[]{:S(2)}) collective-permute-start(bf16[2,64,1024]{2,1,0:T(8,128)(2,1)S(1)} %get-tuple-element.43.refs_1_.refs_5_), channel_id=1, source_target_pairs={{0,4},{4,0},{16,20},{20,16},{1,5},{5,1},{17,21},{21,17},{2,6},{6,2... | collective-permute-start | bytes 786440 | tf_op jit(solution)/shard_map/ppermute | solution.py:43
  55.6 11.5 %collective-permute-start.18 = (bf16[2,64,1024]{2,1,0:T(8,128)(2,1)S(1)}, bf16[2,64,1024]{2,1,0:T(8,128)(2,1)S(1)}, u32[]{:S(2)}, u32[]{:S(2)}) collective-permute-start(bf16[2,64,1024]{2,1,0:T(8,128)(2,1)S(1)} %slice.14), channel_id=1, source_target_pairs={{0,224},{32,0},{64,32},{96,64},{128,96},{160,128},{192,160},{224,1... | collective-permute-start | bytes 786440 | tf_op jit(solution)/shard_map/ppermute | solution.py:48
  58.0 9.0 %collective-permute-start.17 = (bf16[2,64,1024]{2,1,0:T(8,128)(2,1)S(1)}, bf16[2,64,1024]{2,1,0:T(8,128)(2,1)S(1)}, u32[]{:S(2)}, u32[]{:S(2)}) collective-permute-start(bf16[2,64,1024]{2,1,0:T(8,128)(2,1)S(1)} %slice.13), channel_id=1, source_target_pairs={{0,32},{32,64},{64,96},{96,128},{128,160},{160,192},{192,224},{224... | collective-permute-start | bytes 786440 | tf_op jit(solution)/shard_map/ppermute | solution.py:48
  58.8 3.9 %collective-permute-start.15 = (f32[4,1024]{1,0:T(4,128)S(1)}, f32[4,1024]{1,0:T(4,128)S(1)}, u32[]{:S(2)}, u32[]{:S(2)}) collective-permute-start(f32[4,1024]{1,0:T(4,128)S(1)} %moments.7.refs_1_), channel_id=1, source_target_pairs={{0,20},{4,16},{16,4},{20,0},{1,21},{5,17},{17,5},{21,1},{2,22},{6,... | collective-permute-start | bytes 49160 | tf_op jit(solution)/shard_map/ppermute | solution.py:43
  58.9 4.2 %collective-permute-start.14 = (f32[4,1024]{1,0:T(4,128)S(1)}, f32[4,1024]{1,0:T(4,128)S(1)}, u32[]{:S(2)}, u32[]{:S(2)}) collective-permute-start(f32[4,1024]{1,0:T(4,128)S(1)} %moments.7.refs_1_), channel_id=1, source_target_pairs={{0,16},{4,20},{16,0},{20,4},{1,17},{5,21},{17,1},{21,5},{2,18},{6,... | collective-permute-start | bytes 49160 | tf_op jit(solution)/shard_map/ppermute | solution.py:43
  60.0 3.8 %collective-permute-start.13 = (f32[4,1024]{1,0:T(4,128)S(1)}, f32[4,1024]{1,0:T(4,128)S(1)}, u32[]{:S(2)}, u32[]{:S(2)}) collective-permute-start(f32[4,1024]{1,0:T(4,128)S(1)} %moments.7.refs_1_), channel_id=1, source_target_pairs={{0,4},{4,0},{16,20},{20,16},{1,5},{5,1},{17,21},{21,17},{2,6},{6,2... | collective-permute-start | bytes 49160 | tf_op jit(solution)/shard_map/ppermute | solution.py:43
  67.0 12.7 %copy-start = (bf16[128,1024]{1,0:T(8,128)(2,1)S(1)}, bf16[128,1024]{1,0:T(8,128)(2,1)}, u32[]{:S(2)}) copy-start(bf16[128,1024]{1,0:T(8,128)(2,1)} %view_b.1) | copy-start | bytes 786436
  67.0 12.7 %copy-start.1 = (bf16[128,1024]{1,0:T(8,128)(2,1)S(1)}, bf16[128,1024]{1,0:T(8,128)(2,1)}, u32[]{:S(2)}) copy-start(bf16[128,1024]{1,0:T(8,128)(2,1)} %view_a.1) | copy-start | bytes 786436
  68.5 20.6 %collective-permute-start.19 = (bf16[256,512]{1,0:T(8,128)(2,1)S(1)}, bf16[256,512]{1,0:T(8,128)(2,1)S(1)}, u32[]{:S(2)}, u32[]{:S(2)}) collective-permute-start(bf16[256,512]{1,0:T(8,128)(2,1)S(1)} %get-tuple-element.58), channel_id=1, source_target_pairs={{0,8},{1,9},{2,10},{3,11},{8,0},{9,1},{10,2},{11,3},{4,12},{5,13},... | collective-permute-start | bytes 786440 | tf_op jit(solution)/shard_map/ppermute | solution.py:43
  74.3 14.8 %collective-permute-start.24 = (bf16[256,512]{1,0:T(8,128)(2,1)S(1)}, bf16[256,512]{1,0:T(8,128)(2,1)S(1)}, u32[]{:S(2)}, u32[]{:S(2)}) collective-permute-start(bf16[256,512]{1,0:T(8,128)(2,1)S(1)} %get-tuple-element.61), channel_id=1, source_target_pairs={{0,9},{1,8},{2,11},{3,10},{8,1},{9,0},{10,3},{11,2},{4,13},{5,12},... | collective-permute-start | bytes 786440 | tf_op jit(solution)/shard_map/ppermute | solution.py:43
  75.5 14.7 %collective-permute-start.25 = (bf16[256,512]{1,0:T(8,128)(2,1)S(1)}, bf16[256,512]{1,0:T(8,128)(2,1)S(1)}, u32[]{:S(2)}, u32[]{:S(2)}) collective-permute-start(bf16[256,512]{1,0:T(8,128)(2,1)S(1)} %get-tuple-element.62), channel_id=1, source_target_pairs={{0,10},{1,11},{2,8},{3,9},{8,2},{9,3},{10,0},{11,1},{4,14},{5,15},... | collective-permute-start | bytes 786440 | tf_op jit(solution)/shard_map/ppermute | solution.py:43
  78.3 14.8 %collective-permute-start.26 = (bf16[256,512]{1,0:T(8,128)(2,1)S(1)}, bf16[256,512]{1,0:T(8,128)(2,1)S(1)}, u32[]{:S(2)}, u32[]{:S(2)}) collective-permute-start(bf16[256,512]{1,0:T(8,128)(2,1)S(1)} %get-tuple-element.63), channel_id=1, source_target_pairs={{0,11},{1,10},{2,9},{3,8},{8,3},{9,2},{10,1},{11,0},{4,15},{5,14},... | collective-permute-start | bytes 786440 | tf_op jit(solution)/shard_map/ppermute | solution.py:43
  78.4 1.3 collective-permute-start.20
  80.6 1.3 collective-permute-start.21
  81.8 4.4 %collective-permute-start.22 = (f32[4,1024]{1,0:T(4,128)S(1)}, f32[4,1024]{1,0:T(4,128)S(1)}, u32[]{:S(2)}, u32[]{:S(2)}) collective-permute-start(f32[4,1024]{1,0:T(4,128)S(1)} %add.43), channel_id=1, source_target_pairs={{0,16},{16,0},{1,17},{17,1},{2,18},{18,2},{3,19},{19,3},{4,20},{20... | collective-permute-start | bytes 49160 | tf_op jit(solution)/shard_map/ppermute | solution.py:43
  86.2 2.9 %collective-permute-start.23 = (f32[4,1024]{1,0:T(4,128)S(1)}, f32[4,1024]{1,0:T(4,128)S(1)}, u32[]{:S(2)}, u32[]{:S(2)}) collective-permute-start(f32[4,1024]{1,0:T(4,128)S(1)} %add.44), channel_id=1, source_target_pairs={{0,32},{32,0},{64,96},{96,64},{128,160},{160,128},{192,224},{224,1... | collective-permute-start | bytes 49160 | tf_op jit(solution)/shard_map/ppermute | solution.py:43
  93.8 13.8 %collective-permute-start.30 = (bf16[512,256]{1,0:T(8,128)(2,1)S(1)}, bf16[512,256]{1,0:T(8,128)(2,1)S(1)}, u32[]{:S(2)}, u32[]{:S(2)}) collective-permute-start(bf16[512,256]{1,0:T(8,128)(2,1)S(1)} %get-tuple-element.64.refs_1_), channel_id=1, source_target_pairs={{0,8},{8,0},{1,9},{9,1},{2,10},{10,2},{3,11},{11,3},{4,12},{12,4},... | collective-permute-start | bytes 786440 | tf_op jit(solution)/shard_map/ppermute | solution.py:43
  94.1 13.6 %collective-permute-start.27 = (bf16[512,256]{1,0:T(8,128)(2,1)S(1)}, bf16[512,256]{1,0:T(8,128)(2,1)S(1)}, u32[]{:S(2)}, u32[]{:S(2)}) collective-permute-start(bf16[512,256]{1,0:T(8,128)(2,1)S(1)} %get-tuple-element.64.refs_1_), channel_id=1, source_target_pairs={{0,1},{1,0},{2,3},{3,2},{4,5},{5,4},{6,7},{7,6},{8,9},{9,8},{10,11... | collective-permute-start | bytes 786440 | tf_op jit(solution)/shard_map/ppermute | solution.py:43
  94.1 14.5 %collective-permute-start.32 = (bf16[512,256]{1,0:T(8,128)(2,1)S(1)}, bf16[512,256]{1,0:T(8,128)(2,1)S(1)}, u32[]{:S(2)}, u32[]{:S(2)}) collective-permute-start(bf16[512,256]{1,0:T(8,128)(2,1)S(1)} %get-tuple-element.64.refs_1_), channel_id=1, source_target_pairs={{0,3},{1,2},{2,1},{3,0},{4,7},{5,6},{6,5},{7,4},{8,11},{9,10},{10,... | collective-permute-start | bytes 786440 | tf_op jit(solution)/shard_map/ppermute | solution.py:43
  94.5 14.0 %collective-permute-start.31 = (bf16[512,256]{1,0:T(8,128)(2,1)S(1)}, bf16[512,256]{1,0:T(8,128)(2,1)S(1)}, u32[]{:S(2)}, u32[]{:S(2)}) collective-permute-start(bf16[512,256]{1,0:T(8,128)(2,1)S(1)} %get-tuple-element.64.refs_1_), channel_id=1, source_target_pairs={{0,2},{1,3},{2,0},{3,1},{4,6},{5,7},{6,4},{7,5},{8,10},{9,11},{10,... | collective-permute-start | bytes 786440 | tf_op jit(solution)/shard_map/ppermute | solution.py:43
  97.3 3.8 %collective-permute-start.28 = (f32[4,1024]{1,0:T(4,128)S(1)}, f32[4,1024]{1,0:T(4,128)S(1)}, u32[]{:S(2)}, u32[]{:S(2)}) collective-permute-start(f32[4,1024]{1,0:T(4,128)S(1)} %add.45), channel_id=1, source_target_pairs={{0,64},{32,96},{64,0},{96,32},{128,192},{160,224},{192,128},{224,1... | collective-permute-start | bytes 49160 | tf_op jit(solution)/shard_map/ppermute | solution.py:43
  101.1 6.5 %collective-permute-start.29 = (f32[4,1024]{1,0:T(4,128)S(1)}, f32[4,1024]{1,0:T(4,128)S(1)}, u32[]{:S(2)}, u32[]{:S(2)}) collective-permute-start(f32[4,1024]{1,0:T(4,128)S(1)} %add.46), channel_id=1, source_target_pairs={{0,128},{32,160},{64,192},{96,224},{128,0},{160,32},{192,64},{224,... | collective-permute-start | bytes 49160 | tf_op jit(solution)/shard_map/ppermute | solution.py:43
  111.3 7.5 %collective-permute-start.35 = (f32[8,128]{1,0:T(8,128)S(1)}, f32[8,128]{1,0:T(8,128)S(1)}, u32[]{:S(2)}, u32[]{:S(2)}) collective-permute-start(f32[8,128]{1,0:T(8,128)S(1)} %loss.1), channel_id=1, source_target_pairs={{0,3},{1,2},{2,1},{3,0},{4,7},{5,6},{6,5},{7,4},{8,11},{9,10},{10,... | collective-permute-start | bytes 12296 | tf_op jit(solution)/shard_map/ppermute | solution.py:43
  112.4 7.7 %collective-permute-start.34 = (f32[8,128]{1,0:T(8,128)S(1)}, f32[8,128]{1,0:T(8,128)S(1)}, u32[]{:S(2)}, u32[]{:S(2)}) collective-permute-start(f32[8,128]{1,0:T(8,128)S(1)} %loss.1), channel_id=1, source_target_pairs={{0,2},{1,3},{2,0},{3,1},{4,6},{5,7},{6,4},{7,5},{8,10},{9,11},{10,... | collective-permute-start | bytes 12296 | tf_op jit(solution)/shard_map/ppermute | solution.py:43
  112.9 7.1 %collective-permute-start.33 = (f32[8,128]{1,0:T(8,128)S(1)}, f32[8,128]{1,0:T(8,128)S(1)}, u32[]{:S(2)}, u32[]{:S(2)}) collective-permute-start(f32[8,128]{1,0:T(8,128)S(1)} %loss.1), channel_id=1, source_target_pairs={{0,1},{1,0},{2,3},{3,2},{4,5},{5,4},{6,7},{7,6},{8,9},{9,8},{10,11... | collective-permute-start | bytes 12296 | tf_op jit(solution)/shard_map/ppermute | solution.py:43
  114.6 19.0 %collective-permute-start.39 = (bf16[256,1024]{1,0:T(8,128)(2,1)S(1)}, bf16[256,1024]{1,0:T(8,128)(2,1)S(1)}, u32[]{:S(2)}, u32[]{:S(2)}) collective-permute-start(bf16[256,1024]{1,0:T(8,128)(2,1)S(1)} %get-tuple-element.71), channel_id=1, source_target_pairs={{0,4},{4,0},{16,20},{20,16},{1,5},{5,1},{17,21},{21,17},{2,6},{6,2... | collective-permute-start | bytes 1572872 | tf_op jit(solution)/shard_map/ppermute | solution.py:43
  116.2 17.4 %collective-permute-start.40 = (bf16[256,1024]{1,0:T(8,128)(2,1)S(1)}, bf16[256,1024]{1,0:T(8,128)(2,1)S(1)}, u32[]{:S(2)}, u32[]{:S(2)}) collective-permute-start(bf16[256,1024]{1,0:T(8,128)(2,1)S(1)} %get-tuple-element.72), channel_id=1, source_target_pairs={{0,20},{4,16},{16,4},{20,0},{1,21},{5,17},{17,5},{21,1},{2,22},{6,... | collective-permute-start | bytes 1572872 | tf_op jit(solution)/shard_map/ppermute | solution.py:43
  118.8 19.3 %collective-permute-start.41 = (bf16[256,1024]{1,0:T(8,128)(2,1)S(1)}, bf16[256,1024]{1,0:T(8,128)(2,1)S(1)}, u32[]{:S(2)}, u32[]{:S(2)}) collective-permute-start(bf16[256,1024]{1,0:T(8,128)(2,1)S(1)} %get-tuple-element.73), channel_id=1, source_target_pairs={{0,16},{4,20},{16,0},{20,4},{1,17},{5,21},{17,1},{21,5},{2,18},{6,... | collective-permute-start | bytes 1572872 | tf_op jit(solution)/shard_map/ppermute | solution.py:43
  120.1 3.1 %collective-permute-start.36 = (f32[48,128]{1,0:T(8,128)S(1)}, f32[48,128]{1,0:T(8,128)S(1)}, u32[]{:S(2)}, u32[]{:S(2)}) collective-permute-start(f32[48,128]{1,0:T(8,128)S(1)} %pad_maximum_fusion), channel_id=1, source_target_pairs={{0,32},{32,0},{64,96},{96,64},{128,160},{160,128},{192,224},{224,1... | collective-permute-start | bytes 73736 | tf_op jit(solution)/shard_map/ppermute | solution.py:43
  123.1 3.9 %collective-permute-start.37 = (f32[48,128]{1,0:T(8,128)S(1)}, f32[48,128]{1,0:T(8,128)S(1)}, u32[]{:S(2)}, u32[]{:S(2)}) collective-permute-start(f32[48,128]{1,0:T(8,128)S(1)} %fusion), channel_id=1, source_target_pairs={{0,64},{32,96},{64,0},{96,32},{128,192},{160,224},{192,128},{224,1... | collective-permute-start | bytes 73736 | tf_op jit(solution)/shard_map/ppermute | solution.py:43
  127.0 6.6 %collective-permute-start.38 = (f32[48,128]{1,0:T(8,128)S(1)}, f32[48,128]{1,0:T(8,128)S(1)}, u32[]{:S(2)}, u32[]{:S(2)}) collective-permute-start(f32[48,128]{1,0:T(8,128)S(1)} %add.52), channel_id=1, source_target_pairs={{0,128},{32,160},{64,192},{96,224},{128,0},{160,32},{192,64},{224,... | collective-permute-start | bytes 73736 | tf_op jit(solution)/shard_map/ppermute | solution.py:43
  138.9 11.8 %collective-permute-start.46 = (bf16[128,1024]{1,0:T(8,128)(2,1)S(1)}, bf16[128,1024]{1,0:T(8,128)(2,1)S(1)}, u32[]{:S(2)}, u32[]{:S(2)}) collective-permute-start(bf16[128,1024]{1,0:T(8,128)(2,1)S(1)} %get-tuple-element.79), channel_id=1, source_target_pairs={{0,8},{8,0},{1,9},{9,1},{2,10},{10,2},{3,11},{11,3},{4,12},{12,4},... | collective-permute-start | bytes 786440 | tf_op jit(solution)/shard_map/ppermute | solution.py:43
  143.9 4.1 %collective-permute-start.42 = (f32[24,128]{1,0:T(8,128)S(1)}, f32[24,128]{1,0:T(8,128)S(1)}, u32[]{:S(2)}, u32[]{:S(2)}) collective-permute-start(f32[24,128]{1,0:T(8,128)S(1)} %get-tuple-element.85), channel_id=1, source_target_pairs={{0,16},{4,20},{16,0},{20,4},{1,17},{5,21},{17,1},{21,5},{2,18},{6,... | collective-permute-start | bytes 36872 | tf_op jit(solution)/shard_map/ppermute | solution.py:43
  144.5 4.1 %collective-permute-start.44 = (f32[24,128]{1,0:T(8,128)S(1)}, f32[24,128]{1,0:T(8,128)S(1)}, u32[]{:S(2)}, u32[]{:S(2)}) collective-permute-start(f32[24,128]{1,0:T(8,128)S(1)} %get-tuple-element.86), channel_id=1, source_target_pairs={{0,20},{4,16},{16,4},{20,0},{1,21},{5,17},{17,5},{21,1},{2,22},{6,... | collective-permute-start | bytes 36872 | tf_op jit(solution)/shard_map/ppermute | solution.py:43
  145.2 3.3 %collective-permute-start.43 = (f32[24,128]{1,0:T(8,128)S(1)}, f32[24,128]{1,0:T(8,128)S(1)}, u32[]{:S(2)}, u32[]{:S(2)}) collective-permute-start(f32[24,128]{1,0:T(8,128)S(1)} %get-tuple-element.86), channel_id=1, source_target_pairs={{0,4},{4,0},{16,20},{20,16},{1,5},{5,1},{17,21},{21,17},{2,6},{6,2... | collective-permute-start | bytes 36872 | tf_op jit(solution)/shard_map/ppermute | solution.py:43
  148.6 2.1 %collective-permute-start.45 = (f32[24,128]{1,0:T(8,128)S(1)}, f32[24,128]{1,0:T(8,128)S(1)}, u32[]{:S(2)}, u32[]{:S(2)}) collective-permute-start(f32[24,128]{1,0:T(8,128)S(1)} %add_add_fusion.refs_1_), channel_id=1, source_target_pairs={{0,8},{8,0},{1,9},{9,1},{2,10},{10,2},{3,11},{11,3},{4,12},{12,4},... | collective-permute-start | bytes 36872 | tf_op jit(solution)/shard_map/ppermute | solution.py:43

commit v3 on v2

--- a/solution.py
+++ b/solution.py
@@ -415,9 +415,9 @@
         flops=10**11,
     )[0]
     loss = loss + swap(loss, "x", 1) + swap(loss, "x", 2) + swap(loss, "x", 3)
-    sums = exchange_sum(jnp.concatenate([near_sums, loss, far_sums, loss]), "z", (1, 2, 4))
+    sums = exchange_sum(jnp.concatenate([near_sums, far_sums, loss]), "z", (1, 2, 4))
     sums = tie(sums, come_far, come_both, come_near)
-    near_sums, far_sums = jnp.split(sums, 2)
+    near_sums, far_sums = jnp.concatenate([sums[: 2 * lanes], sums[4 * lanes :]]), sums[2 * lanes :]
     back = near_sums + swap(near_sums, RING, 2) + swap(far_sums, RING, 1) + swap(far_sums, RING, 3)
     keep, give = call(
         add_kernel,

time: 152 us -> 153 us (level)
  no operation moved by 1% of the time
where the time goes in v3:
time: 153 us; the launch traced here: 152 us
  waiting for transfers between devices  68.1 us (45%)
  starting transfers between devices  64.6 us (42%)
  Pallas kernels  17.6 us (12%)
    ppermute x36, waiting for transfers between devices, swap(): return lax.ppermute(values, axes, [(k, k ^ step) for k in range(count)])  48.4 us
    ppermute x36, starting transfers between devices, swap(): return lax.ppermute(values, axes, [(k, k ^ step) for k in range(count)])  45.6 us
    ppermute x11, waiting for transfers between devices, shift(): lax.ppermute(values, 'z', [(k, (k + steps) % count) for k in range(count)])  19.7 us
    ppermute x11, starting transfers between devices, shift(): lax.ppermute(values, 'z', [(k, (k + steps) % count) for k in range(count)])  18.9 us
    pallas_call x15, Pallas kernels, call(): pl.pallas_call(kernel, in_specs=[SMEM] + [VMEM] * len(args), out_specs=[V...  17.6 us
  transfers between devices with their start and end apart: 47, of which 29 were waited for; matrix products, arithmetic and copies ran while one was open for 0% of the time, Pallas kernels for 6%

profile of v3, /device:TPU:1, one launch (start us, length us, event | category | flops | bytes accessed | tf_op | source)
XLA Modules:
  0.0 152.4 jit_solution(13508833344665154938)
XLA Ops:
  0.6 1.1 broadcast_select_fusion
  1.7 3.3 %collective-permute-start = (bf16[128,1024]{1,0:T(8,128)(2,1)S(1)}, bf16[128,1024]{1,0:T(8,128)(2,1)S(1)}, u32[]{:S(2)}, u32[]{:S(2)}) collective-permute-start(bf16[128,1024]{1,0:T(8,128)(2,1)S(1)} %get-tuple-element.83), channel_id=1, source_target_pairs={{0,8},{8,0},{1,9},{9,1},{2,10},{10,2},{3,11},{11,3},{4,12},{12,4},... | collective-permute-start | bytes 786440 | tf_op jit(solution)/shard_map/ppermute | solution.py:43
  5.1 1.1 collective-permute-done.got
  6.9 1.4 collective-permute-start.6
  8.4 5.6 %collective-permute-start.3 = (bf16[2,64,1024]{2,1,0:T(8,128)(2,1)S(1)}, bf16[2,64,1024]{2,1,0:T(8,128)(2,1)S(1)}, u32[]{:S(2)}, u32[]{:S(2)}) collective-permute-start(bf16[2,64,1024]{2,1,0:T(8,128)(2,1)S(1)} %get-tuple-element.43.refs_1_.refs_5_), channel_id=1, source_target_pairs={{0,224},{32,0},{64,32},{96,64},{128,96},{160,128},{192,160},{224,1... | collective-permute-start | bytes 786440 | tf_op jit(solution)/shard_map/ppermute | solution.py:48
  14.4 3.8 %collective-permute-start.5 = (bf16[2,64,1024]{2,1,0:T(8,128)(2,1)S(1)}, bf16[2,64,1024]{2,1,0:T(8,128)(2,1)S(1)}, u32[]{:S(2)}, u32[]{:S(2)}) collective-permute-start(bf16[2,64,1024]{2,1,0:T(8,128)(2,1)S(1)} %collective-permute-done.1.refs_2_.refs_8_), channel_id=1, source_target_pairs={{0,224},{32,0},{64,32},{96,64},{128,96},{160,128},{192,160},{224,1... | collective-permute-start | bytes 786440 | tf_op jit(solution)/shard_map/ppermute | solution.py:48
  18.6 3.1 %collective-permute-done.2.refs_2_.right_near = bf16[2,64,1024]{2,1,0:T(8,128)(2,1)S(1)} collective-permute-done((bf16[2,64,1024]{2,1,0:T(8,128)(2,1)S(1)}, bf16[2,64,1024]{2,1,0:T(8,128)(2,1)S(1)}, u32[]{:S(2)}, u32[]{:S(2)}) %collective-permute-start.2) | collective-permute-done | bytes 262176 | tf_op jit(solution)/shard_map/ppermute | solution.py:48
  21.7 2.7 %collective-permute-done.5.refs_5_.left_far = bf16[2,64,1024]{2,1,0:T(8,128)(2,1)S(1)} collective-permute-done((bf16[2,64,1024]{2,1,0:T(8,128)(2,1)S(1)}, bf16[2,64,1024]{2,1,0:T(8,128)(2,1)S(1)}, u32[]{:S(2)}, u32[]{:S(2)}) %collective-permute-start.5) | collective-permute-done | bytes 262176 | tf_op jit(solution)/shard_map/ppermute | solution.py:48
  24.5 3.4 %collective-permute-done.4.refs_4_.right_far = bf16[2,64,1024]{2,1,0:T(8,128)(2,1)S(1)} collective-permute-done((bf16[2,64,1024]{2,1,0:T(8,128)(2,1)S(1)}, bf16[2,64,1024]{2,1,0:T(8,128)(2,1)S(1)}, u32[]{:S(2)}, u32[]{:S(2)}) %collective-permute-start.4) | collective-permute-done | bytes 262176 | tf_op jit(solution)/shard_map/ppermute | solution.py:48
  28.6 2.7 %collective-permute-start.8 = (bf16[4,64,1024]{2,1,0:T(8,128)(2,1)S(1)}, bf16[4,64,1024]{2,1,0:T(8,128)(2,1)S(1)}, u32[]{:S(2)}, u32[]{:S(2)}) collective-permute-start(bf16[4,64,1024]{2,1,0:T(8,128)(2,1)S(1)} %get-tuple-element.49.refs_12_), channel_id=1, source_target_pairs={{0,224},{32,0},{64,32},{96,64},{128,96},{160,128},{192,160},{224,1... | collective-permute-start | bytes 1572872 | tf_op jit(solution)/shard_map/ppermute | solution.py:48
  31.2 0.8 collective-permute-start.10
  32.1 0.7 moments.4.refs_1_
  32.8 1.6 %collective-permute-start.9 = (f32[4,1024]{1,0:T(4,128)S(1)}, f32[4,1024]{1,0:T(4,128)S(1)}, u32[]{:S(2)}, u32[]{:S(2)}) collective-permute-start(f32[4,1024]{1,0:T(4,128)S(1)} %moments.4.refs_1_), channel_id=1, source_target_pairs={{0,128},{32,160},{64,192},{96,224},{128,0},{160,32},{192,64},{224,... | collective-permute-start | bytes 49160 | tf_op jit(solution)/shard_map/ppermute | solution.py:48
  34.4 0.8 moments.5.refs_1_
  35.2 6.7 %collective-permute-done.7.refs_2_.refs_13_ = bf16[4,64,1024]{2,1,0:T(8,128)(2,1)S(1)} collective-permute-done((bf16[4,64,1024]{2,1,0:T(8,128)(2,1)S(1)}, bf16[4,64,1024]{2,1,0:T(8,128)(2,1)S(1)}, u32[]{:S(2)}, u32[]{:S(2)}) %collective-permute-start.7) | collective-permute-done | bytes 524320 | tf_op jit(solution)/shard_map/ppermute | solution.py:48
  41.9 0.8 moments.6.refs_1_
  42.7 1.2 collective-permute-done.10.refs_7_
  44.0 2.7 %collective-permute-start.12 = (bf16[4,64,1024]{2,1,0:T(8,128)(2,1)S(1)}, bf16[4,64,1024]{2,1,0:T(8,128)(2,1)S(1)}, u32[]{:S(2)}, u32[]{:S(2)}) collective-permute-start(bf16[4,64,1024]{2,1,0:T(8,128)(2,1)S(1)} %collective-permute-done.8.refs_3_.refs_14_), channel_id=1, source_target_pairs={{0,224},{32,0},{64,32},{96,64},{128,96},{160,128},{192,160},{224,1... | collective-permute-start | bytes 1572872 | tf_op jit(solution)/shard_map/ppermute | solution.py:48
  46.7 5.5 %collective-permute-done.16.refs_9_ = bf16[2,64,1024]{2,1,0:T(8,128)(2,1)S(1)} collective-permute-done((bf16[2,64,1024]{2,1,0:T(8,128)(2,1)S(1)}, bf16[2,64,1024]{2,1,0:T(8,128)(2,1)S(1)}, u32[]{:S(2)}, u32[]{:S(2)}) %collective-permute-start.16) | collective-permute-done | bytes 262176 | tf_op jit(solution)/shard_map/ppermute | solution.py:43
  52.2 3.3 %collective-permute-done.11.refs_3_.refs_15_ = bf16[4,64,1024]{2,1,0:T(8,128)(2,1)S(1)} collective-permute-done((bf16[4,64,1024]{2,1,0:T(8,128)(2,1)S(1)}, bf16[4,64,1024]{2,1,0:T(8,128)(2,1)S(1)}, u32[]{:S(2)}, u32[]{:S(2)}) %collective-permute-start.11) | collective-permute-done | bytes 524320 | tf_op jit(solution)/shard_map/ppermute | solution.py:48
  55.6 2.5 %collective-permute-start.18 = (bf16[2,64,1024]{2,1,0:T(8,128)(2,1)S(1)}, bf16[2,64,1024]{2,1,0:T(8,128)(2,1)S(1)}, u32[]{:S(2)}, u32[]{:S(2)}) collective-permute-start(bf16[2,64,1024]{2,1,0:T(8,128)(2,1)S(1)} %slice.23), channel_id=1, source_target_pairs={{0,224},{32,0},{64,32},{96,64},{128,96},{160,128},{192,160},{224,1... | collective-permute-start | bytes 786440 | tf_op jit(solution)/shard_map/ppermute | solution.py:48
  58.0 0.8 moments.7.refs_1_
  58.9 1.0 collective-permute-start.14
  60.0 2.2 %collective-permute-start.13 = (f32[4,1024]{1,0:T(4,128)S(1)}, f32[4,1024]{1,0:T(4,128)S(1)}, u32[]{:S(2)}, u32[]{:S(2)}) collective-permute-start(f32[4,1024]{1,0:T(4,128)S(1)} %moments.7.refs_1_), channel_id=1, source_target_pairs={{0,4},{4,0},{16,20},{20,16},{1,5},{5,1},{17,21},{21,17},{2,6},{6,2... | collective-permute-start | bytes 49160 | tf_op jit(solution)/shard_map/ppermute | solution.py:43
  63.1 0.7 collective-permute-done.13.refs_2_
  63.8 3.2 %gram.1 = (bf16[3,256,512]{2,1,0:T(8,128)(2,1)S(1)}, bf16[1024,2048]{1,0:T(8,128)(2,1)S(1)}, bf16[512,2048]{1,0:T(8,128)(2,1)S(1)}, f32[4,1024]{1,0:T(4,128)S(1)}) custom-call(s32[3]{0:T(128)S(1)} %pad_add_fusion.ids.refs_0_, f32[4,1024]{1,0:T(4,128)S(1)} %moments.7.refs_1_, f32[4,1024]{1,0:T(4,128)S(1)} %collective-permute-done.13.refs_2_, ...), custom_call_target="tpu_custom_call" | custom-call | flops 1610612736 | tf_op jit(solution)/shard_map/gram/pallas_call | solution.py:28
  67.0 1.4 last_gram.1
  68.5 5.8 %collective-permute-start.19 = (bf16[256,512]{1,0:T(8,128)(2,1)S(1)}, bf16[256,512]{1,0:T(8,128)(2,1)S(1)}, u32[]{:S(2)}, u32[]{:S(2)}) collective-permute-start(bf16[256,512]{1,0:T(8,128)(2,1)S(1)} %get-tuple-element.58), channel_id=1, source_target_pairs={{0,8},{1,9},{2,10},{3,11},{8,0},{9,1},{10,2},{11,3},{4,12},{5,13},... | collective-permute-start | bytes 786440 | tf_op jit(solution)/shard_map/ppermute | solution.py:43
  74.3 1.2 collective-permute-start.24
  75.5 2.8 %collective-permute-start.25 = (bf16[256,512]{1,0:T(8,128)(2,1)S(1)}, bf16[256,512]{1,0:T(8,128)(2,1)S(1)}, u32[]{:S(2)}, u32[]{:S(2)}) collective-permute-start(bf16[256,512]{1,0:T(8,128)(2,1)S(1)} %get-tuple-element.62), channel_id=1, source_target_pairs={{0,10},{1,11},{2,8},{3,9},{8,2},{9,3},{10,0},{11,1},{4,14},{5,15},... | collective-permute-start | bytes 786440 | tf_op jit(solution)/shard_map/ppermute | solution.py:43
  78.9 0.8 collective-permute-done.20.theirs
  79.7 0.8 native.1
  81.0 0.8 collective-permute-done.21
  81.8 1.7 %collective-permute-start.22 = (f32[4,1024]{1,0:T(4,128)S(1)}, f32[4,1024]{1,0:T(4,128)S(1)}, u32[]{:S(2)}, u32[]{:S(2)}) collective-permute-start(f32[4,1024]{1,0:T(4,128)S(1)} %add.43), channel_id=1, source_target_pairs={{0,16},{16,0},{1,17},{17,1},{2,18},{18,2},{3,19},{19,3},{4,20},{20... | collective-permute-start | bytes 49160 | tf_op jit(solution)/shard_map/ppermute | solution.py:43
  83.6 2.6 %collective-permute-done.22 = f32[4,1024]{1,0:T(4,128)S(1)} collective-permute-done((f32[4,1024]{1,0:T(4,128)S(1)}, f32[4,1024]{1,0:T(4,128)S(1)}, u32[]{:S(2)}, u32[]{:S(2)}) %collective-permute-start.22) | collective-permute-done | bytes 16416 | tf_op jit(solution)/shard_map/ppermute | solution.py:43
  86.2 2.9 %collective-permute-done.23 = f32[4,1024]{1,0:T(4,128)S(1)} collective-permute-done((f32[4,1024]{1,0:T(4,128)S(1)}, f32[4,1024]{1,0:T(4,128)S(1)}, u32[]{:S(2)}, u32[]{:S(2)}) %collective-permute-start.23) | collective-permute-done | bytes 16416 | tf_op jit(solution)/shard_map/ppermute | solution.py:43
  89.1 1.1 collective-permute-done.25.refs_2_
  90.2 2.9 %collective-permute-done.26.refs_3_ = bf16[256,512]{1,0:T(8,128)(2,1)S(1)} collective-permute-done((bf16[256,512]{1,0:T(8,128)(2,1)S(1)}, bf16[256,512]{1,0:T(8,128)(2,1)S(1)}, u32[]{:S(2)}, u32[]{:S(2)}) %collective-permute-start.26) | collective-permute-done | bytes 262176 | tf_op jit(solution)/shard_map/ppermute | solution.py:43
  93.1 0.7 reduce.1
  94.5 2.8 %collective-permute-start.31 = (bf16[512,256]{1,0:T(8,128)(2,1)S(1)}, bf16[512,256]{1,0:T(8,128)(2,1)S(1)}, u32[]{:S(2)}, u32[]{:S(2)}) collective-permute-start(bf16[512,256]{1,0:T(8,128)(2,1)S(1)} %get-tuple-element.64.refs_1_), channel_id=1, source_target_pairs={{0,2},{1,3},{2,0},{3,1},{4,6},{5,7},{6,4},{7,5},{8,10},{9,11},{10,... | collective-permute-start | bytes 786440 | tf_op jit(solution)/shard_map/ppermute | solution.py:43
  97.3 3.8 %collective-permute-done.28 = f32[4,1024]{1,0:T(4,128)S(1)} collective-permute-done((f32[4,1024]{1,0:T(4,128)S(1)}, f32[4,1024]{1,0:T(4,128)S(1)}, u32[]{:S(2)}, u32[]{:S(2)}) %collective-permute-start.28) | collective-permute-done | bytes 16416 | tf_op jit(solution)/shard_map/ppermute | solution.py:43
  101.1 1.5 collective-permute-start.29
  102.6 5.0 %collective-permute-done.29 = f32[4,1024]{1,0:T(4,128)S(1)} collective-permute-done((f32[4,1024]{1,0:T(4,128)S(1)}, f32[4,1024]{1,0:T(4,128)S(1)}, u32[]{:S(2)}, u32[]{:S(2)}) %collective-permute-start.29) | collective-permute-done | bytes 16416 | tf_op jit(solution)/shard_map/ppermute | solution.py:43
  107.6 0.9 collective-permute-done.32.refs_4_
  108.6 1.9 %products.3 = (bf16[256,1024]{1,0:T(8,128)(2,1)S(1)}, bf16[256,1024]{1,0:T(8,128)(2,1)S(1)}, f32[16,128]{1,0:T(8,128)S(1)}) custom-call(s32[3]{0:T(128)S(1)} %pad_add_fusion.ids.refs_0_, bf16[512,256]{1,0:T(8,128)(2,1)S(1)} %get-tuple-element.64.refs_1_, bf16[512,256]{1,0:T(8,128)(2,1)S(1)} %collective-permute-done.27.refs_2_, ...), custom_call_target="tpu_custom_call" | custom-call | flops 1073741824 | tf_op jit(solution)/shard_map/products/pallas_call | solution.py:28
  110.5 0.8 loss.1
  111.3 1.1 collective-permute-start.35
  112.9 1.7 %collective-permute-start.33 = (f32[8,128]{1,0:T(8,128)S(1)}, f32[8,128]{1,0:T(8,128)S(1)}, u32[]{:S(2)}, u32[]{:S(2)}) collective-permute-start(f32[8,128]{1,0:T(8,128)S(1)} %loss.1), channel_id=1, source_target_pairs={{0,1},{1,0},{2,3},{3,2},{4,5},{5,4},{6,7},{7,6},{8,9},{9,8},{10,11... | collective-permute-start | bytes 12296 | tf_op jit(solution)/shard_map/ppermute | solution.py:43
  114.6 1.6 %collective-permute-start.39 = (bf16[256,1024]{1,0:T(8,128)(2,1)S(1)}, bf16[256,1024]{1,0:T(8,128)(2,1)S(1)}, u32[]{:S(2)}, u32[]{:S(2)}) collective-permute-start(bf16[256,1024]{1,0:T(8,128)(2,1)S(1)} %get-tuple-element.71), channel_id=1, source_target_pairs={{0,4},{4,0},{16,20},{20,16},{1,5},{5,1},{17,21},{21,17},{2,6},{6,2... | collective-permute-start | bytes 1572872 | tf_op jit(solution)/shard_map/ppermute | solution.py:43
  116.9 1.9 %products.2 = (f32[256,1024]{1,0:T(8,128)S(1)}, bf16[256,1024]{1,0:T(8,128)(2,1)S(1)}, f32[16,128]{1,0:T(8,128)S(1)}) custom-call(s32[3]{0:T(128)S(1)} %pad_add_fusion.ids.refs_0_, bf16[512,256]{1,0:T(8,128)(2,1)S(1)} %get-tuple-element.64.refs_1_, bf16[512,256]{1,0:T(8,128)(2,1)S(1)} %collective-permute-done.27.refs_2_, ...), custom_call_target="tpu_custom_call" | custom-call | flops 99999997952 | tf_op jit(solution)/shard_map/products/pallas_call | solution.py:28
  118.8 1.3 collective-permute-start.41
  120.2 2.9 %collective-permute-done.36 = f32[40,128]{1,0:T(8,128)S(1)} collective-permute-done((f32[40,128]{1,0:T(8,128)S(1)}, f32[40,128]{1,0:T(8,128)S(1)}, u32[]{:S(2)}, u32[]{:S(2)}) %collective-permute-start.36) | collective-permute-done | bytes 20512 | tf_op jit(solution)/shard_map/ppermute | solution.py:43
  123.1 0.7 collective-permute-start.37
  123.8 3.1 %collective-permute-done.37 = f32[40,128]{1,0:T(8,128)S(1)} collective-permute-done((f32[40,128]{1,0:T(8,128)S(1)}, f32[40,128]{1,0:T(8,128)S(1)}, u32[]{:S(2)}, u32[]{:S(2)}) %collective-permute-start.37) | collective-permute-done | bytes 20512 | tf_op jit(solution)/shard_map/ppermute | solution.py:43
  126.9 2.4 %collective-permute-start.38 = (f32[40,128]{1,0:T(8,128)S(1)}, f32[40,128]{1,0:T(8,128)S(1)}, u32[]{:S(2)}, u32[]{:S(2)}) collective-permute-start(f32[40,128]{1,0:T(8,128)S(1)} %add.52), channel_id=1, source_target_pairs={{0,128},{32,160},{64,192},{96,224},{128,0},{160,32},{192,64},{224,... | collective-permute-start | bytes 61448 | tf_op jit(solution)/shard_map/ppermute | solution.py:43
  129.3 4.2 %collective-permute-done.38 = f32[40,128]{1,0:T(8,128)S(1)} collective-permute-done((f32[40,128]{1,0:T(8,128)S(1)}, f32[40,128]{1,0:T(8,128)S(1)}, u32[]{:S(2)}, u32[]{:S(2)}) %collective-permute-start.38) | collective-permute-done | bytes 20512 | tf_op jit(solution)/shard_map/ppermute | solution.py:43
  133.5 4.6 %collective-permute-done.41.refs_2_ = bf16[256,1024]{1,0:T(8,128)(2,1)S(1)} collective-permute-done((bf16[256,1024]{1,0:T(8,128)(2,1)S(1)}, bf16[256,1024]{1,0:T(8,128)(2,1)S(1)}, u32[]{:S(2)}, u32[]{:S(2)}) %collective-permute-start.41) | collective-permute-done | bytes 524320 | tf_op jit(solution)/shard_map/ppermute | solution.py:43
  138.1 0.8 add.68
  138.9 5.0 %collective-permute-start.46 = (bf16[128,1024]{1,0:T(8,128)(2,1)S(1)}, bf16[128,1024]{1,0:T(8,128)(2,1)S(1)}, u32[]{:S(2)}, u32[]{:S(2)}) collective-permute-start(bf16[128,1024]{1,0:T(8,128)(2,1)S(1)} %get-tuple-element.79), channel_id=1, source_target_pairs={{0,8},{8,0},{1,9},{9,1},{2,10},{10,2},{3,11},{11,3},{4,12},{12,4},... | collective-permute-start | bytes 786440 | tf_op jit(solution)/shard_map/ppermute | solution.py:43
  145.1 1.4 collective-permute-start.43
  146.5 1.4 collective-permute-done.42
  148.5 1.4 collective-permute-start.45
  149.9 0.8 collective-permute-done.45.refs_2_
  150.7 1.7 %finish.1 = (bf16[128,1024]{1,0:T(8,128)(2,1)}, bf16[128,1024]{1,0:T(8,128)(2,1)}, f32[1,128]{1,0:T(1,128)}) custom-call(s32[3]{0:T(128)S(1)} %pad_add_fusion.ids.refs_0_, f32[24,128]{1,0:T(8,128)S(1)} %add_add_fusion.refs_1_, f32[24,128]{1,0:T(8,128)S(1)} %collective-permute-done.45.refs_2_, f32[4,1024]{1,0:T(4,128)S(1)} %add.47.refs_3_, ...), custom_call_target="tpu_custom_call" | custom-call | tf_op jit(solution)/shard_map/finish/pallas_call | solution.py:28
  (69 shorter events, 8.4 us)
Async XLA Ops:
  1.7 4.5 %collective-permute-start = (bf16[128,1024]{1,0:T(8,128)(2,1)S(1)}, bf16[128,1024]{1,0:T(8,128)(2,1)S(1)}, u32[]{:S(2)}, u32[]{:S(2)}) collective-permute-start(bf16[128,1024]{1,0:T(8,128)(2,1)S(1)} %get-tuple-element.83), channel_id=1, source_target_pairs={{0,8},{8,0},{1,9},{9,1},{2,10},{10,2},{3,11},{11,3},{4,12},{12,4},... | collective-permute-start | bytes 786440 | tf_op jit(solution)/shard_map/ppermute | solution.py:43
  6.8 7.6 %collective-permute-start.1 = (bf16[2,64,1024]{2,1,0:T(8,128)(2,1)S(1)}, bf16[2,64,1024]{2,1,0:T(8,128)(2,1)S(1)}, u32[]{:S(2)}, u32[]{:S(2)}) collective-permute-start(bf16[2,64,1024]{2,1,0:T(8,128)(2,1)S(1)} %get-tuple-element.44.refs_6_), channel_id=1, source_target_pairs={{0,4},{4,0},{16,20},{20,16},{1,5},{5,1},{17,21},{21,17},{2,6},{6,2... | collective-permute-start | bytes 786440 | tf_op jit(solution)/shard_map/ppermute | solution.py:43
  6.9 21.6 %collective-permute-start.6 = (bf16[4,64,1024]{2,1,0:T(8,128)(2,1)S(1)}, bf16[4,64,1024]{2,1,0:T(8,128)(2,1)S(1)}, u32[]{:S(2)}, u32[]{:S(2)}) collective-permute-start(bf16[4,64,1024]{2,1,0:T(8,128)(2,1)S(1)} %get-tuple-element.47), channel_id=1, source_target_pairs={{0,20},{4,16},{16,4},{20,0},{1,21},{5,17},{17,5},{21,1},{2,22},{6,... | collective-permute-start | bytes 1572872 | tf_op jit(solution)/shard_map/ppermute | solution.py:43
  8.4 10.2 %collective-permute-start.3 = (bf16[2,64,1024]{2,1,0:T(8,128)(2,1)S(1)}, bf16[2,64,1024]{2,1,0:T(8,128)(2,1)S(1)}, u32[]{:S(2)}, u32[]{:S(2)}) collective-permute-start(bf16[2,64,1024]{2,1,0:T(8,128)(2,1)S(1)} %get-tuple-element.43.refs_1_.refs_5_), channel_id=1, source_target_pairs={{0,224},{32,0},{64,32},{96,64},{128,96},{160,128},{192,160},{224,1... | collective-permute-start | bytes 786440 | tf_op jit(solution)/shard_map/ppermute | solution.py:48
  13.9 7.8 %collective-permute-start.2 = (bf16[2,64,1024]{2,1,0:T(8,128)(2,1)S(1)}, bf16[2,64,1024]{2,1,0:T(8,128)(2,1)S(1)}, u32[]{:S(2)}, u32[]{:S(2)}) collective-permute-start(bf16[2,64,1024]{2,1,0:T(8,128)(2,1)S(1)} %get-tuple-element.43.refs_1_.refs_5_), channel_id=1, source_target_pairs={{0,32},{32,64},{64,96},{96,128},{128,160},{160,192},{192,224},{224... | collective-permute-start | bytes 786440 | tf_op jit(solution)/shard_map/ppermute | solution.py:48
  14.4 10.0 %collective-permute-start.5 = (bf16[2,64,1024]{2,1,0:T(8,128)(2,1)S(1)}, bf16[2,64,1024]{2,1,0:T(8,128)(2,1)S(1)}, u32[]{:S(2)}, u32[]{:S(2)}) collective-permute-start(bf16[2,64,1024]{2,1,0:T(8,128)(2,1)S(1)} %collective-permute-done.1.refs_2_.refs_8_), channel_id=1, source_target_pairs={{0,224},{32,0},{64,32},{96,64},{128,96},{160,128},{192,160},{224,1... | collective-permute-start | bytes 786440 | tf_op jit(solution)/shard_map/ppermute | solution.py:48
  18.3 9.6 %collective-permute-start.4 = (bf16[2,64,1024]{2,1,0:T(8,128)(2,1)S(1)}, bf16[2,64,1024]{2,1,0:T(8,128)(2,1)S(1)}, u32[]{:S(2)}, u32[]{:S(2)}) collective-permute-start(bf16[2,64,1024]{2,1,0:T(8,128)(2,1)S(1)} %collective-permute-done.1.refs_2_.refs_8_), channel_id=1, source_target_pairs={{0,32},{32,64},{64,96},{96,128},{128,160},{160,192},{192,224},{224... | collective-permute-start | bytes 786440 | tf_op jit(solution)/shard_map/ppermute | solution.py:48
  28.5 13.4 %collective-permute-start.7 = (bf16[4,64,1024]{2,1,0:T(8,128)(2,1)S(1)}, bf16[4,64,1024]{2,1,0:T(8,128)(2,1)S(1)}, u32[]{:S(2)}, u32[]{:S(2)}) collective-permute-start(bf16[4,64,1024]{2,1,0:T(8,128)(2,1)S(1)} %get-tuple-element.48.refs_11_), channel_id=1, source_target_pairs={{0,32},{32,64},{64,96},{96,128},{128,160},{160,192},{192,224},{224... | collective-permute-start | bytes 1572872 | tf_op jit(solution)/shard_map/ppermute | solution.py:48
  28.6 13.3 %collective-permute-start.8 = (bf16[4,64,1024]{2,1,0:T(8,128)(2,1)S(1)}, bf16[4,64,1024]{2,1,0:T(8,128)(2,1)S(1)}, u32[]{:S(2)}, u32[]{:S(2)}) collective-permute-start(bf16[4,64,1024]{2,1,0:T(8,128)(2,1)S(1)} %get-tuple-element.49.refs_12_), channel_id=1, source_target_pairs={{0,224},{32,0},{64,32},{96,64},{128,96},{160,128},{192,160},{224,1... | collective-permute-start | bytes 1572872 | tf_op jit(solution)/shard_map/ppermute | solution.py:48
  31.2 12.7 %collective-permute-start.10 = (bf16[4,64,1024]{2,1,0:T(8,128)(2,1)S(1)}, bf16[4,64,1024]{2,1,0:T(8,128)(2,1)S(1)}, u32[]{:S(2)}, u32[]{:S(2)}) collective-permute-start(bf16[4,64,1024]{2,1,0:T(8,128)(2,1)S(1)} %get-tuple-element.47), channel_id=1, source_target_pairs={{0,16},{4,20},{16,0},{20,4},{1,17},{5,21},{17,1},{21,5},{2,18},{6,... | collective-permute-start | bytes 1572872 | tf_op jit(solution)/shard_map/ppermute | solution.py:43
  32.8 10.0 %collective-permute-start.9 = (f32[4,1024]{1,0:T(4,128)S(1)}, f32[4,1024]{1,0:T(4,128)S(1)}, u32[]{:S(2)}, u32[]{:S(2)}) collective-permute-start(f32[4,1024]{1,0:T(4,128)S(1)} %moments.4.refs_1_), channel_id=1, source_target_pairs={{0,128},{32,160},{64,192},{96,224},{128,0},{160,32},{192,64},{224,... | collective-permute-start | bytes 49160 | tf_op jit(solution)/shard_map/ppermute | solution.py:48
  44.0 11.5 %collective-permute-start.11 = (bf16[4,64,1024]{2,1,0:T(8,128)(2,1)S(1)}, bf16[4,64,1024]{2,1,0:T(8,128)(2,1)S(1)}, u32[]{:S(2)}, u32[]{:S(2)}) collective-permute-start(bf16[4,64,1024]{2,1,0:T(8,128)(2,1)S(1)} %collective-permute-done.7.refs_2_.refs_13_), channel_id=1, source_target_pairs={{0,32},{32,64},{64,96},{96,128},{128,160},{160,192},{192,224},{224... | collective-permute-start | bytes 1572872 | tf_op jit(solution)/shard_map/ppermute | solution.py:48
  44.0 11.5 %collective-permute-start.12 = (bf16[4,64,1024]{2,1,0:T(8,128)(2,1)S(1)}, bf16[4,64,1024]{2,1,0:T(8,128)(2,1)S(1)}, u32[]{:S(2)}, u32[]{:S(2)}) collective-permute-start(bf16[4,64,1024]{2,1,0:T(8,128)(2,1)S(1)} %collective-permute-done.8.refs_3_.refs_14_), channel_id=1, source_target_pairs={{0,224},{32,0},{64,32},{96,64},{128,96},{160,128},{192,160},{224,1... | collective-permute-start | bytes 1572872 | tf_op jit(solution)/shard_map/ppermute | solution.py:48
  46.7 5.5 %collective-permute-start.16 = (bf16[2,64,1024]{2,1,0:T(8,128)(2,1)S(1)}, bf16[2,64,1024]{2,1,0:T(8,128)(2,1)S(1)}, u32[]{:S(2)}, u32[]{:S(2)}) collective-permute-start(bf16[2,64,1024]{2,1,0:T(8,128)(2,1)S(1)} %get-tuple-element.43.refs_1_.refs_5_), channel_id=1, source_target_pairs={{0,4},{4,0},{16,20},{20,16},{1,5},{5,1},{17,21},{21,17},{2,6},{6,2... | collective-permute-start | bytes 786440 | tf_op jit(solution)/shard_map/ppermute | solution.py:43
  55.6 11.5 %collective-permute-start.18 = (bf16[2,64,1024]{2,1,0:T(8,128)(2,1)S(1)}, bf16[2,64,1024]{2,1,0:T(8,128)(2,1)S(1)}, u32[]{:S(2)}, u32[]{:S(2)}) collective-permute-start(bf16[2,64,1024]{2,1,0:T(8,128)(2,1)S(1)} %slice.23), channel_id=1, source_target_pairs={{0,224},{32,0},{64,32},{96,64},{128,96},{160,128},{192,160},{224,1... | collective-permute-start | bytes 786440 | tf_op jit(solution)/shard_map/ppermute | solution.py:48
  58.0 9.0 %collective-permute-start.17 = (bf16[2,64,1024]{2,1,0:T(8,128)(2,1)S(1)}, bf16[2,64,1024]{2,1,0:T(8,128)(2,1)S(1)}, u32[]{:S(2)}, u32[]{:S(2)}) collective-permute-start(bf16[2,64,1024]{2,1,0:T(8,128)(2,1)S(1)} %slice.22), channel_id=1, source_target_pairs={{0,32},{32,64},{64,96},{96,128},{128,160},{160,192},{192,224},{224... | collective-permute-start | bytes 786440 | tf_op jit(solution)/shard_map/ppermute | solution.py:48
  58.8 3.9 %collective-permute-start.15 = (f32[4,1024]{1,0:T(4,128)S(1)}, f32[4,1024]{1,0:T(4,128)S(1)}, u32[]{:S(2)}, u32[]{:S(2)}) collective-permute-start(f32[4,1024]{1,0:T(4,128)S(1)} %moments.7.refs_1_), channel_id=1, source_target_pairs={{0,20},{4,16},{16,4},{20,0},{1,21},{5,17},{17,5},{21,1},{2,22},{6,... | collective-permute-start | bytes 49160 | tf_op jit(solution)/shard_map/ppermute | solution.py:43
  58.9 4.2 %collective-permute-start.14 = (f32[4,1024]{1,0:T(4,128)S(1)}, f32[4,1024]{1,0:T(4,128)S(1)}, u32[]{:S(2)}, u32[]{:S(2)}) collective-permute-start(f32[4,1024]{1,0:T(4,128)S(1)} %moments.7.refs_1_), channel_id=1, source_target_pairs={{0,16},{4,20},{16,0},{20,4},{1,17},{5,21},{17,1},{21,5},{2,18},{6,... | collective-permute-start | bytes 49160 | tf_op jit(solution)/shard_map/ppermute | solution.py:43
  60.0 3.8 %collective-permute-start.13 = (f32[4,1024]{1,0:T(4,128)S(1)}, f32[4,1024]{1,0:T(4,128)S(1)}, u32[]{:S(2)}, u32[]{:S(2)}) collective-permute-start(f32[4,1024]{1,0:T(4,128)S(1)} %moments.7.refs_1_), channel_id=1, source_target_pairs={{0,4},{4,0},{16,20},{20,16},{1,5},{5,1},{17,21},{21,17},{2,6},{6,2... | collective-permute-start | bytes 49160 | tf_op jit(solution)/shard_map/ppermute | solution.py:43
  67.0 12.7 %copy-start = (bf16[128,1024]{1,0:T(8,128)(2,1)S(1)}, bf16[128,1024]{1,0:T(8,128)(2,1)}, u32[]{:S(2)}) copy-start(bf16[128,1024]{1,0:T(8,128)(2,1)} %view_b.1) | copy-start | bytes 786436
  67.0 12.7 %copy-start.1 = (bf16[128,1024]{1,0:T(8,128)(2,1)S(1)}, bf16[128,1024]{1,0:T(8,128)(2,1)}, u32[]{:S(2)}) copy-start(bf16[128,1024]{1,0:T(8,128)(2,1)} %view_a.1) | copy-start | bytes 786436
  68.5 20.6 %collective-permute-start.19 = (bf16[256,512]{1,0:T(8,128)(2,1)S(1)}, bf16[256,512]{1,0:T(8,128)(2,1)S(1)}, u32[]{:S(2)}, u32[]{:S(2)}) collective-permute-start(bf16[256,512]{1,0:T(8,128)(2,1)S(1)} %get-tuple-element.58), channel_id=1, source_target_pairs={{0,8},{1,9},{2,10},{3,11},{8,0},{9,1},{10,2},{11,3},{4,12},{5,13},... | collective-permute-start | bytes 786440 | tf_op jit(solution)/shard_map/ppermute | solution.py:43
  74.3 14.8 %collective-permute-start.24 = (bf16[256,512]{1,0:T(8,128)(2,1)S(1)}, bf16[256,512]{1,0:T(8,128)(2,1)S(1)}, u32[]{:S(2)}, u32[]{:S(2)}) collective-permute-start(bf16[256,512]{1,0:T(8,128)(2,1)S(1)} %get-tuple-element.61), channel_id=1, source_target_pairs={{0,9},{1,8},{2,11},{3,10},{8,1},{9,0},{10,3},{11,2},{4,13},{5,12},... | collective-permute-start | bytes 786440 | tf_op jit(solution)/shard_map/ppermute | solution.py:43
  75.5 14.7 %collective-permute-start.25 = (bf16[256,512]{1,0:T(8,128)(2,1)S(1)}, bf16[256,512]{1,0:T(8,128)(2,1)S(1)}, u32[]{:S(2)}, u32[]{:S(2)}) collective-permute-start(bf16[256,512]{1,0:T(8,128)(2,1)S(1)} %get-tuple-element.62), channel_id=1, source_target_pairs={{0,10},{1,11},{2,8},{3,9},{8,2},{9,3},{10,0},{11,1},{4,14},{5,15},... | collective-permute-start | bytes 786440 | tf_op jit(solution)/shard_map/ppermute | solution.py:43
  78.3 14.8 %collective-permute-start.26 = (bf16[256,512]{1,0:T(8,128)(2,1)S(1)}, bf16[256,512]{1,0:T(8,128)(2,1)S(1)}, u32[]{:S(2)}, u32[]{:S(2)}) collective-permute-start(bf16[256,512]{1,0:T(8,128)(2,1)S(1)} %get-tuple-element.63), channel_id=1, source_target_pairs={{0,11},{1,10},{2,9},{3,8},{8,3},{9,2},{10,1},{11,0},{4,15},{5,14},... | collective-permute-start | bytes 786440 | tf_op jit(solution)/shard_map/ppermute | solution.py:43
  78.4 1.3 collective-permute-start.20
  80.6 1.3 collective-permute-start.21
  81.8 4.4 %collective-permute-start.22 = (f32[4,1024]{1,0:T(4,128)S(1)}, f32[4,1024]{1,0:T(4,128)S(1)}, u32[]{:S(2)}, u32[]{:S(2)}) collective-permute-start(f32[4,1024]{1,0:T(4,128)S(1)} %add.43), channel_id=1, source_target_pairs={{0,16},{16,0},{1,17},{17,1},{2,18},{18,2},{3,19},{19,3},{4,20},{20... | collective-permute-start | bytes 49160 | tf_op jit(solution)/shard_map/ppermute | solution.py:43
  86.2 2.9 %collective-permute-start.23 = (f32[4,1024]{1,0:T(4,128)S(1)}, f32[4,1024]{1,0:T(4,128)S(1)}, u32[]{:S(2)}, u32[]{:S(2)}) collective-permute-start(f32[4,1024]{1,0:T(4,128)S(1)} %add.44), channel_id=1, source_target_pairs={{0,32},{32,0},{64,96},{96,64},{128,160},{160,128},{192,224},{224,1... | collective-permute-start | bytes 49160 | tf_op jit(solution)/shard_map/ppermute | solution.py:43
  93.8 13.8 %collective-permute-start.30 = (bf16[512,256]{1,0:T(8,128)(2,1)S(1)}, bf16[512,256]{1,0:T(8,128)(2,1)S(1)}, u32[]{:S(2)}, u32[]{:S(2)}) collective-permute-start(bf16[512,256]{1,0:T(8,128)(2,1)S(1)} %get-tuple-element.64.refs_1_), channel_id=1, source_target_pairs={{0,8},{8,0},{1,9},{9,1},{2,10},{10,2},{3,11},{11,3},{4,12},{12,4},... | collective-permute-start | bytes 786440 | tf_op jit(solution)/shard_map/ppermute | solution.py:43
  94.1 13.6 %collective-permute-start.27 = (bf16[512,256]{1,0:T(8,128)(2,1)S(1)}, bf16[512,256]{1,0:T(8,128)(2,1)S(1)}, u32[]{:S(2)}, u32[]{:S(2)}) collective-permute-start(bf16[512,256]{1,0:T(8,128)(2,1)S(1)} %get-tuple-element.64.refs_1_), channel_id=1, source_target_pairs={{0,1},{1,0},{2,3},{3,2},{4,5},{5,4},{6,7},{7,6},{8,9},{9,8},{10,11... | collective-permute-start | bytes 786440 | tf_op jit(solution)/shard_map/ppermute | solution.py:43
  94.1 14.5 %collective-permute-start.32 = (bf16[512,256]{1,0:T(8,128)(2,1)S(1)}, bf16[512,256]{1,0:T(8,128)(2,1)S(1)}, u32[]{:S(2)}, u32[]{:S(2)}) collective-permute-start(bf16[512,256]{1,0:T(8,128)(2,1)S(1)} %get-tuple-element.64.refs_1_), channel_id=1, source_target_pairs={{0,3},{1,2},{2,1},{3,0},{4,7},{5,6},{6,5},{7,4},{8,11},{9,10},{10,... | collective-permute-start | bytes 786440 | tf_op jit(solution)/shard_map/ppermute | solution.py:43
  94.5 14.0 %collective-permute-start.31 = (bf16[512,256]{1,0:T(8,128)(2,1)S(1)}, bf16[512,256]{1,0:T(8,128)(2,1)S(1)}, u32[]{:S(2)}, u32[]{:S(2)}) collective-permute-start(bf16[512,256]{1,0:T(8,128)(2,1)S(1)} %get-tuple-element.64.refs_1_), channel_id=1, source_target_pairs={{0,2},{1,3},{2,0},{3,1},{4,6},{5,7},{6,4},{7,5},{8,10},{9,11},{10,... | collective-permute-start | bytes 786440 | tf_op jit(solution)/shard_map/ppermute | solution.py:43
  97.3 3.8 %collective-permute-start.28 = (f32[4,1024]{1,0:T(4,128)S(1)}, f32[4,1024]{1,0:T(4,128)S(1)}, u32[]{:S(2)}, u32[]{:S(2)}) collective-permute-start(f32[4,1024]{1,0:T(4,128)S(1)} %add.45), channel_id=1, source_target_pairs={{0,64},{32,96},{64,0},{96,32},{128,192},{160,224},{192,128},{224,1... | collective-permute-start | bytes 49160 | tf_op jit(solution)/shard_map/ppermute | solution.py:43
  101.1 6.5 %collective-permute-start.29 = (f32[4,1024]{1,0:T(4,128)S(1)}, f32[4,1024]{1,0:T(4,128)S(1)}, u32[]{:S(2)}, u32[]{:S(2)}) collective-permute-start(f32[4,1024]{1,0:T(4,128)S(1)} %add.46), channel_id=1, source_target_pairs={{0,128},{32,160},{64,192},{96,224},{128,0},{160,32},{192,64},{224,... | collective-permute-start | bytes 49160 | tf_op jit(solution)/shard_map/ppermute | solution.py:43
  111.3 7.5 %collective-permute-start.35 = (f32[8,128]{1,0:T(8,128)S(1)}, f32[8,128]{1,0:T(8,128)S(1)}, u32[]{:S(2)}, u32[]{:S(2)}) collective-permute-start(f32[8,128]{1,0:T(8,128)S(1)} %loss.1), channel_id=1, source_target_pairs={{0,3},{1,2},{2,1},{3,0},{4,7},{5,6},{6,5},{7,4},{8,11},{9,10},{10,... | collective-permute-start | bytes 12296 | tf_op jit(solution)/shard_map/ppermute | solution.py:43
  112.4 7.7 %collective-permute-start.34 = (f32[8,128]{1,0:T(8,128)S(1)}, f32[8,128]{1,0:T(8,128)S(1)}, u32[]{:S(2)}, u32[]{:S(2)}) collective-permute-start(f32[8,128]{1,0:T(8,128)S(1)} %loss.1), channel_id=1, source_target_pairs={{0,2},{1,3},{2,0},{3,1},{4,6},{5,7},{6,4},{7,5},{8,10},{9,11},{10,... | collective-permute-start | bytes 12296 | tf_op jit(solution)/shard_map/ppermute | solution.py:43
  112.9 7.1 %collective-permute-start.33 = (f32[8,128]{1,0:T(8,128)S(1)}, f32[8,128]{1,0:T(8,128)S(1)}, u32[]{:S(2)}, u32[]{:S(2)}) collective-permute-start(f32[8,128]{1,0:T(8,128)S(1)} %loss.1), channel_id=1, source_target_pairs={{0,1},{1,0},{2,3},{3,2},{4,5},{5,4},{6,7},{7,6},{8,9},{9,8},{10,11... | collective-permute-start | bytes 12296 | tf_op jit(solution)/shard_map/ppermute | solution.py:43
  114.6 18.8 %collective-permute-start.39 = (bf16[256,1024]{1,0:T(8,128)(2,1)S(1)}, bf16[256,1024]{1,0:T(8,128)(2,1)S(1)}, u32[]{:S(2)}, u32[]{:S(2)}) collective-permute-start(bf16[256,1024]{1,0:T(8,128)(2,1)S(1)} %get-tuple-element.71), channel_id=1, source_target_pairs={{0,4},{4,0},{16,20},{20,16},{1,5},{5,1},{17,21},{21,17},{2,6},{6,2... | collective-permute-start | bytes 1572872 | tf_op jit(solution)/shard_map/ppermute | solution.py:43
  116.2 17.3 %collective-permute-start.40 = (bf16[256,1024]{1,0:T(8,128)(2,1)S(1)}, bf16[256,1024]{1,0:T(8,128)(2,1)S(1)}, u32[]{:S(2)}, u32[]{:S(2)}) collective-permute-start(bf16[256,1024]{1,0:T(8,128)(2,1)S(1)} %get-tuple-element.72), channel_id=1, source_target_pairs={{0,20},{4,16},{16,4},{20,0},{1,21},{5,17},{17,5},{21,1},{2,22},{6,... | collective-permute-start | bytes 1572872 | tf_op jit(solution)/shard_map/ppermute | solution.py:43
  118.8 19.3 %collective-permute-start.41 = (bf16[256,1024]{1,0:T(8,128)(2,1)S(1)}, bf16[256,1024]{1,0:T(8,128)(2,1)S(1)}, u32[]{:S(2)}, u32[]{:S(2)}) collective-permute-start(bf16[256,1024]{1,0:T(8,128)(2,1)S(1)} %get-tuple-element.73), channel_id=1, source_target_pairs={{0,16},{4,20},{16,0},{20,4},{1,17},{5,21},{17,1},{21,5},{2,18},{6,... | collective-permute-start | bytes 1572872 | tf_op jit(solution)/shard_map/ppermute | solution.py:43
  120.1 3.0 %collective-permute-start.36 = (f32[40,128]{1,0:T(8,128)S(1)}, f32[40,128]{1,0:T(8,128)S(1)}, u32[]{:S(2)}, u32[]{:S(2)}) collective-permute-start(f32[40,128]{1,0:T(8,128)S(1)} %pad_maximum_fusion), channel_id=1, source_target_pairs={{0,32},{32,0},{64,96},{96,64},{128,160},{160,128},{192,224},{224,1... | collective-permute-start | bytes 61448 | tf_op jit(solution)/shard_map/ppermute | solution.py:43
  123.1 3.8 %collective-permute-start.37 = (f32[40,128]{1,0:T(8,128)S(1)}, f32[40,128]{1,0:T(8,128)S(1)}, u32[]{:S(2)}, u32[]{:S(2)}) collective-permute-start(f32[40,128]{1,0:T(8,128)S(1)} %fusion), channel_id=1, source_target_pairs={{0,64},{32,96},{64,0},{96,32},{128,192},{160,224},{192,128},{224,1... | collective-permute-start | bytes 61448 | tf_op jit(solution)/shard_map/ppermute | solution.py:43
  126.9 6.5 %collective-permute-start.38 = (f32[40,128]{1,0:T(8,128)S(1)}, f32[40,128]{1,0:T(8,128)S(1)}, u32[]{:S(2)}, u32[]{:S(2)}) collective-permute-start(f32[40,128]{1,0:T(8,128)S(1)} %add.52), channel_id=1, source_target_pairs={{0,128},{32,160},{64,192},{96,224},{128,0},{160,32},{192,64},{224,... | collective-permute-start | bytes 61448 | tf_op jit(solution)/shard_map/ppermute | solution.py:43
  138.9 11.9 %collective-permute-start.46 = (bf16[128,1024]{1,0:T(8,128)(2,1)S(1)}, bf16[128,1024]{1,0:T(8,128)(2,1)S(1)}, u32[]{:S(2)}, u32[]{:S(2)}) collective-permute-start(bf16[128,1024]{1,0:T(8,128)(2,1)S(1)} %get-tuple-element.79), channel_id=1, source_target_pairs={{0,8},{8,0},{1,9},{9,1},{2,10},{10,2},{3,11},{11,3},{4,12},{12,4},... | collective-permute-start | bytes 786440 | tf_op jit(solution)/shard_map/ppermute | solution.py:43
  143.9 4.0 %collective-permute-start.42 = (f32[24,128]{1,0:T(8,128)S(1)}, f32[24,128]{1,0:T(8,128)S(1)}, u32[]{:S(2)}, u32[]{:S(2)}) collective-permute-start(f32[24,128]{1,0:T(8,128)S(1)} %pad_maximum_fusion.1), channel_id=1, source_target_pairs={{0,16},{4,20},{16,0},{20,4},{1,17},{5,21},{17,1},{21,5},{2,18},{6,... | collective-permute-start | bytes 36872 | tf_op jit(solution)/shard_map/ppermute | solution.py:43
  144.5 4.1 %collective-permute-start.44 = (f32[24,128]{1,0:T(8,128)S(1)}, f32[24,128]{1,0:T(8,128)S(1)}, u32[]{:S(2)}, u32[]{:S(2)}) collective-permute-start(f32[24,128]{1,0:T(8,128)S(1)} %slice.27), channel_id=1, source_target_pairs={{0,20},{4,16},{16,4},{20,0},{1,21},{5,17},{17,5},{21,1},{2,22},{6,... | collective-permute-start | bytes 36872 | tf_op jit(solution)/shard_map/ppermute | solution.py:43
  145.1 3.4 %collective-permute-start.43 = (f32[24,128]{1,0:T(8,128)S(1)}, f32[24,128]{1,0:T(8,128)S(1)}, u32[]{:S(2)}, u32[]{:S(2)}) collective-permute-start(f32[24,128]{1,0:T(8,128)S(1)} %slice.27), channel_id=1, source_target_pairs={{0,4},{4,0},{16,20},{20,16},{1,5},{5,1},{17,21},{21,17},{2,6},{6,2... | collective-permute-start | bytes 36872 | tf_op jit(solution)/shard_map/ppermute | solution.py:43
  148.5 2.2 %collective-permute-start.45 = (f32[24,128]{1,0:T(8,128)S(1)}, f32[24,128]{1,0:T(8,128)S(1)}, u32[]{:S(2)}, u32[]{:S(2)}) collective-permute-start(f32[24,128]{1,0:T(8,128)S(1)} %add_add_fusion.refs_1_), channel_id=1, source_target_pairs={{0,8},{8,0},{1,9},{9,1},{2,10},{10,2},{3,11},{11,3},{4,12},{12,4},... | collective-permute-start | bytes 36872 | tf_op jit(solution)/shard_map/ppermute | solution.py:43
